TPU v7x, 32 devices: a whole 2x2x4 slice. The times are simulated.
32 devices in a mesh: section: 2 (over core), dp: 4 (over z), expert: 4 (over y, x).
Axes of the slice: x: 2, y: 2, z: 4, core: 2. Of those that a mesh axis runs over, the one named last changes fastest.
Arguments:
- inputs: bfloat16 [2, 3072, 1152], P(None, ('dp', 'expert')), may hold values from -6 to 6
- cotangent: bfloat16 [2, 3072, 1152], P(None, ('dp', 'expert')), may hold values from -6 to 6
- routes: int32 [2, 2, 3072, 1], P('section', None, ('dp', 'expert')), may hold values from 0 to 3; in each aligned block of 192 rows (0 to 191, 192 to 383, ..., all dimensions but the last counted through in order) at most 96 rows name the same one
- lengths: int32 [2, 4, 4], P(None, 'dp'), may hold values from 1 to 720, 768 in all within a row
- mixer_gain: float32 [2, 1152], P('section', ('dp', 'expert')), may hold values from 0.5 to 1.5
- input_weight: float32 [2, 1152, 4608], P('section', ('dp', 'expert')), may hold values from -0.1875 to 0.1875
- conv_weight: float32 [2, 4, 2304], P('section', None, ('dp', 'expert')), may hold values from -3 to 3
- conv_bias: float32 [2, 2304], P('section', ('dp', 'expert')), may hold values from -3 to 3
- select_weight: float32 [2, 2304, 104], P('section', ('dp', 'expert')), may hold values from -0.125 to 0.125
- step_weight: float32 [2, 72, 2304], P('section', None, ('dp', 'expert')), may hold values from -0.75 to 0.75
- step_bias: float32 [2, 2304], P('section', ('dp', 'expert')), may hold values from -9 to -2
- decay_log: float32 [2, 2304, 16], P('section', ('dp', 'expert')), may hold values from -2 to 2.5
- skip_gain: float32 [2, 2304], P('section', ('dp', 'expert')), may hold values from 0.5 to 1.5
- output_weight: float32 [2, 2304, 1152], P('section', ('dp', 'expert')), may hold values from -0.5 to 0.5
- expert_gain: float32 [2, 1152], P('section', ('dp', 'expert')), may hold values from 0.5 to 1.5
- router_weight: float32 [2, 1152, 4], P('section', ('dp', 'expert')), may hold values from -0.09375 to 0.09375
- up_weight: float32 [2, 4, 1152, 3072], P('section', 'expert', None, 'dp'), may hold values from -0.1875 to 0.1875
- down_weight: float32 [2, 4, 3072, 1152], P('section', 'expert', 'dp'), may hold values from -0.875 to 0.875
Outputs:
- layer_out: bfloat16 [2, 2, 3072, 1152], P('section', None, ('dp', 'expert'))
- input_grad: float32 [2, 2, 3072, 1152], P('section', None, ('dp', 'expert'))
- mixer_gain_grad: float32 [2, 1152], P('section', ('dp', 'expert'))
- input_weight_grad: float32 [2, 1152, 4608], P('section', ('dp', 'expert'))
- conv_weight_grad: float32 [2, 4, 2304], P('section', None, ('dp', 'expert'))
- conv_bias_grad: float32 [2, 2304], P('section', ('dp', 'expert'))
- select_weight_grad: float32 [2, 2304, 104], P('section', ('dp', 'expert'))
- step_weight_grad: float32 [2, 72, 2304], P('section', None, ('dp', 'expert'))
- step_bias_grad: float32 [2, 2304], P('section', ('dp', 'expert'))
- decay_log_grad: float32 [2, 2304, 16], P('section', ('dp', 'expert'))
- skip_gain_grad: float32 [2, 2304], P('section', ('dp', 'expert'))
- output_weight_grad: float32 [2, 2304, 1152], P('section', ('dp', 'expert'))
- expert_gain_grad: float32 [2, 1152], P('section', ('dp', 'expert'))
- router_weight_grad: float32 [2, 1152, 4], P('section', ('dp', 'expert'))
- up_weight_grad: float32 [2, 4, 1152, 3072], P('section', 'expert', None, 'dp')
- down_weight_grad: float32 [2, 4, 3072, 1152], P('section', 'expert', 'dp')
Inputs may be any that keep to these rules, and one draw needn't show every extreme that they name: `routes`: within one layer and micro-batch, the 192 tokens of one device send at most 96 tokens to any one expert, and some expert receives exactly 96 of some device's tokens. Each row holds the 4 sequence lengths of one group in order; they sum to 768, and the longest is exactly 720.
All inputs are finite; a program needn't handle non-finite values.
Results may differ from a plain program's by a relative error of at most 0.025.
The roundings to bfloat16 on the way count: a program that leaves them out, or rounds other values in their place, can miss the bound.
Values may be sent and summed in bfloat16 or wider, within the bound.
A program may use at most 320 MiB of HBM per device.

v0:
```python
import math

import jax
import jax.numpy as jnp
from jax import lax
from jax.sharding import PartitionSpec as P

epsilon = 1e-05
block_rows = 16


def from_behind(array, axis, by):
    length = lax.axis_size(axis)
    pairs = [(i, i + by) for i in range(length) if 0 <= i + by < length]
    return lax.ppermute(array, axis, pairs)


def prefix(array, axis, combine, identity):
    length, here = (lax.axis_size(axis), lax.axis_index(axis))
    everything = jax.tree.map(lambda part: lax.all_gather(part, axis), array)
    start = jax.tree.map(
        lambda part, zero: jnp.broadcast_to(jnp.asarray(zero, part.dtype), part.shape),
        array,
        identity,
    )

    def hop(k, before):
        reached = k < here
        new = combine(before, jax.tree.map(lambda part: part[k], everything))
        return jax.tree.map(lambda a, b: jnp.where(reached, a, b), new, before)

    return lax.fori_loop(0, length, hop, start)


def carried_in(array, axis, join, neutral):
    count = lax.axis_size(axis)
    place = lax.axis_index(axis)
    ahead = count - 1 - place
    gathered = jax.tree.map(
        lambda a, kind: lax.all_gather(a.astype(kind), axis),
        array,
        jax.tree.map(lambda a: jnp.bfloat16 if a.dtype == jnp.float32 else a.dtype, array),
    )
    state = jax.tree.map(lambda a, e: jnp.zeros_like(a) + jnp.asarray(e, a.dtype), array, neutral)

    def one(hop, state):
        source = count - 1 - hop
        return join(
            state,
            jax.tree.map(
                lambda a, own: lax.dynamic_index_in_dim(a, source, 0, False).astype(own.dtype),
                gathered,
                array,
            ),
        )

    return lax.fori_loop(0, ahead, one, state)


def norm_scale(residual, gain):
    return (
        residual * lax.rsqrt(jnp.mean(residual * residual, axis=-1, keepdims=True) + epsilon) * gain
    )


def product(left, right):
    return jnp.dot(left, right, preferred_element_type=jnp.float32)


def cross_rows(left, right):
    return lax.dot_general(
        left, right, (((0,), (0,)), ((), ())), preferred_element_type=jnp.float32
    )


def cross_cols(left, right):
    return lax.dot_general(
        left, right, (((1,), (1,)), ((), ())), preferred_element_type=jnp.float32
    )


def gate_product(values, gates):
    return values * jax.nn.silu(gates)


def doc_ids(lengths_row, positions):
    boundaries = jnp.cumsum(lengths_row, dtype=jnp.int32)
    counted = jnp.sum(
        (positions[:, None] >= boundaries[None, :]).astype(jnp.int32), axis=1, dtype=jnp.int32
    )
    return jnp.where(positions < 0, -1, counted)


def conv_act(wide_in, taps_weight, taps_bias, documents):
    tap_count = taps_weight.shape[0]
    row_count = wide_in.shape[0] - tap_count + 1
    own_docs = documents[tap_count - 1 :]
    summed = taps_bias + taps_weight[tap_count - 1] * wide_in[tap_count - 1 :]
    for offset in range(1, tap_count):
        start_row = tap_count - 1 - offset
        lagged = wide_in[start_row : start_row + row_count]
        same_doc = (documents[start_row : start_row + row_count] == own_docs)[:, None]
        summed = summed + taps_weight[start_row] * jnp.where(same_doc, lagged, 0.0)
    return jax.nn.silu(summed)


def end_state(activated, step_size, input_map, decay_log, documents):
    row_count = activated.shape[0]
    decay_rate = -jnp.exp(decay_log)
    own_docs = documents[-row_count:]
    previous = documents[-row_count - 1]
    rising = jnp.cumsum(step_size, axis=0)
    keep_rows = own_docs == own_docs[row_count - 1]
    remain = jnp.where(keep_rows[:, None], rising[row_count - 1][None, :] - rising, 0.0)
    tail_weight = jnp.where(keep_rows[:, None, None], jnp.exp(remain[:, :, None] * decay_rate), 0.0)
    ending = jnp.einsum("scn,sn,sc->cn", tail_weight, input_map, step_size * activated)
    through = jnp.exp(rising[row_count - 1][:, None] * decay_rate) * jnp.where(
        previous == own_docs[row_count - 1], 1.0, 0.0
    )
    return (through, ending)


def block_scan(
    activated, step_size, input_map, output_map, decay_log, skip_gain, entry_state, documents
):
    row_count, inner_width = activated.shape
    length = math.gcd(row_count, block_rows)
    count_blocks = row_count // length
    decay_rate = -jnp.exp(decay_log)
    own_docs = documents[-row_count:]
    before = documents[-row_count - 1 : -1]
    driving = step_size * activated

    def blocked(values):
        return values.reshape((count_blocks, length) + values.shape[1:])

    def one_block(carried, pieces):
        drive_part, step_part, in_part, out_part, doc_part, prior_part = pieces
        rising = jnp.cumsum(step_part, axis=0)
        causal_mask = jnp.arange(length)[:, None] >= jnp.arange(length)[None, :]
        allowed = causal_mask & (doc_part[:, None] == doc_part[None, :])
        log_gap = jnp.where(allowed[:, :, None], rising[:, None, :] - rising[None, :, :], 0.0)
        weight = jnp.where(allowed[:, :, None, None], jnp.exp(log_gap[..., None] * decay_rate), 0.0)
        paired = out_part[:, None, :] * in_part[None, :, :]
        inside = jnp.einsum("tscn,tsn,sc->tc", weight, paired, drive_part)
        prior_doc = prior_part[0]
        continues = (doc_part == prior_doc)[:, None, None]
        decays = jnp.where(continues, jnp.exp(rising[:, :, None] * decay_rate), 0.0)
        outside = jnp.einsum("tcn,cn,tn->tc", decays, carried, out_part)
        last_doc = doc_part[length - 1]
        same_last = doc_part == last_doc
        remain = jnp.where(same_last[:, None], rising[length - 1][None, :] - rising, 0.0)
        tail_weight = jnp.where(
            same_last[:, None, None], jnp.exp(remain[:, :, None] * decay_rate), 0.0
        )
        fresh_state = jnp.einsum("scn,sn,sc->cn", tail_weight, in_part, drive_part)
        whole_decay = jnp.exp(rising[length - 1][:, None] * decay_rate)
        new_state = fresh_state + jnp.where(prior_doc == last_doc, whole_decay, 0.0) * carried
        return (new_state, inside + outside)

    pieces = tuple(
        (
            blocked(values)
            for values in (driving, step_size, input_map, output_map, own_docs, before)
        )
    )
    _, outputs = lax.scan(jax.checkpoint(one_block), entry_state, pieces)
    return outputs.reshape(row_count, inner_width) + skip_gain * activated


def chain_state(earlier, later):
    return (later[0] * earlier[0], later[0] * earlier[1] + later[1])


def dispatch_tables(chosen, capacity):
    indicator = chosen.astype(jnp.int32)
    row_count, expert_count = indicator.shape
    earlier_rows = jnp.cumsum(indicator, axis=0, dtype=jnp.int32) - indicator
    slot_rank = jnp.sum(earlier_rows * indicator, axis=1, dtype=jnp.int32)
    expert_of = jnp.sum(
        indicator * jnp.arange(expert_count, dtype=jnp.int32)[None, :], axis=1, dtype=jnp.int32
    )
    slot_index = expert_of * capacity + slot_rank
    all_slots = jnp.arange(expert_count * capacity, dtype=jnp.int32)
    matches = slot_index[None, :] == all_slots[:, None]
    token_index = jnp.sum(
        jnp.where(matches, jnp.arange(row_count, dtype=jnp.int32)[None, :], 0),
        axis=1,
        dtype=jnp.int32,
    )
    token_index = token_index + row_count * (1 - jnp.any(matches, axis=1).astype(jnp.int32))
    return (slot_index, token_index)


def layer_forward(residual, weights, experts, routing, documents):
    (
        mixer_gain,
        input_weight,
        conv_weight,
        conv_bias,
        select_weight,
        step_weight,
        step_bias,
        decay_log,
        skip_gain,
        output_weight,
        expert_gain,
        router_weight,
    ) = weights
    up_weight, down_weight = experts
    row_count, model_width = residual.shape
    inner_width = input_weight.shape[1] // 2
    low_rank = step_weight.shape[0]
    state_width = decay_log.shape[1]
    tap_count = conv_weight.shape[0]
    expert_count = router_weight.shape[1]
    capacity = 2 * row_count // expert_count
    normed = norm_scale(residual, mixer_gain.astype(jnp.float32)).astype(jnp.bfloat16)
    mixed_in = product(normed, input_weight).astype(jnp.bfloat16)
    conv_in = mixed_in[:, :inner_width]
    gate_in = mixed_in[:, inner_width:]
    rim_rows = from_behind(conv_in[row_count - tap_count + 1 :], "expert", 1)
    wide_in = jnp.concatenate([rim_rows, conv_in], axis=0)
    activated = conv_act(
        wide_in.astype(jnp.float32),
        conv_weight.astype(jnp.float32),
        conv_bias.astype(jnp.float32),
        documents,
    ).astype(jnp.bfloat16)
    projected = product(activated, select_weight)
    step_low = projected[:, :low_rank].astype(jnp.bfloat16)
    input_map = projected[:, low_rank : low_rank + state_width]
    output_map = projected[:, low_rank + state_width :]
    step_pre = product(step_low, step_weight) + step_bias.astype(jnp.float32)
    step_size = jax.nn.softplus(step_pre)
    act_float = activated.astype(jnp.float32)
    decay_float = decay_log.astype(jnp.float32)
    through, ending = end_state(act_float, step_size, input_map, decay_float, documents)
    entry_state = prefix(
        (through, ending), "expert", chain_state, (jnp.ones_like(through), jnp.zeros_like(ending))
    )[1]
    scanned = block_scan(
        act_float,
        step_size,
        input_map,
        output_map,
        decay_float,
        skip_gain.astype(jnp.float32),
        entry_state,
        documents,
    )
    gated_out = gate_product(scanned, gate_in.astype(jnp.float32)).astype(jnp.bfloat16)
    middle = residual + product(gated_out, output_weight)
    normed_two = norm_scale(middle, expert_gain.astype(jnp.float32)).astype(jnp.bfloat16)
    logits = product(normed_two, router_weight)
    probability = jax.nn.softmax(logits, axis=-1)
    chosen = routing[:, None] == jnp.arange(expert_count, dtype=jnp.int32)[None, :]
    gate_value = jnp.sum(jnp.where(chosen, probability, 0.0), axis=1)
    slot_index, token_index = dispatch_tables(chosen, capacity)
    padded = jnp.concatenate([normed_two, jnp.zeros((1, model_width), jnp.bfloat16)], axis=0)
    outgoing = padded[token_index].reshape(expert_count, capacity, model_width)
    arrived = lax.all_to_all(outgoing, "expert", split_axis=0, concat_axis=0, tiled=True)
    leading = arrived.shape[:2]
    flat_rows = arrived.reshape(-1, model_width)
    pre_act = product(flat_rows, up_weight)
    hidden = jax.nn.gelu(pre_act).astype(jnp.bfloat16)
    result = product(hidden, down_weight).astype(jnp.bfloat16)
    result, pre_act, hidden, arrived = (
        result.reshape(leading + (model_width,)),
        pre_act.reshape(leading + (-1,)),
        hidden.reshape(leading + (-1,)),
        arrived,
    )
    returned = lax.all_to_all(result, "expert", split_axis=0, concat_axis=0, tiled=True)
    back_rows = jnp.concatenate(
        [returned.reshape(-1, model_width), jnp.zeros((1, model_width), jnp.bfloat16)], axis=0
    )
    mixture = back_rows[slot_index].astype(jnp.float32)
    out_residual = middle + gate_value[:, None] * mixture
    stored = (
        residual,
        normed,
        wide_in,
        gate_in,
        activated,
        step_low,
        step_pre,
        step_size,
        input_map,
        output_map,
        through,
        entry_state,
        scanned,
        gated_out,
        middle,
        normed_two,
        probability,
        chosen,
        gate_value,
        slot_index,
        token_index,
        pre_act,
        hidden,
        arrived,
        mixture,
        documents,
    )
    return (out_residual, stored)


def layer_backward(grad_out, stored, weights, experts):
    (
        residual,
        normed,
        wide_in,
        gate_in,
        activated,
        step_low,
        step_pre,
        step_size,
        input_map,
        output_map,
        through,
        entry_state,
        scanned,
        gated_out,
        middle,
        normed_two,
        probability,
        chosen,
        gate_value,
        slot_index,
        token_index,
        pre_act,
        hidden,
        arrived,
        mixture,
        documents,
    ) = stored
    (
        mixer_gain,
        input_weight,
        conv_weight,
        conv_bias,
        select_weight,
        step_weight,
        step_bias,
        decay_log,
        skip_gain,
        output_weight,
        expert_gain,
        router_weight,
    ) = weights
    up_weight, down_weight = experts
    row_count, model_width = grad_out.shape
    tap_count = conv_weight.shape[0]
    expert_count, capacity = (arrived.shape[0], arrived.shape[1])
    back_gate = jnp.sum(grad_out * mixture, axis=1)
    back_result = (gate_value[:, None] * grad_out).astype(jnp.bfloat16)
    padded = jnp.concatenate([back_result, jnp.zeros((1, model_width), jnp.bfloat16)], axis=0)
    back_outgoing = padded[token_index].reshape(expert_count, capacity, model_width)
    back_arrived = lax.all_to_all(back_outgoing, "expert", split_axis=0, concat_axis=0, tiled=True)
    back_flat = back_arrived.reshape(-1, model_width)
    slot_total = back_flat.shape[0]
    hidden_rows = hidden.reshape(slot_total, -1)
    pre_rows = pre_act.reshape(slot_total, -1)
    grad_down = cross_rows(hidden_rows, back_flat)
    back_hidden = cross_cols(back_flat, down_weight)
    back_pre = jax.vjp(jax.nn.gelu, pre_rows)[1](back_hidden)[0].astype(jnp.bfloat16)
    grad_up = cross_rows(arrived.reshape(slot_total, -1), back_pre)
    back_expert = (
        cross_cols(back_pre, up_weight)
        .astype(jnp.bfloat16)
        .reshape(expert_count, capacity, model_width)
    )
    back_returned = lax.all_to_all(back_expert, "expert", split_axis=0, concat_axis=0, tiled=True)
    back_rows = jnp.concatenate(
        [back_returned.reshape(-1, model_width), jnp.zeros((1, model_width), jnp.bfloat16)], axis=0
    )
    back_tokens = back_rows[slot_index].astype(jnp.float32)
    back_logits = (
        (back_gate * gate_value)[:, None] * (chosen.astype(jnp.float32) - probability)
    ).astype(jnp.bfloat16)
    grad_router = cross_rows(normed_two, back_logits)
    back_normed_two = back_tokens + cross_cols(back_logits, router_weight)
    back_mid_norm, grad_expert_gain = jax.vjp(norm_scale, middle, expert_gain.astype(jnp.float32))[
        1
    ](back_normed_two)
    back_middle = grad_out + back_mid_norm
    back_branch = back_middle.astype(jnp.bfloat16)
    grad_output = cross_rows(gated_out, back_branch)
    back_gated = cross_cols(back_branch, output_weight)
    back_scanned, back_gate_in = jax.vjp(gate_product, scanned, gate_in.astype(jnp.float32))[1](
        back_gated
    )
    act_float = activated.astype(jnp.float32)
    decay_float = decay_log.astype(jnp.float32)

    def scan_piece(act_in, step_in, in_map, out_map, decay_in, skip_in, entry_in):
        return block_scan(act_in, step_in, in_map, out_map, decay_in, skip_in, entry_in, documents)

    (
        back_act_one,
        back_step_one,
        back_in_one,
        back_out_map,
        back_decay_one,
        grad_skip,
        back_entry,
    ) = jax.vjp(
        scan_piece,
        act_float,
        step_size,
        input_map,
        output_map,
        decay_float,
        skip_gain.astype(jnp.float32),
        entry_state,
    )[
        1
    ](
        back_scanned
    )
    adjoint = carried_in(
        (through, back_entry),
        "expert",
        chain_state,
        (jnp.ones_like(through), jnp.zeros_like(back_entry)),
    )[1]

    def end_piece(act_in, step_in, in_map, decay_in):
        return end_state(act_in, step_in, in_map, decay_in, documents)

    back_act_two, back_step_two, back_in_two, back_decay_two = jax.vjp(
        end_piece, act_float, step_size, input_map, decay_float
    )[1]((entry_state * adjoint, adjoint))
    back_step_pre = (back_step_one + back_step_two) * jax.nn.sigmoid(step_pre)
    grad_step_bias = jnp.sum(back_step_pre, axis=0)
    back_step_low = back_step_pre.astype(jnp.bfloat16)
    grad_step = cross_rows(step_low, back_step_low)
    back_rank = cross_cols(back_step_low, step_weight)
    back_projected = jnp.concatenate(
        [back_rank, back_in_one + back_in_two, back_out_map], axis=1
    ).astype(jnp.bfloat16)
    grad_select = cross_rows(activated, back_projected)
    back_activated = back_act_one + back_act_two + cross_cols(back_projected, select_weight)

    def conv_piece(wide_float, taps_in, bias_in):
        return conv_act(wide_float, taps_in, bias_in, documents)

    back_wide, grad_conv, grad_conv_bias = jax.vjp(
        conv_piece,
        wide_in.astype(jnp.float32),
        conv_weight.astype(jnp.float32),
        conv_bias.astype(jnp.float32),
    )[1](back_activated)
    rim_back = from_behind(back_wide[: tap_count - 1], "expert", -1)
    back_conv_in = back_wide[tap_count - 1 :] + jnp.pad(
        rim_back, ((row_count - tap_count + 1, 0), (0, 0))
    )
    back_mixed = jnp.concatenate([back_conv_in, back_gate_in], axis=1).astype(jnp.bfloat16)
    grad_input = cross_rows(normed, back_mixed)
    back_normed = cross_cols(back_mixed, input_weight)
    back_residual_norm, grad_mixer_gain = jax.vjp(
        norm_scale, residual, mixer_gain.astype(jnp.float32)
    )[1](back_normed)
    back_residual = back_middle + back_residual_norm
    mamba_grads = (
        grad_mixer_gain,
        grad_input,
        grad_conv,
        grad_conv_bias,
        grad_select,
        grad_step,
        grad_step_bias,
        back_decay_one + back_decay_two,
        grad_skip,
        grad_output,
        grad_expert_gain,
        grad_router,
    )
    return (back_residual, mamba_grads, (grad_up, grad_down))


def reduce_grads(mamba_grads, expert_grads):
    mamba_part = (
        lax.psum_scatter(mamba_grads[0], ("dp", "expert"), scatter_dimension=0, tiled=True),
        lax.psum_scatter(mamba_grads[1], ("dp", "expert"), scatter_dimension=0, tiled=True),
        lax.psum_scatter(mamba_grads[2], ("dp", "expert"), scatter_dimension=1, tiled=True),
        lax.psum_scatter(mamba_grads[3], ("dp", "expert"), scatter_dimension=0, tiled=True),
        lax.psum_scatter(mamba_grads[4], ("dp", "expert"), scatter_dimension=0, tiled=True),
        lax.psum_scatter(mamba_grads[5], ("dp", "expert"), scatter_dimension=1, tiled=True),
        lax.psum_scatter(mamba_grads[6], ("dp", "expert"), scatter_dimension=0, tiled=True),
        lax.psum_scatter(mamba_grads[7], ("dp", "expert"), scatter_dimension=0, tiled=True),
        lax.psum_scatter(mamba_grads[8], ("dp", "expert"), scatter_dimension=0, tiled=True),
        lax.psum_scatter(mamba_grads[9], ("dp", "expert"), scatter_dimension=0, tiled=True),
        lax.psum_scatter(mamba_grads[10], ("dp", "expert"), scatter_dimension=0, tiled=True),
        lax.psum_scatter(mamba_grads[11], ("dp", "expert"), scatter_dimension=0, tiled=True),
    )
    expert_part = (
        lax.psum_scatter(
            expert_grads[0].astype(jnp.bfloat16), "dp", scatter_dimension=1, tiled=True
        ).astype(jnp.float32),
        lax.psum_scatter(
            expert_grads[1].astype(jnp.bfloat16), "dp", scatter_dimension=0, tiled=True
        ).astype(jnp.float32),
    )
    return (tuple(mamba_part), tuple(expert_part))


def shards(
    inputs,
    cotangent,
    routes,
    lengths,
    mixer_gain,
    input_weight,
    conv_weight,
    conv_bias,
    select_weight,
    step_weight,
    step_bias,
    decay_log,
    skip_gain,
    output_weight,
    expert_gain,
    router_weight,
    up_weight,
    down_weight,
):
    section_index = lax.axis_index("section")
    on_first = section_index == 0
    group_place = lax.axis_index("expert")
    micro_count, row_count, model_width = inputs.shape
    tap_count = conv_weight.shape[1]
    weights = (
        lax.all_gather(mixer_gain[0].astype(jnp.bfloat16), ("dp", "expert"), axis=0, tiled=True),
        lax.all_gather(input_weight[0].astype(jnp.bfloat16), ("dp", "expert"), axis=0, tiled=True),
        lax.all_gather(conv_weight[0].astype(jnp.bfloat16), ("dp", "expert"), axis=1, tiled=True),
        lax.all_gather(conv_bias[0].astype(jnp.bfloat16), ("dp", "expert"), axis=0, tiled=True),
        lax.all_gather(select_weight[0].astype(jnp.bfloat16), ("dp", "expert"), axis=0, tiled=True),
        lax.all_gather(step_weight[0].astype(jnp.bfloat16), ("dp", "expert"), axis=1, tiled=True),
        lax.all_gather(step_bias[0].astype(jnp.bfloat16), ("dp", "expert"), axis=0, tiled=True),
        lax.all_gather(decay_log[0].astype(jnp.bfloat16), ("dp", "expert"), axis=0, tiled=True),
        lax.all_gather(skip_gain[0].astype(jnp.bfloat16), ("dp", "expert"), axis=0, tiled=True),
        lax.all_gather(output_weight[0].astype(jnp.bfloat16), ("dp", "expert"), axis=0, tiled=True),
        lax.all_gather(expert_gain[0].astype(jnp.bfloat16), ("dp", "expert"), axis=0, tiled=True),
        lax.all_gather(router_weight[0].astype(jnp.bfloat16), ("dp", "expert"), axis=0, tiled=True),
    )
    weights = tuple(weights)
    experts = (
        lax.all_gather(up_weight[0, 0].astype(jnp.bfloat16), "dp", axis=1, tiled=True),
        lax.all_gather(down_weight[0, 0].astype(jnp.bfloat16), "dp", axis=0, tiled=True),
    )
    experts = tuple(experts)
    positions = group_place * row_count + jnp.arange(1 - tap_count, row_count, dtype=jnp.int32)
    received = jnp.zeros((row_count, model_width), jnp.bfloat16)
    outputs_seen = []
    stored_steps = []
    for timestep in range(micro_count + 1):
        micro_index = jnp.clip(timestep - section_index, 0, micro_count - 1)
        routing = lax.dynamic_index_in_dim(routes[0, :, :, 0], micro_index, 0, keepdims=False)
        lengths_row = lax.dynamic_index_in_dim(lengths[:, 0, :], micro_index, 0, keepdims=False)
        documents = doc_ids(lengths_row, positions)
        own_input = inputs[timestep] if timestep < micro_count else jnp.zeros_like(inputs[0])
        residual = jnp.where(on_first, own_input, received).astype(jnp.float32)
        out_residual, stored = layer_forward(residual, weights, experts, routing, documents)
        sent_rows = out_residual.astype(jnp.bfloat16)
        outputs_seen.append(sent_rows)
        stored_steps.append(stored)
        if timestep < micro_count:
            received = from_behind(sent_rows, "section", 1)
    grad_received = jnp.zeros((row_count, model_width), jnp.bfloat16)
    input_grads = []
    collected = []
    for timestep in range(micro_count + 1):
        own_grad = (
            cotangent[micro_count - 1 - timestep]
            if timestep < micro_count
            else jnp.zeros_like(cotangent[0])
        )
        grad_out = jnp.where(on_first, grad_received, own_grad).astype(jnp.float32)
        back_residual, mamba_grads, expert_grads = layer_backward(
            grad_out, stored_steps[micro_count - timestep], weights, experts
        )
        input_grads.append(back_residual)
        collected.append(reduce_grads(mamba_grads, expert_grads))
        if timestep < micro_count:
            grad_received = from_behind(back_residual.astype(jnp.bfloat16), "section", -1)
    totals = collected[0]
    for further in collected[1:]:
        totals = jax.tree.map(jnp.add, totals, further)
    mamba_total, expert_total = totals
    layer_out = jnp.stack(
        [
            jnp.where(on_first, outputs_seen[number], outputs_seen[number + 1])
            for number in range(micro_count)
        ]
    )[None]
    input_grad = jnp.stack(
        [
            jnp.where(
                on_first, input_grads[micro_count - number], input_grads[micro_count - 1 - number]
            )
            for number in range(micro_count)
        ]
    )[None]
    return (
        (layer_out, input_grad)
        + tuple((gradient[None] for gradient in mamba_total))
        + (expert_total[0][None, None], expert_total[1][None, None])
    )


def solution(mesh):
    return jax.shard_map(
        shards,
        mesh=mesh,
        in_specs=(
            P(None, ("dp", "expert"), None),
            P(None, ("dp", "expert"), None),
            P("section", None, ("dp", "expert"), None),
            P(None, "dp", None),
            P("section", ("dp", "expert")),
            P("section", ("dp", "expert"), None),
            P("section", None, ("dp", "expert")),
            P("section", ("dp", "expert")),
            P("section", ("dp", "expert"), None),
            P("section", None, ("dp", "expert")),
            P("section", ("dp", "expert")),
            P("section", ("dp", "expert"), None),
            P("section", ("dp", "expert")),
            P("section", ("dp", "expert"), None),
            P("section", ("dp", "expert")),
            P("section", ("dp", "expert"), None),
            P("section", "expert", None, "dp"),
            P("section", "expert", "dp", None),
        ),
        out_specs=(
            P("section", None, ("dp", "expert"), None),
            P("section", None, ("dp", "expert"), None),
            P("section", ("dp", "expert")),
            P("section", ("dp", "expert"), None),
            P("section", None, ("dp", "expert")),
            P("section", ("dp", "expert")),
            P("section", ("dp", "expert"), None),
            P("section", None, ("dp", "expert")),
            P("section", ("dp", "expert")),
            P("section", ("dp", "expert"), None),
            P("section", ("dp", "expert")),
            P("section", ("dp", "expert"), None),
            P("section", ("dp", "expert")),
            P("section", ("dp", "expert"), None),
            P("section", "expert", None, "dp"),
            P("section", "expert", "dp", None),
        ),
        check_vma=False,
    )
```

profile of v0, /device:TPU:0, one launch (start us, length us, event | category | flops | bytes accessed | tf_op | source)
XLA Modules:
  0.0 5890.7 jit_solution(17861095561633040516)
XLA Ops:
  26.8 80.4 %all-reduce.72 = (bf16[1152]{0:T(1024)(128)(2,1)S(1)}, bf16[2304]{0:T(1024)(128)(2,1)S(1)}, bf16[2304]{0:T(1024)(128)(2,1)S(1)}, bf16[2304]{0:T(1024)(128)(2,1)S(1)}, bf16[1152]{0:T(1024)(128)(2,1)S(1)}) all-reduce(bf16[1152]{0:T(1024)(128)(2,1)S(1)} %dynamic-update-slice.1, ...), channel_id=4, replica_groups=mesh['section'=2,'dp'=4,'expert'=4] {'dp','expert'}, use_global_device_ids=true, to_apply=%add.61 | all-reduce | flops 9216 | bytes 36864
  108.3 56.1 all-gather.1
  165.7 48.4 slice_reduce_fusion.12
  214.4 55.6 all-gather.5
  270.0 42.9 all-gather.4
  327.2 58.4 all-gather.7
  449.6 215.5 %while.234 = (s32[]{:T(128)}, f32[2304,16]{0,1:T(8,128)S(1)}, f32[12,16,2304]{2,1,0:T(8,128)}, f32[12,16,2304]{2,1,0:T(8,128)S(1)}, s32[12,16]{1,0:T(8,128)}, /*...) while((s32[]{:T(128)}, f32[2304,16]{0,1:T(8,128)S(1)}, ...), condition=%wide.region_9.10_spmd, body=%wide.region_7.9_spmd.sunk | while | flops 46748448 | bytes 13504191 | solution.py:167
  680.8 58.1 all-gather.13
  850.1 216.5 %while.235 = (s32[]{:T(128)}, f32[2304,16]{0,1:T(8,128)S(1)}, f32[12,16,2304]{2,1,0:T(8,128)}, f32[12,16,2304]{2,1,0:T(8,128)S(1)}, s32[12,16]{1,0:T(8,128)}, /*...) while((s32[]{:T(128)}, f32[2304,16]{0,1:T(8,128)S(1)}, ...), condition=%wide.region_29.30_spmd, body=%wide.region_27.29_spmd.sunk | while | flops 46748448 | bytes 13504191 | solution.py:167
  1198.9 229.8 %while.236 = (s32[]{:T(128)}, f32[2304,16]{0,1:T(8,128)S(1)}, f32[12,16,2304]{2,1,0:T(8,128)}, f32[12,16,2304]{2,1,0:T(8,128)S(1)}, s32[12,16]{1,0:T(8,128)}, /*...) while((s32[]{:T(128)}, f32[2304,16]{0,1:T(8,128)S(1)}, ...), condition=%wide.region_49.50_spmd, body=%wide.region_47.49_spmd.sunk | while | flops 46748448 | bytes 14143231 | solution.py:167
  1525.3 63.7 %while.237 = (s32[]{:T(128)}, f32[2304,16]{0,1:T(8,128)S(1)}, f32[12,2304,16]{1,2,0:T(8,128)}, f32[12,16,2304]{2,1,0:T(8,128)}, s32[12,16]{1,0:T(8,128)}, /*inde...) while((s32[]{:T(128)}, f32[2304,16]{0,1:T(8,128)S(1)}, ...), condition=%wide.region_64.65_spmd, body=%wide.region_62.64_spmd.sunk | while | flops 3686419 | bytes 2694679 | solution.py:167
  1617.0 632.1 %while.246 = (s32[]{:T(128)}, f32[2304,16]{0,1:T(8,128)S(1)}, f32[2304,16]{0,1:T(8,128)S(1)}, f32[12,16,2304]{2,1,0:T(8,128)}, f32[12,16,2304]{2,1,0:T(8,128)}, ...) while((s32[]{:T(128)}, f32[2304,16]{0,1:T(8,128)S(1)}, ...), condition=%wide.region_80.81_spmd.clone, body=%wide.region_65.80_spmd.clone.sunk | while | flops 180539424 | bytes 43401956 | solution.py:167
  1635.1 18.8 multiply_reduce_fusion.70
  1687.7 18.8 multiply_reduce_fusion.70
  1740.3 18.8 multiply_reduce_fusion.70
  1792.9 18.8 multiply_reduce_fusion.70
  1845.5 18.8 multiply_reduce_fusion.70
  1898.2 18.8 multiply_reduce_fusion.70
  1950.8 18.8 multiply_reduce_fusion.70
  2003.4 18.8 multiply_reduce_fusion.70
  2056.1 18.8 multiply_reduce_fusion.70
  2108.7 18.8 multiply_reduce_fusion.70
  2161.4 18.8 multiply_reduce_fusion.70
  2214.0 18.8 multiply_reduce_fusion.70
  2302.7 20.9 fusion.334
  2394.4 72.1 %while.239 = (s32[]{:T(128)}, f32[2304,16]{0,1:T(8,128)S(1)}, f32[12,2304,16]{1,2,0:T(8,128)}, f32[12,16,2304]{2,1,0:T(8,128)}, s32[12,16]{1,0:T(8,128)}, /*inde...) while((s32[]{:T(128)}, f32[2304,16]{0,1:T(8,128)S(1)}, ...), condition=%wide.region_93.94_spmd, body=%wide.region_91.93_spmd.sunk | while | flops 3686419 | bytes 2694679 | solution.py:167
  2493.5 639.3 %while.247 = (s32[]{:T(128)}, f32[2304,16]{0,1:T(8,128)S(1)}, f32[2304,16]{0,1:T(8,128)S(1)}, f32[12,16,2304]{2,1,0:T(8,128)}, f32[12,16,2304]{2,1,0:T(8,128)}, ...) while((s32[]{:T(128)}, f32[2304,16]{0,1:T(8,128)S(1)}, ...), condition=%wide.region_109.110_spmd.clone, body=%wide.region_94.109_spmd.clone.sunk | while | flops 180539424 | bytes 43303596 | solution.py:167
  2512.2 18.8 multiply_reduce_fusion.74
  2565.5 18.8 multiply_reduce_fusion.74
  2618.7 18.8 multiply_reduce_fusion.74
  2671.9 18.8 multiply_reduce_fusion.74
  2725.2 18.8 multiply_reduce_fusion.74
  2778.4 18.8 multiply_reduce_fusion.74
  2831.6 18.8 multiply_reduce_fusion.74
  2884.8 18.8 multiply_reduce_fusion.74
  2938.1 18.8 multiply_reduce_fusion.74
  2991.3 18.8 multiply_reduce_fusion.74
  3044.5 18.8 multiply_reduce_fusion.74
  3097.7 18.8 multiply_reduce_fusion.74
  3188.7 20.9 fusion.332
  3280.7 63.8 %while.241 = (s32[]{:T(128)}, f32[2304,16]{0,1:T(8,128)S(1)}, f32[12,2304,16]{1,2,0:T(8,128)S(1)}, f32[12,16,2304]{2,1,0:T(8,128)}, s32[12,16]{1,0:T(8,128)}, /*...) while((s32[]{:T(128)}, f32[2304,16]{0,1:T(8,128)S(1)}, ...), condition=%wide.region_122.123_spmd, body=%wide.region_120.122_spmd.sunk | while | flops 3686419 | bytes 2694679 | solution.py:167
  3378.8 638.7 %while.248 = (s32[]{:T(128)}, f32[2304,16]{0,1:T(8,128)S(1)}, f32[2304,16]{0,1:T(8,128)S(1)}, f32[12,16,2304]{2,1,0:T(8,128)}, f32[12,16,2304]{2,1,0:T(8,128)}, ...) while((s32[]{:T(128)}, f32[2304,16]{0,1:T(8,128)S(1)}, ...), condition=%wide.region_138.139_spmd.clone, body=%wide.region_123.138_spmd.clone.sunk | while | flops 180539424 | bytes 43303596 | solution.py:167
  3397.4 18.8 multiply_reduce_fusion.78
  3450.6 18.8 multiply_reduce_fusion.78
  3503.8 18.8 multiply_reduce_fusion.78
  3557.0 18.8 multiply_reduce_fusion.78
  3610.2 18.8 multiply_reduce_fusion.78
  3663.3 18.8 multiply_reduce_fusion.78
  3716.5 18.8 multiply_reduce_fusion.78
  3769.7 18.8 multiply_reduce_fusion.78
  3822.9 18.8 multiply_reduce_fusion.78
  4077.2 20.9 fusion.330
  4259.2 73.1 %all-reduce.71 = (f32[1152]{0:T(1024)S(1)}, f32[2304]{0:T(1024)S(1)}, f32[2304]{0:T(1024)S(1)}, f32[2304]{0:T(1024)S(1)}, f32[1152]{0:T(1024)S(1)}, /*index=5*/f32[1152,4]{0,1:T(4,128)S(1)}) all-reduce(f32[1152]{0:T(1024)S(1)} %add_add_fusion.11, ...), channel_id=52, replica_groups=mesh['section'=2,'dp'=4,'expert'=4] {'dp','expert'}, use_global_device_ids=true, to_apply=%region_148.149.clone | all-reduce | flops 13824 | bytes 110592
  4341.3 21.2 reduce-scatter.42.cloned.1.call-done
  4364.1 126.5 %reduce-scatter.40.cloned.1.call-done = f32[144,72]{1,0:T(8,128)} async-done(((f32[2304,72]{1,0:T(8,128)}), f32[144,72]{1,0:T(8,128)}) %reduce-scatter.40.cloned.1.call-update) | async-done | bytes 41488
  4492.2 123.3 %reduce-scatter.20.cloned.1.call-done = bf16[1152,768]{1,0:T(8,128)(2,1)} async-done(((bf16[1152,3072]{1,0:T(8,128)(2,1)}), bf16[1152,768]{1,0:T(8,128)(2,1)}) %reduce-scatter.20.cloned.1.call-update) | async-done | bytes 1769488 | tf_op jit(solution)/shard_map/reduce_scatter | solution.py:501
  4615.5 126.3 %reduce-scatter.22.cloned.1.call-done = bf16[1152,768]{1,0:T(8,128)(2,1)} async-done(((bf16[1152,3072]{1,0:T(8,128)(2,1)}), bf16[1152,768]{1,0:T(8,128)(2,1)}) %reduce-scatter.22.cloned.1.call-update) | async-done | bytes 1769488 | tf_op jit(solution)/shard_map/reduce_scatter | solution.py:501
  4741.8 126.2 %reduce-scatter.24.cloned.1.call-done = bf16[1152,768]{1,0:T(8,128)(2,1)} async-done(((bf16[1152,3072]{1,0:T(8,128)(2,1)}), bf16[1152,768]{1,0:T(8,128)(2,1)}) %reduce-scatter.24.cloned.1.call-update) | async-done | bytes 1769488 | tf_op jit(solution)/shard_map/reduce_scatter | solution.py:501
  4872.9 121.4 %reduce-scatter.26.cloned.1.call-done = bf16[768,1152]{1,0:T(8,128)(2,1)} async-done(((bf16[3072,1152]{1,0:T(8,128)(2,1)}), bf16[768,1152]{1,0:T(8,128)(2,1)}) %reduce-scatter.26.cloned.1.call-update) | async-done | bytes 1769488 | tf_op jit(solution)/shard_map/reduce_scatter | solution.py:504
  4994.3 126.2 %reduce-scatter.28.cloned.1.call-done = bf16[768,1152]{1,0:T(8,128)(2,1)} async-done(((bf16[3072,1152]{1,0:T(8,128)(2,1)}), bf16[768,1152]{1,0:T(8,128)(2,1)}) %reduce-scatter.28.cloned.1.call-update) | async-done | bytes 1769488 | tf_op jit(solution)/shard_map/reduce_scatter | solution.py:504
  5120.5 126.3 %reduce-scatter.30.cloned.1.call-done = bf16[768,1152]{1,0:T(8,128)(2,1)} async-done(((bf16[3072,1152]{1,0:T(8,128)(2,1)}), bf16[768,1152]{1,0:T(8,128)(2,1)}) %reduce-scatter.30.cloned.1.call-update) | async-done | bytes 1769488 | tf_op jit(solution)/shard_map/reduce_scatter | solution.py:504
  5251.7 124.2 %reduce-scatter.34.cloned.1.call-done = f32[144,104]{1,0:T(8,128)} async-done(((f32[2304,104]{1,0:T(8,128)}), f32[144,104]{1,0:T(8,128)}) %reduce-scatter.34.cloned.1.call-update) | async-done | bytes 59920 | tf_op jit(solution)/shard_map/reduce_scatter | solution.py:491
  5376.0 187.4 %reduce-scatter.36.cloned.1.call-done = f32[144,1152]{1,0:T(8,128)} async-done(((f32[2304,1152]{1,0:T(8,128)}), f32[144,1152]{1,0:T(8,128)}) %reduce-scatter.36.cloned.1.call-update) | async-done | bytes 663568 | tf_op jit(solution)/shard_map/reduce_scatter | solution.py:496
  5563.4 320.4 %reduce-scatter.32.cloned.1.call-done = f32[72,4608]{1,0:T(8,128)} async-done(((f32[1152,4608]{1,0:T(8,128)}), f32[72,4608]{1,0:T(8,128)}) %reduce-scatter.32.cloned.1.call-update) | async-done | bytes 1327120 | tf_op jit(solution)/shard_map/reduce_scatter | solution.py:488
  (4700 shorter events, 3097.1 us)
Async XLA Ops:
  7.2 309.2 %all-gather.31.cloned.1.call-start = ((), (), s32[]{:S(2)}) async-start(), calls=%async_computation.30 | async-start | bytes 11280384 | tf_op jit(solution)/shard_map/all_gather | solution.py:538
  9.5 659.5 %all-gather.33.cloned.1.call-start = ((), (), s32[]{:S(2)}) async-start(), calls=%async_computation.31 | async-start | bytes 5640192 | tf_op jit(solution)/shard_map/all_gather | solution.py:546
  10.4 730.3 %all-gather.35.cloned.1.call-start = ((), (), s32[]{:S(2)}) async-start(), calls=%async_computation.32 | async-start | bytes 8847360 | tf_op jit(solution)/shard_map/all_gather | solution.py:552
  13.9 735.1 %all-gather.37.cloned.1.call-start = ((), (), s32[]{:S(2)}) async-start(), calls=%async_computation.33 | async-start | bytes 8847360 | tf_op jit(solution)/shard_map/all_gather | solution.py:553
  17.4 89.8 %copy-start.112 = (bf16[2,192,1152]{2,1,0:T(8,128)(2,1)S(1)}, bf16[2,192,1152]{2,1,0:T(8,128)(2,1)}, u32[]{:S(2)}) copy-start(bf16[2,192,1152]{2,1,0:T(8,128)(2,1)} %param.48) | copy-start | bytes 2654212
  17.4 90.8 %copy-start.431 = (f32[1,4,144]{2,1,0:T(4,128)S(1)}, f32[1,4,144]{2,1,0:T(4,128)}, u32[]{:S(2)}) copy-start(f32[1,4,144]{2,1,0:T(4,128)} %param.54) | copy-start | bytes 6916
  19.3 87.8 %copy-start.303 = (s32[1,1,192,1]{2,3,1,0:T(1,128)}, s32[1,1,192,1]{2,3,1,0:T(1,128)S(1)}, u32[]{:S(2)}) copy-start(s32[1,1,192,1]{2,3,1,0:T(1,128)S(1)} %get-tuple-element.3416) | copy-start | bytes 2308
  19.3 87.8 %copy-start.307 = (s32[1,1,192,1]{2,3,1,0:T(1,128)}, s32[1,1,192,1]{2,3,1,0:T(1,128)S(1)}, u32[]{:S(2)}) copy-start(s32[1,1,192,1]{2,3,1,0:T(1,128)S(1)} %get-tuple-element.3417) | copy-start | bytes 2308
  19.3 294.8 %copy-start.311 = (s32[1,1,192,1]{2,3,1,0:T(1,128)}, s32[1,1,192,1]{2,3,1,0:T(1,128)S(1)}, u32[]{:S(2)}) copy-start(s32[1,1,192,1]{2,3,1,0:T(1,128)S(1)} %get-tuple-element.3415) | copy-start | bytes 2308
  107.2 209.2 %copy-start.173 = (f32[1152]{0:T(1024)}, f32[1152]{0:T(1024)S(1)}, u32[]{:S(2)}) copy-start(f32[1152]{0:T(1024)S(1)} %convert_element_type.685) | copy-start | bytes 13828
  107.4 209.0 %copy-start.342 = (f32[192]{0:T(256)}, f32[192]{0:T(256)S(1)}, u32[]{:S(2)}) copy-start(f32[192]{0:T(256)S(1)} %fusion.516) | copy-start | bytes 2308
  108.1 286.5 %copy-start.436 = (pred[192]{0:T(512)(128)(4,1)}, pred[192]{0:T(512)(128)(4,1)S(1)}, u32[]{:S(2)}) copy-start(pred[192]{0:T(512)(128)(4,1)S(1)} %get-tuple-element.3437) | copy-start | bytes 580
  108.1 286.5 %copy-start.438 = (pred[192]{0:T(512)(128)(4,1)}, pred[192]{0:T(512)(128)(4,1)S(1)}, u32[]{:S(2)}) copy-start(pred[192]{0:T(512)(128)(4,1)S(1)} %get-tuple-element.3438) | copy-start | bytes 580
  108.1 286.5 %copy-start.440 = (pred[192]{0:T(512)(128)(4,1)}, pred[192]{0:T(512)(128)(4,1)S(1)}, u32[]{:S(2)}) copy-start(pred[192]{0:T(512)(128)(4,1)S(1)} %get-tuple-element.3439) | copy-start | bytes 580
  108.1 311.7 %copy-start.417 = (pred[192]{0:T(512)(128)(4,1)}, pred[192]{0:T(512)(128)(4,1)S(1)}, u32[]{:S(2)}) copy-start(pred[192]{0:T(512)(128)(4,1)S(1)} %get-tuple-element.3436) | copy-start | bytes 580
  165.7 104.3 %copy-start.295 = (f32[1,144,104]{2,1,0:T(8,128)S(1)}, f32[1,144,104]{2,1,0:T(8,128)}, u32[]{:S(2)}) copy-start(f32[1,144,104]{2,1,0:T(8,128)} %param.56) | copy-start | bytes 179716
  214.1 180.6 %copy-start.245 = (f32[2304]{0:T(1024)}, f32[2304]{0:T(1024)S(1)}, u32[]{:S(2)}) copy-start(f32[2304]{0:T(1024)S(1)} %get-tuple-element.2980) | copy-start | bytes 27652
  214.1 180.6 %copy-start.251 = (f32[2304]{0:T(1024)}, f32[2304]{0:T(1024)S(1)}, u32[]{:S(2)}) copy-start(f32[2304]{0:T(1024)S(1)} %get-tuple-element.2981) | copy-start | bytes 27652
  214.1 180.6 %copy-start.257 = (f32[2304]{0:T(1024)}, f32[2304]{0:T(1024)S(1)}, u32[]{:S(2)}) copy-start(f32[2304]{0:T(1024)S(1)} %get-tuple-element.2982) | copy-start | bytes 27652
  214.1 180.6 %copy-start.263 = (f32[2304]{0:T(1024)}, f32[2304]{0:T(1024)S(1)}, u32[]{:S(2)}) copy-start(f32[2304]{0:T(1024)S(1)} %get-tuple-element.2983) | copy-start | bytes 27652
  324.2 70.2 %collective-permute-start = (bf16[3,2304]{1,0:T(4,128)(2,1)S(1)}, bf16[3,2304]{1,0:T(4,128)(2,1)S(1)}, u32[]{:S(2)}, u32[]{:S(2)}) collective-permute-start(bf16[3,2304]{1,0:T(4,128)(2,1)S(1)} %slice.684), channel_id=1, source_target_pairs={{0,1},{1,2},{2,3},{4,5},{5,6},{6,7},{8,9},{9,10},{10,11},{12,13},{... | collective-permute-start | bytes 41480 | tf_op jit(solution)/shard_map/ppermute | solution.py:15
  397.4 267.8 %copy-start.6 = (bf16[192,2304]{1,0:T(8,128)(2,1)}, bf16[192,2304]{1,0:T(8,128)(2,1)S(1)}, u32[]{:S(2)}) copy-start(bf16[192,2304]{1,0:T(8,128)(2,1)S(1)} %get-tuple-element.3310) | copy-start | bytes 2654212
  673.3 98.3 %copy-start.16 = (f32[192,1152]{1,0:T(8,128)}, f32[192,1152]{1,0:T(8,128)S(1)}, u32[]{:S(2)}) copy-start(f32[192,1152]{1,0:T(8,128)S(1)} %get-tuple-element.3450) | copy-start | bytes 2654212
  674.1 87.9 %copy-start.82 = (bf16[192,1152]{1,0:T(8,128)(2,1)}, bf16[192,1152]{1,0:T(8,128)(2,1)S(1)}, u32[]{:S(2)}) copy-start(bf16[192,1152]{1,0:T(8,128)(2,1)S(1)} %multiply_convert_fusion.11) | copy-start | bytes 1327108
  676.9 63.7 %all-to-all-start = ((bf16[4,96,1152]{2,1,0:T(8,128)(2,1)}), bf16[4,96,1152]{2,1,0:T(8,128)(2,1)S(1)}, u32[]{:S(2)}, u32[]{:S(2)}) async-start(bf16[4,96,1152]{2,1,0:T(8,128)(2,1)} %bitcast.179), calls=%async_computation | async-start | bytes 1769472 | tf_op jit(solution)/shard_map/all_to_all | solution.py:262
  758.4 12.0 all-to-all-start.1
  771.9 2.7 collective-permute-start.1
  783.3 6.8 collective-permute-start.2
  793.1 273.4 %copy-start.9 = (bf16[192,2304]{1,0:T(8,128)(2,1)}, bf16[192,2304]{1,0:T(8,128)(2,1)S(1)}, u32[]{:S(2)}) copy-start(bf16[192,2304]{1,0:T(8,128)(2,1)S(1)} %get-tuple-element.3306) | copy-start | bytes 2654212
  1077.5 12.9 all-to-all-start.2
  1105.9 12.0 all-to-all-start.3
  1120.2 2.7 collective-permute-start.3
  1132.1 6.8 collective-permute-start.4
  1141.9 464.6 %copy-start.13 = (bf16[192,2304]{1,0:T(8,128)(2,1)}, bf16[192,2304]{1,0:T(8,128)(2,1)S(1)}, u32[]{:S(2)}) copy-start(bf16[192,2304]{1,0:T(8,128)(2,1)S(1)} %get-tuple-element.3304) | copy-start | bytes 2654212
  1197.5 295.7 %copy-start.25 = (f32[2304,16]{0,1:T(8,128)}, f32[2304,16]{0,1:T(8,128)S(1)}, u32[]{:S(2)}) copy-start(f32[2304,16]{0,1:T(8,128)S(1)} %get-tuple-element.4756) | copy-start | bytes 442372
  1436.5 168.7 %copy-start.18 = (f32[192,1152]{1,0:T(8,128)}, f32[192,1152]{1,0:T(8,128)S(1)}, u32[]{:S(2)}) copy-start(f32[192,1152]{1,0:T(8,128)S(1)} %get-tuple-element.3462) | copy-start | bytes 2654212
  1469.0 12.8 all-to-all-start.5
  1473.5 129.3 %copy-start.292 = (f32[192,4]{0,1:T(4,128)}, f32[192,4]{0,1:T(4,128)S(1)}, u32[]{:S(2)}) copy-start(f32[192,4]{0,1:T(4,128)S(1)} %get-tuple-element.3464) | copy-start | bytes 9220
  1473.6 129.3 %copy-start.340 = (f32[192]{0:T(256)}, f32[192]{0:T(256)S(1)}, u32[]{:S(2)}) copy-start(f32[192]{0:T(256)S(1)} %get-tuple-element.3463) | copy-start | bytes 2308
  1473.6 129.2 %copy-start.366 = (f32[192]{0:T(256)}, f32[192]{0:T(256)S(1)}, u32[]{:S(2)}) copy-start(f32[192]{0:T(256)S(1)} %fusion.512) | copy-start | bytes 2308
  1473.7 125.8 %copy-start.356 = (f32[192]{0:T(256)}, f32[192]{0:T(256)S(1)}, u32[]{:S(2)}) copy-start(f32[192]{0:T(256)S(1)} %select_reduce_fusion.16) | copy-start | bytes 2308
  1489.0 12.0 all-to-all-start.6
  1519.5 80.0 %all-to-all-start.7 = ((bf16[4,96,1152]{2,1,0:T(8,128)(2,1)}), bf16[4,96,1152]{2,1,0:T(8,128)(2,1)}, u32[]{:S(2)}, u32[]{:S(2)}) async-start(bf16[4,96,1152]{2,1,0:T(8,128)(2,1)} %bitcast.1801), calls=%async_computation.7 | async-start | bytes 1769472 | tf_op jit(solution)/shard_map/all_to_all | solution.py:376
  2336.5 6.1 collective-permute-start.5
  2347.5 3.8 collective-permute-start.6
  2354.6 16.3 all-to-all-start.8
  2389.4 87.7 %all-to-all-start.9 = ((bf16[4,96,1152]{2,1,0:T(8,128)(2,1)}), bf16[4,96,1152]{2,1,0:T(8,128)(2,1)S(1)}, u32[]{:S(2)}, u32[]{:S(2)}) async-start(bf16[4,96,1152]{2,1,0:T(8,128)(2,1)} %bitcast.1800), calls=%async_computation.9 | async-start | bytes 1769472 | tf_op jit(solution)/shard_map/all_to_all | solution.py:376
  3222.5 6.1 collective-permute-start.7
  3234.5 3.7 collective-permute-start.8
  3241.2 16.3 all-to-all-start.10
  3276.1 87.2 %all-to-all-start.11 = ((bf16[4,96,1152]{2,1,0:T(8,128)(2,1)}), bf16[4,96,1152]{2,1,0:T(8,128)(2,1)}, u32[]{:S(2)}, u32[]{:S(2)}) async-start(bf16[4,96,1152]{2,1,0:T(8,128)(2,1)} %bitcast.287), calls=%async_computation.11 | async-start | bytes 1769472 | tf_op jit(solution)/shard_map/all_to_all | solution.py:376
  3280.4 1059.4 %reduce-scatter.38.cloned.1.call-start = ((), (), s32[]{:S(2)}) async-start(), calls=%async_computation.37 | async-start | bytes 1253376
  4114.0 248.5 %reduce-scatter.42.cloned.1.call-start = ((), (), s32[]{:S(2)}) async-start(), calls=%async_computation.39 | async-start | bytes 1253376
  4116.8 373.7 %reduce-scatter.40.cloned.1.call-start = ((), (), s32[]{:S(2)}) async-start(), calls=%async_computation.38 | async-start | bytes 1253376
  4119.9 495.6 %reduce-scatter.20.cloned.1.call-start = ((), (), s32[]{:S(2)}) async-start(), calls=%async_computation.24 | async-start | bytes 8847360 | tf_op jit(solution)/shard_map/reduce_scatter | solution.py:501
  4127.3 614.5 %reduce-scatter.22.cloned.1.call-start = ((), (), s32[]{:S(2)}) async-start(), calls=%async_computation.25 | async-start | bytes 8847360 | tf_op jit(solution)/shard_map/reduce_scatter | solution.py:501
  4135.9 732.1 %reduce-scatter.24.cloned.1.call-start = ((), (), s32[]{:S(2)}) async-start(), calls=%async_computation.26 | async-start | bytes 8847360 | tf_op jit(solution)/shard_map/reduce_scatter | solution.py:501
  4144.5 849.8 %reduce-scatter.26.cloned.1.call-start = ((), (), s32[]{:S(2)}) async-start(), calls=%async_computation.27 | async-start | bytes 8847360 | tf_op jit(solution)/shard_map/reduce_scatter | solution.py:504
  4155.5 965.0 %reduce-scatter.28.cloned.1.call-start = ((), (), s32[]{:S(2)}) async-start(), calls=%async_computation.28 | async-start | bytes 8847360 | tf_op jit(solution)/shard_map/reduce_scatter | solution.py:504
  4166.5 1080.3 %reduce-scatter.30.cloned.1.call-start = ((), (), s32[]{:S(2)}) async-start(), calls=%async_computation.29 | async-start | bytes 8847360 | tf_op jit(solution)/shard_map/reduce_scatter | solution.py:504
  4177.6 1198.3 %reduce-scatter.34.cloned.1.call-start = ((), (), s32[]{:S(2)}) async-start(), calls=%async_computation.35 | async-start | bytes 1253376 | tf_op jit(solution)/shard_map/reduce_scatter | solution.py:491
  4181.5 1382.0 %reduce-scatter.36.cloned.1.call-start = ((), (), s32[]{:S(2)}) async-start(), calls=%async_computation.36 | async-start | bytes 11280384 | tf_op jit(solution)/shard_map/reduce_scatter | solution.py:496
  4191.0 1692.9 %reduce-scatter.32.cloned.1.call-start = ((), (), s32[]{:S(2)}) async-start(), calls=%async_computation.34 | async-start | bytes 22560768 | tf_op jit(solution)/shard_map/reduce_scatter | solution.py:488
  4221.8 6.0 collective-permute-start.9
  (822 other events, 7400.4 us)
Sparse Core Ops, SparseCore 0:
  11.4 157.9 all-gather.30
  172.7 101.7 all-gather.32
  276.1 139.6 all-gather.34
  417.8 129.0 all-gather.36
  4114.1 120.4 reduce-scatter.37
  4239.2 123.2 reduce-scatter.41
  4367.3 123.2 reduce-scatter.39
  4492.9 122.5 reduce-scatter.19
  4617.8 123.9 reduce-scatter.21
  4744.0 123.9 reduce-scatter.23
  4870.3 123.9 reduce-scatter.25
  4996.5 123.9 reduce-scatter.27
  5122.8 123.9 reduce-scatter.29
  5252.0 123.9 reduce-scatter.33
  5382.2 181.1 reduce-scatter.35
  5570.9 312.9 reduce-scatter.31
where the time goes:
time: 5920 us; the launch traced here: 5890 us
  other arithmetic  1700 us (29%)
  waiting for transfers between devices  1610 us (27%)
  matrix products  1070 us (18%)
  local copies, waits for them, and re-layouts  752 us (13%)
  blocking collectives  558 us (9%)
  loops' own time  108 us (2%)
  starting transfers between devices  63.7 us (1%)
    dot_general x108, matrix products, one_block(): inside = jnp.einsum('tscn,tsn,sc->tc', weight, paired, drive_part)  705 us
    reduce_sum x36, other arithmetic, one_block(): log_gap[..., None] * decay_rate  678 us
    reduce_scatter x3, waiting for transfers between devices, reduce_grads(): lax.psum_scatter(expert_grads[0].astype(jnp.bfloat16), 'dp', scatter_dime...  376 us
    reduce_scatter x3, waiting for transfers between devices, reduce_grads(): lax.psum_scatter(expert_grads[1].astype(jnp.bfloat16), 'dp', scatter_dime...  374 us
    reduce_scatter x1, waiting for transfers between devices, reduce_grads(): lax.psum_scatter(mamba_grads[1], ('dp', 'expert'), scatter_dimension=0, t...  320 us
    squeeze x432, local copies, waits for them, and re-layouts, block_scan(): _, outputs = lax.scan(jax.checkpoint(one_block), entry_state, pieces)  304 us
    dot_general x144, other arithmetic, one_block(): fresh_state = jnp.einsum('scn,sn,sc->cn', tail_weight, in_part, drive_part)  189 us
    reduce_scatter x1, waiting for transfers between devices, reduce_grads(): lax.psum_scatter(mamba_grads[9], ('dp', 'expert'), scatter_dimension=0, t...  187 us

commit v1 on v0

v1 whole, which is shorter than its diff:
```python
import functools
from types import SimpleNamespace

import jax
import jax.numpy as jnp
from jax import lax
from jax.experimental import pallas as pl
from jax.experimental.pallas import tpu as pltpu
from jax.sharding import PartitionSpec as P

epsilon = 1e-05
lanes = 128
group = 8
reset = 1e30


def row_of(tile, index, states):
    return jnp.broadcast_to(tile[index : index + 1, :], (states, tile.shape[1]))


def end_kernel(step_ref, act_ref, start_ref, in_ref, rate_ref, end_ref):
    rows, width = step_ref.shape
    states = rate_ref.shape[0]
    tiles = width // lanes
    cols = [slice(j * lanes, (j + 1) * lanes) for j in range(tiles)]

    def body(g, carry):
        state, total = carry
        at = pl.ds(pl.multiple_of(g * group, group), group)
        state = list(state)
        total = list(total)
        begin = start_ref[at, :]
        for j in range(tiles):
            step = step_ref[at, cols[j]]
            drive = step * act_ref[at, cols[j]].astype(jnp.float32)
            fall = step + begin
            total[j] = total[j] + fall
            rate = rate_ref[:, cols[j]]
            for i in range(group):
                decay = jnp.exp(row_of(fall, i, states) * rate)
                state[j] = decay * state[j] + row_of(drive, i, states) * in_ref[g * group + i]
        return tuple(state), tuple(total)

    zero = tuple(jnp.zeros((states, lanes), jnp.float32) for _ in range(tiles))
    none = tuple(jnp.zeros((group, lanes), jnp.float32) for _ in range(tiles))
    state, total = lax.fori_loop(0, rows // group, body, (zero, none))
    for j in range(tiles):
        end_ref[:states, cols[j]] = state[j]
        end_ref[states:, cols[j]] = total[j]


def scan_kernel(step_ref, act_ref, start_ref, in_ref, out_ref, rate_ref, entry_ref, skip_ref, y_ref):
    rows, width = step_ref.shape
    states = rate_ref.shape[0]
    tiles = width // lanes
    cols = [slice(j * lanes, (j + 1) * lanes) for j in range(tiles)]
    which = lax.broadcasted_iota(jnp.int32, (group, lanes), 0)

    def body(g, state):
        at = pl.ds(pl.multiple_of(g * group, group), group)
        state = list(state)
        begin = start_ref[at, :]
        for j in range(tiles):
            step = step_ref[at, cols[j]]
            act = act_ref[at, cols[j]].astype(jnp.float32)
            drive = step * act
            fall = step + begin
            rate = rate_ref[:, cols[j]]
            y = skip_ref[:, cols[j]] * act
            for i in range(group):
                decay = jnp.exp(row_of(fall, i, states) * rate)
                state[j] = decay * state[j] + row_of(drive, i, states) * in_ref[g * group + i]
                part = jnp.sum(state[j] * out_ref[g * group + i], axis=0, keepdims=True)
                y = y + jnp.where(which == i, part, 0.0)
            y_ref[at, cols[j]] = y
        return tuple(state)

    lax.fori_loop(
        0, rows // group, body, tuple(entry_ref[:, cols[j]] for j in range(tiles))
    )


def entry_kernel(step_ref, start_ref, out_ref, rate_ref, grad_ref, end_ref):
    rows, width = step_ref.shape
    states = rate_ref.shape[0]
    tiles = width // lanes
    cols = [slice(j * lanes, (j + 1) * lanes) for j in range(tiles)]
    groups = rows // group

    def body(k, state):
        g = groups - 1 - k
        at = pl.ds(pl.multiple_of(g * group, group), group)
        state = list(state)
        begin = start_ref[at, :]
        for j in range(tiles):
            fall = step_ref[at, cols[j]] + begin
            grad = grad_ref[at, cols[j]]
            rate = rate_ref[:, cols[j]]
            for i in reversed(range(group)):
                decay = jnp.exp(row_of(fall, i, states) * rate)
                state[j] = decay * (state[j] + row_of(grad, i, states) * out_ref[g * group + i])
        return tuple(state)

    zero = tuple(jnp.zeros((states, lanes), jnp.float32) for _ in range(tiles))
    state = lax.fori_loop(0, groups, body, zero)
    for j in range(tiles):
        end_ref[:, cols[j]] = state[j]


def back_kernel(
    step_ref, act_ref, start_ref, in_ref, out_ref, rate_ref, entry_ref, adj_ref, skip_ref, grad_ref,
    back_act_ref, back_step_ref, back_rate_ref, back_in_ref, back_out_ref, kept, decays,
):
    rows, width = step_ref.shape
    states = rate_ref.shape[0]
    tiles = width // lanes
    cols = [slice(j * lanes, (j + 1) * lanes) for j in range(tiles)]
    groups = rows // group
    which = lax.broadcasted_iota(jnp.int32, (group, lanes), 0)

    @pl.when(pl.program_id(0) == 0)
    def _():
        back_in_ref[...] = jnp.zeros_like(back_in_ref)
        back_out_ref[...] = jnp.zeros_like(back_out_ref)

    for j in range(tiles):
        kept[0, :, cols[j]] = entry_ref[:, cols[j]]

    def ahead(g, state):
        at = pl.ds(pl.multiple_of(g * group, group), group)
        state = list(state)
        begin = start_ref[at, :]
        for j in range(tiles):
            step = step_ref[at, cols[j]]
            drive = step * act_ref[at, cols[j]].astype(jnp.float32)
            fall = step + begin
            rate = rate_ref[:, cols[j]]
            for i in range(group):
                decay = jnp.exp(row_of(fall, i, states) * rate)
                decays[g * group + i, :, cols[j]] = decay
                state[j] = decay * state[j] + row_of(drive, i, states) * in_ref[g * group + i]
                kept[g * group + i + 1, :, cols[j]] = state[j]
        return tuple(state)

    lax.fori_loop(0, groups, ahead, tuple(entry_ref[:, cols[j]] for j in range(tiles)))

    def behind(k, carry):
        flow, slope = carry
        g = groups - 1 - k
        at = pl.ds(pl.multiple_of(g * group, group), group)
        flow = list(flow)
        slope = list(slope)
        back_in = [back_in_ref[g * group + i] for i in range(group)]
        back_out = [back_out_ref[g * group + i] for i in range(group)]
        for j in range(tiles):
            step = step_ref[at, cols[j]]
            act = act_ref[at, cols[j]].astype(jnp.float32)
            drive = step * act
            grad = grad_ref[at, cols[j]]
            rate = rate_ref[:, cols[j]]
            back_drive = jnp.zeros((group, lanes), jnp.float32)
            back_fall = jnp.zeros((group, lanes), jnp.float32)
            for i in reversed(range(group)):
                t = g * group + i
                grad_row = row_of(grad, i, states)
                adj = flow[j] + grad_row * out_ref[t]
                back_out[i] = back_out[i] + kept[t + 1, :, cols[j]] * grad_row
                back_in[i] = back_in[i] + adj * row_of(drive, i, states)
                part = jnp.sum(adj * in_ref[t], axis=0, keepdims=True)
                back_drive = back_drive + jnp.where(which == i, part, 0.0)
                flow[j] = adj * decays[t, :, cols[j]]
                turn = flow[j] * kept[t, :, cols[j]]
                part = jnp.sum(turn * rate, axis=0, keepdims=True)
                back_fall = back_fall + jnp.where(which == i, part, 0.0)
                slope[j] = slope[j] + row_of(step, i, states) * turn
            back_act_ref[at, cols[j]] = step * back_drive + skip_ref[:, cols[j]] * grad
            back_step_ref[at, cols[j]] = act * back_drive + back_fall
        for i in range(group):
            back_in_ref[g * group + i] = back_in[i]
            back_out_ref[g * group + i] = back_out[i]
        return tuple(flow), tuple(slope)

    zero = tuple(jnp.zeros((states, lanes), jnp.float32) for _ in range(tiles))
    _, slope = lax.fori_loop(
        0, groups, behind, (tuple(adj_ref[:, cols[j]] for j in range(tiles)), zero)
    )
    for j in range(tiles):
        back_rate_ref[:, cols[j]] = slope[j] * rate_ref[:, cols[j]]


def specs(rows, states, block):
    wide = pl.BlockSpec((rows, block), lambda c: (0, c))
    mark = pl.BlockSpec((rows, lanes), lambda c: (0, 0))
    maps = pl.BlockSpec((rows, states, lanes), lambda c: (0, 0, 0))
    held = pl.BlockSpec((states, block), lambda c: (0, c))
    line = pl.BlockSpec((1, block), lambda c: (0, c))
    total = pl.BlockSpec((states + group, block), lambda c: (0, c))
    return wide, mark, maps, held, line, total


def params(mib):
    return pltpu.CompilerParams(
        dimension_semantics=("arbitrary",), vmem_limit_bytes=mib * 1024 * 1024
    )


def block_of(width, most):
    best = lanes
    for tiles in range(1, most // lanes + 1):
        if width % (tiles * lanes) == 0:
            best = tiles * lanes
    return best


def f32(*shape):
    return jax.ShapeDtypeStruct(shape, jnp.float32)


def end_call(step, act, start, in_map, rate, block=None):
    rows, width = step.shape
    states = rate.shape[0]
    block = block or block_of(width, 384)
    wide, mark, maps, held, line, total = specs(rows, states, block)
    return pl.pallas_call(
        end_kernel,
        grid=(width // block,),
        in_specs=[wide, wide, mark, maps, held],
        out_specs=total,
        out_shape=f32(states + group, width),
        compiler_params=params(40),
        cost_estimate=pl.CostEstimate(flops=8 * rows * states * width, bytes_accessed=6 * rows * width, transcendentals=rows * states * width),
        name="state_end",
    )(step, act, start, in_map, rate)


def scan_call(step, act, start, in_map, out_map, rate, entry, skip, block=None):
    rows, width = step.shape
    states = rate.shape[0]
    block = block or block_of(width, 384)
    wide, mark, maps, held, line, total = specs(rows, states, block)
    return pl.pallas_call(
        scan_kernel,
        grid=(width // block,),
        in_specs=[wide, wide, mark, maps, maps, held, held, line],
        out_specs=wide,
        out_shape=f32(rows, width),
        compiler_params=params(40),
        cost_estimate=pl.CostEstimate(flops=12 * rows * states * width, bytes_accessed=10 * rows * width, transcendentals=rows * states * width),
        name="state_scan",
    )(step, act, start, in_map, out_map, rate, entry, skip)


def entry_call(step, start, out_map, rate, grad, block=None):
    rows, width = step.shape
    states = rate.shape[0]
    block = block or block_of(width, 384)
    wide, mark, maps, held, line, total = specs(rows, states, block)
    return pl.pallas_call(
        entry_kernel,
        grid=(width // block,),
        in_specs=[wide, mark, maps, held, wide],
        out_specs=held,
        out_shape=f32(states, width),
        compiler_params=params(40),
        cost_estimate=pl.CostEstimate(flops=8 * rows * states * width, bytes_accessed=8 * rows * width, transcendentals=rows * states * width),
        name="adjoint_entry",
    )(step, start, out_map, rate, grad)


def back_call(step, act, start, in_map, out_map, rate, entry, adj, skip, grad, block=None):
    rows, width = step.shape
    states = rate.shape[0]
    block = block or block_of(width, 384)
    wide, mark, maps, held, line, total = specs(rows, states, block)
    return pl.pallas_call(
        back_kernel,
        grid=(width // block,),
        in_specs=[wide, wide, mark, maps, maps, held, held, held, line, wide],
        out_specs=[wide, wide, held, maps, maps],
        out_shape=[
            f32(rows, width), f32(rows, width), f32(states, width),
            f32(rows, states, lanes), f32(rows, states, lanes),
        ],
        scratch_shapes=[
            pltpu.VMEM((rows + 1, states, block), jnp.float32),
            pltpu.VMEM((rows, states, block), jnp.float32),
        ],
        compiler_params=params(56),
        cost_estimate=pl.CostEstimate(flops=40 * rows * states * width, bytes_accessed=20 * rows * width, transcendentals=rows * states * width),
        name="scan_back",
    )(step, act, start, in_map, out_map, rate, entry, adj, skip, grad)


def from_behind(array, axis, by):
    length = lax.axis_size(axis)
    pairs = [(i, i + by) for i in range(length) if 0 <= i + by < length]
    return lax.ppermute(array, axis, pairs)


def norm_scale(residual, gain):
    return (
        residual * lax.rsqrt(jnp.mean(residual * residual, axis=-1, keepdims=True) + epsilon) * gain
    )


def product(left, right):
    return jnp.dot(left, right, preferred_element_type=jnp.float32)


def cross_rows(left, right):
    return lax.dot_general(
        left, right, (((0,), (0,)), ((), ())), preferred_element_type=jnp.float32
    )


def cross_cols(left, right):
    return lax.dot_general(
        left, right, (((1,), (1,)), ((), ())), preferred_element_type=jnp.float32
    )


def gate_product(values, gates):
    return values * jax.nn.silu(gates)


def doc_ids(lengths_row, positions):
    boundaries = jnp.cumsum(lengths_row, dtype=jnp.int32)
    counted = jnp.sum(
        (positions[:, None] >= boundaries[None, :]).astype(jnp.int32), axis=1, dtype=jnp.int32
    )
    return jnp.where(positions < 0, -1, counted)


def conv_act(wide_in, taps_weight, taps_bias, documents):
    tap_count = taps_weight.shape[0]
    row_count = wide_in.shape[0] - tap_count + 1
    own_docs = documents[tap_count - 1 :]
    summed = taps_bias + taps_weight[tap_count - 1] * wide_in[tap_count - 1 :]
    for offset in range(1, tap_count):
        start_row = tap_count - 1 - offset
        lagged = wide_in[start_row : start_row + row_count]
        same_doc = (documents[start_row : start_row + row_count] == own_docs)[:, None]
        summed = summed + taps_weight[start_row] * jnp.where(same_doc, lagged, 0.0)
    return jax.nn.silu(summed)


def dispatch_tables(chosen, capacity):
    indicator = chosen.astype(jnp.int32)
    row_count, expert_count = indicator.shape
    earlier_rows = jnp.cumsum(indicator, axis=0, dtype=jnp.int32) - indicator
    slot_rank = jnp.sum(earlier_rows * indicator, axis=1, dtype=jnp.int32)
    expert_of = jnp.sum(
        indicator * jnp.arange(expert_count, dtype=jnp.int32)[None, :], axis=1, dtype=jnp.int32
    )
    slot_index = expert_of * capacity + slot_rank
    all_slots = jnp.arange(expert_count * capacity, dtype=jnp.int32)
    matches = slot_index[None, :] == all_slots[:, None]
    token_index = jnp.sum(
        jnp.where(matches, jnp.arange(row_count, dtype=jnp.int32)[None, :], 0),
        axis=1,
        dtype=jnp.int32,
    )
    token_index = token_index + row_count * (1 - jnp.any(matches, axis=1).astype(jnp.int32))
    return (slot_index, token_index)


def gather_kernel(
    phase, along_dp, along_expert, own_refs, layer_refs,
    here_sem, z_send, z_recv, xy_send, xy_recv, c_send, c_recv,
):
    section = lax.axis_index("section")
    d = lax.axis_index("dp")
    e = lax.axis_index("expert")
    arrays = range(len(layer_refs[0]))
    mesh_id = pl.DeviceIdType.MESH
    ways = (1, -1)
    direct = [m for m in range(1, along_expert) if m != 3]

    def exists(index):
        return jnp.logical_and(index >= 0, index < along_dp)

    barrier = pltpu.get_barrier_semaphore()
    peers = [(section, d, e ^ m) for m in range(1, along_expert)] + [(1 - section, d, e)]
    for peer in peers:
        pl.semaphore_signal(barrier, inc=1, device_id=peer, device_id_type=mesh_id)
    expected = len(peers)
    if phase == 0:
        for way in ways:

            @pl.when(exists(d + way))
            def _():
                pl.semaphore_signal(
                    barrier, inc=1, device_id=(section, d + way, e), device_id_type=mesh_id
                )

        expected = expected + jnp.where(d > 0, 1, 0) + jnp.where(d < along_dp - 1, 1, 0)
    pl.semaphore_wait(barrier, expected)

    items = [(0, 0, 0)] + [
        (1 + 2 * step + (way < 0), way, step) for step in range(along_dp - 1) for way in ways
    ]

    def origin(item):
        index, way, step = item
        return d - way * (step + 1) if way else d

    def mine(item):
        if item[1] == 0:
            return phase == 0
        if item[2] > 0:
            return phase == 1
        return True if item[1] < 0 else phase == 0

    def here_now(item):
        if item[1] < 0 and item[2] == 0:
            return (d == 0) if phase == 0 else (d > 0)
        return d >= 0

    def when(item, *more):
        if item[1] == 0 and not more:
            return lambda work: work()
        alive = exists(origin(item))
        for other in more:
            alive = jnp.logical_and(alive, other)
        return pl.when(alive)

    def work(all_refs, other_refs):
        def place(item, m):
            return origin(item) * along_expert + (e ^ m)

        def copy(item, m, a, peer, send, recv):
            held = all_refs[a].at[place(item, m)]
            own = phase == 0 and item[1] == 0 and m == 0
            return pltpu.make_async_remote_copy(
                src_ref=own_refs[a] if own else held,
                dst_ref=held,
                send_sem=send,
                recv_sem=recv,
                device_id=peer,
                device_id_type=mesh_id,
            )

        def onward(item, way, a):
            step = item[2] + 1 if item[1] else 0
            k = 0 if way > 0 else 1
            peer = (section, d + way, e)
            return copy(item, 0, a, peer, z_send.at[k, step, a], z_recv.at[k, step, a])

        def to_expert(item, m, a):
            peer = (section, d, e ^ m)
            sems = (xy_send.at[item[0], m - 1, a], xy_recv.at[item[0], m - 1, a])
            return copy(item, 0, a, peer, *sems)

        def relayed(item, a):
            return 1 + (a + (item[2] + 1 if a == arrays[-1] else 0)) % 2

        def relay(item, m, a):
            peer = (section, d, e ^ 3 ^ m)
            sems = (xy_send.at[item[0], 2, a], xy_recv.at[item[0], 2, a])
            return copy(item, m, a, peer, *sems)

        def to_core(item, m, a):
            peer = (1 - section, d, e)
            return copy(item, m, a, peer, c_send.at[item[0], m, a], c_recv.at[item[0], m, a])

        def landed(ref, sem):
            pltpu.make_async_copy(ref, ref, sem).wait()

        def here(a):
            return pltpu.make_async_copy(
                own_refs[a], all_refs[a].at[place(items[0], 0)], here_sem.at[a]
            )

        def share(item):
            for a in arrays:
                for m in direct:
                    to_expert(item, m, a).start()

        def gather(item):
            for m in direct:
                for a in arrays:
                    landed(all_refs[a].at[place(item, m)], xy_recv.at[item[0], m - 1, a])
                    if m < 3 and relayed(item, a) == 3 - m:
                        relay(item, m, a).start()
                    to_core(item, m, a).start()

        def gather_last(item):
            for a in arrays:
                landed(all_refs[a].at[place(item, 3)], xy_recv.at[item[0], 2, a])
                to_core(item, 3, a).start()

        def finish_shared(item):
            for a in arrays:
                for m in direct:
                    to_expert(item, m, a).wait_send()
                relay(item, 3 - relayed(item, a), a).wait_send()
                for m in range(1, along_expert):
                    finish_core(item, m, a)

        def finish_core(item, m, a):
            to_core(item, m, a).wait_send()
            landed(other_refs[a].at[place(item, m)], c_recv.at[item[0], m, a])

        if phase == 0:
            for a in arrays:
                here(a).start()
                for way in ways:

                    @pl.when(exists(d + way))
                    def _():
                        onward(items[0], way, a).start()

                for m in direct:
                    to_expert(items[0], m, a).start()
                to_core(items[0], 0, a).start()
            queue = [items[0]]
            for step in range(along_dp - 1):
                for item in [item for item in items[1:] if item[2] == step]:
                    k = 0 if item[1] > 0 else 1

                    @when(item)
                    def _():
                        for a in arrays:
                            landed(all_refs[a].at[place(item, 0)], z_recv.at[k, step, a])

                    if step < along_dp - 2:

                        @when(item, exists(d + item[1]))
                        def _():
                            for a in arrays:
                                onward(item, item[1], a).start()

                    @when(item)
                    def _():
                        for a in arrays:
                            to_core(item, 0, a).start()

                    if mine(item):
                        when(item, here_now(item))(lambda: share(item))
                for item in queue:
                    when(item, here_now(item))(lambda: gather(item))
                queue = [item for item in items[1:] if item[2] == step and mine(item)]
            for item in queue:
                when(item, here_now(item))(lambda: gather(item))
            for item in items:
                if mine(item):
                    when(item, here_now(item))(lambda: gather_last(item))
            for a in arrays:
                here(a).wait()
            for item in items:
                if mine(item):
                    when(item, here_now(item))(lambda: finish_shared(item))

                @when(item)
                def _():
                    for a in arrays:
                        finish_core(item, 0, a)

                for way in ways if item[1] == 0 else (item[1],):
                    if item[1] == 0 or item[2] < along_dp - 2:

                        @when(item, exists(d + way))
                        def _():
                            for a in arrays:
                                onward(item, way, a).wait_send()
        else:
            rest = [item for item in items if mine(item)]
            for step in (share, gather, gather_last, finish_shared):
                for item in rest:
                    when(item, here_now(item))(lambda: step(item))

    @pl.when(section == 0)
    def _():
        work(layer_refs[0], layer_refs[1])

    @pl.when(section == 1)
    def _():
        work(layer_refs[1], layer_refs[0])


def gather_call(phase, parts, held=()):
    along_dp, along_expert = lax.axis_size("dp"), lax.axis_size("expert")
    total = len(parts) if phase == 0 else len(held) // 2
    given = parts if phase == 0 else held
    items = 2 * along_dp - 1

    def body(*refs):
        outs = refs[len(given) : len(given) + 2 * total]
        gather_kernel(
            phase, along_dp, along_expert, refs[: len(given)], (outs[:total], outs[total:]),
            *refs[len(given) + 2 * total :],
        )

    dma = pltpu.SemaphoreType.DMA
    shapes = [
        jax.ShapeDtypeStruct((along_dp * along_expert,) + part.shape, part.dtype)
        for part in parts
    ]
    return pl.pallas_call(
        body,
        in_specs=[pl.BlockSpec(memory_space=pltpu.HBM)] * len(given),
        out_specs=[pl.BlockSpec(memory_space=pltpu.HBM)] * (2 * total),
        out_shape=shapes * 2
        if phase == 0
        else [jax.ShapeDtypeStruct(part.shape, part.dtype) for part in held],
        input_output_aliases={} if phase == 0 else {k: k for k in range(2 * total)},
        scratch_shapes=[
            dma((total,)),
            dma((2, along_dp - 1, total)),
            dma((2, along_dp - 1, total)),
            dma((items, along_expert - 1, total)),
            dma((items, along_expert - 1, total)),
            dma((items, along_expert, total)),
            dma((items, along_expert, total)),
        ],
        compiler_params=pltpu.CompilerParams(collective_id=phase, has_side_effects=True),
        cost_estimate=pl.CostEstimate(flops=0, bytes_accessed=250 * 2**20, transcendentals=0),
        name="weights_along_dp" if phase == 0 else "weights_across",
    )(*given)


def carry_kernel(count, backward, *refs):
    if backward:
        end_ref, totals_ref, rate_ref, entry_ref, ends_ref, send_sem, recv_sem = refs
        shared = [ends_ref]
    else:
        end_ref, rate_ref, entry_ref, totals_ref, ends_ref, send_sem, recv_sem = refs
        shared = [ends_ref, totals_ref]
    states = rate_ref.shape[0]
    e = lax.axis_index("expert")
    mesh_id = pl.DeviceIdType.MESH

    def peer(m):
        return (lax.axis_index("section"), lax.axis_index("dp"), e ^ m)

    barrier = pltpu.get_barrier_semaphore()
    for m in range(1, count):
        pl.semaphore_signal(barrier, inc=1, device_id=peer(m), device_id_type=mesh_id)
    pl.semaphore_wait(barrier, count - 1)
    ends_ref[e] = end_ref[:states].astype(jnp.bfloat16)
    if not backward:
        totals_ref[e] = jnp.sum(end_ref[states:], axis=0, keepdims=True)

    def copy(m, a):
        return pltpu.make_async_remote_copy(
            src_ref=shared[a].at[e],
            dst_ref=shared[a].at[e],
            send_sem=send_sem.at[m - 1, a],
            recv_sem=recv_sem.at[m - 1, a],
            device_id=peer(m),
            device_id_type=mesh_id,
        )

    for m in range(1, count):
        for a in range(len(shared)):
            copy(m, a).start()
    for m in range(1, count):
        for a in range(len(shared)):
            there = shared[a].at[e ^ m]
            pltpu.make_async_copy(there, there, recv_sem.at[m - 1, a]).wait()
    width = rate_ref.shape[1]
    for start in range(0, width, lanes):
        cols = slice(start, start + lanes)
        state = jnp.zeros((states, lanes), jnp.float32)
        for k in range(count - 1, -1, -1) if backward else range(count):
            reached = jnp.where(k > e if backward else k < e, 1.0, 0.0)
            kept = jnp.exp(rate_ref[:, cols] * totals_ref[k, :, cols])
            new = kept * state + ends_ref[k, :, cols].astype(jnp.float32)
            state = state + reached * (new - state)
        entry_ref[:, cols] = state
    for m in range(1, count):
        for a in range(len(shared)):
            copy(m, a).wait_send()


def carry_call(end, rate, totals=None):
    count = lax.axis_size("expert")
    states, width = rate.shape
    backward = totals is not None
    dma = pltpu.SemaphoreType.DMA
    vmem = pl.BlockSpec(memory_space=pltpu.VMEM)
    operands = (end, totals, rate) if backward else (end, rate)
    total_shape = jax.ShapeDtypeStruct((count, 1, width), jnp.float32)
    out = pl.pallas_call(
        functools.partial(carry_kernel, count, backward),
        in_specs=[vmem] * len(operands),
        out_specs=[vmem] if backward else [vmem, vmem],
        out_shape=[f32(states, width)] + ([] if backward else [total_shape]),
        scratch_shapes=[
            pltpu.VMEM((count, states, width), jnp.bfloat16),
            dma((count - 1, 2)),
            dma((count - 1, 2)),
        ],
        compiler_params=pltpu.CompilerParams(
            collective_id=3 if backward else 2, has_side_effects=True
        ),
        name="adjoint_carry" if backward else "state_carry",
    )(*operands)
    return out


def swap(array):
    return lax.ppermute(array, "section", [(0, 1), (1, 0)])


def pick(first, left, right):
    return jnp.where(first, left, right), jnp.where(first, right, left)


def halves(array, first, axis):
    width = array.shape[axis] // 2
    low = lax.slice_in_dim(array, 0, width, axis=axis)
    high = lax.slice_in_dim(array, width, 2 * width, axis=axis)
    return pick(first, low, high)


def turned(array, axis, hop):
    length = lax.axis_size(axis)
    return lax.ppermute(array, axis, [(i, (i + hop) % length) for i in range(length)])


def crossed(array, axis, mask):
    length = lax.axis_size(axis)
    return lax.ppermute(array, axis, [(i, i ^ mask) for i in range(length)])


def expert_parts(up, down, first):
    pairs = [
        halves(master.astype(jnp.bfloat16), first, axis)
        for axis, master in enumerate((down, up))
    ]
    others = [swap(sent) for _, sent in pairs]
    down, up = [pick(first, own, got) for (own, _), got in zip(pairs, others)]
    return [up[0], down[0], up[1], down[1]]


def expert_spread(up, down):
    return tuple(
        lax.all_gather(part, ("section", "dp"), axis=axis, tiled=True)
        for axis, part in ((1, up), (0, down))
    )


def tie(values, after):
    count = len(values)

    def body(*refs):
        del refs

    return pl.pallas_call(
        body,
        in_specs=[pl.BlockSpec(memory_space=pl.ANY)] * (count + len(after)),
        out_specs=[pl.BlockSpec(memory_space=pl.ANY)] * count,
        out_shape=[jax.ShapeDtypeStruct(value.shape, value.dtype) for value in values],
        input_output_aliases={k: k for k in range(count)},
        name="order",
    )(*values, *after)


class LineSum:
    def __init__(self, up, down):
        self.parts = (up, down)
        self.here, self.count = lax.axis_index("dp"), lax.axis_size("dp")
        self.width = up.shape[0] // self.count
        self.step, self.moving = 0, (None, None)

    def chunk(self, index):
        start = jnp.clip(index, 0, self.count - 1) * self.width
        cuts = [lax.dynamic_slice_in_dim(part, start, self.width, 0) for part in self.parts]
        return jnp.stack(cuts).astype(jnp.float32)

    def advance(self, steps=1):
        for _ in range(steps):
            ahead = self.count - 1 - self.step
            if ahead == 0:
                break
            moved = []
            for way, moving in zip((1, -1), self.moving):
                held = self.chunk(self.here + way * ahead)
                if moving is not None:
                    held = held + moving.astype(jnp.float32)
                pairs = [
                    (i, i + way) for i in range(self.count) if 0 <= i + way * ahead < self.count
                ]
                moved.append(lax.ppermute(held.astype(jnp.bfloat16), "dp", pairs))
            self.moving = tuple(moved)
            self.step += 1
        return self.moving

    def total(self):
        up, down = self.advance(self.count)
        summed = self.chunk(self.here) + up.astype(jnp.float32) + down.astype(jnp.float32)
        return summed.astype(jnp.bfloat16)


def joined(pair, product_of):
    sent = swap(product_of(pair[1]).astype(jnp.bfloat16))
    return (product_of(pair[0]) + sent.astype(jnp.float32)).astype(jnp.bfloat16)


def by_expert(array, split):
    rows, width = array.shape
    across, along = lax.axis_size("dp"), lax.axis_size("expert")
    parts = array.reshape(rows, across, along, split, width // (across * along * split))
    return parts.transpose(0, 3, 2, 1, 4).reshape(rows, width)


def settle(total):
    part = lax.psum_scatter(total, "expert", scatter_dimension=0, tiled=True)
    return lax.psum_scatter(part, "dp", scatter_dimension=0, tiled=True)


def settle_direct(total):
    here, along = lax.axis_index("expert"), lax.axis_size("expert")
    width = total.shape[0] // along

    def chunk(array, index, size):
        return lax.dynamic_slice_in_dim(array, index * size, size, 0)

    summed = chunk(total, here, width).astype(jnp.float32)
    for mask in range(1, along):
        summed = summed + crossed(chunk(total, here ^ mask, width), "expert", mask).astype(
            jnp.float32
        )
    total = summed.astype(jnp.bfloat16)
    here, across = lax.axis_index("dp"), lax.axis_size("dp")
    width = width // across
    summed = chunk(total, here, width).astype(jnp.float32)
    for hop in range(1, across):
        there = lax.rem(here + hop, across)
        summed = summed + turned(chunk(total, there, width), "dp", hop).astype(jnp.float32)
    return summed.astype(jnp.bfloat16)


def hand_back(parts, first, cut):
    own, sent = pick(first, parts[0], parts[1])
    low, high = pick(first, own, swap(sent))
    return jnp.concatenate([low, high], axis=cut).astype(jnp.float32)


def widen(array):
    return jnp.pad(array, ((0, 0), (0, lanes - array.shape[1])))


def pack(select, step, rows, model):
    model = jnp.pad(model, ((0, 0), (0, rows.shape[1] - model.shape[1])))
    thin = jnp.concatenate([rows, model], axis=0).T
    return jnp.stack([widen(select), widen(step), widen(thin)])


def layer_forward(residual, small, big, routing, documents, mark, low_rank):
    conv_part, gate_part, output_weight, up_weight, down_weight = big
    row_count, model_width = residual.shape
    tap_count = small.conv.shape[0]
    states = small.rate.shape[0]
    expert_count = small.router.shape[0]
    capacity = 2 * row_count // expert_count
    normed = norm_scale(residual, small.mixer_gain).astype(jnp.bfloat16)
    conv_in = product(normed, conv_part).astype(jnp.bfloat16)
    gate_in = product(normed, gate_part).astype(jnp.bfloat16)
    rim_rows = from_behind(conv_in[row_count - tap_count + 1 :], "expert", 1)
    wide_in = jnp.concatenate([rim_rows, conv_in], axis=0)
    activated = conv_act(
        wide_in.astype(jnp.float32), small.conv, small.conv_bias, documents
    ).astype(jnp.bfloat16)
    projected = product(activated, small.select)
    step_low = jnp.where(jnp.arange(lanes) < low_rank, projected, 0.0).astype(jnp.bfloat16)
    in_wide = jnp.broadcast_to(
        projected[:, low_rank : low_rank + states, None], (row_count, states, lanes)
    )
    out_wide = jnp.broadcast_to(
        projected[:, low_rank + states : low_rank + 2 * states, None], (row_count, states, lanes)
    )
    step_pre = cross_cols(step_low, small.step) + small.step_bias
    step_size = jax.nn.softplus(step_pre)
    ends = end_call(step_size, activated, mark, in_wide, small.rate)
    entry_state, totals = carry_call(ends, small.rate)
    scanned = scan_call(
        step_size, activated, mark, in_wide, out_wide, small.rate, entry_state, small.skip
    )
    gated_out = gate_product(scanned, gate_in.astype(jnp.float32)).astype(jnp.bfloat16)
    middle = residual + product(gated_out, output_weight)
    normed_two = norm_scale(middle, small.expert_gain).astype(jnp.bfloat16)
    logits = cross_cols(normed_two, small.router)
    probability = jax.nn.softmax(logits, axis=-1)
    chosen = routing[:, None] == jnp.arange(expert_count, dtype=jnp.int32)[None, :]
    gate_value = jnp.sum(jnp.where(chosen, probability, 0.0), axis=1)
    slot_index, token_index = dispatch_tables(chosen, capacity)
    padded = jnp.concatenate([normed_two, jnp.zeros((1, model_width), jnp.bfloat16)], axis=0)
    outgoing = padded[token_index].reshape(expert_count, capacity, model_width)
    arrived = lax.all_to_all(outgoing, "expert", split_axis=0, concat_axis=0, tiled=True)
    flat_rows = arrived.reshape(-1, model_width)
    pre_act = product(flat_rows, up_weight)
    hidden = jax.nn.gelu(pre_act).astype(jnp.bfloat16)
    result = product(hidden, down_weight).astype(jnp.bfloat16).reshape(arrived.shape)
    returned = lax.all_to_all(result, "expert", split_axis=0, concat_axis=0, tiled=True)
    mixture = returned.reshape(-1, model_width)[slot_index].astype(jnp.float32)
    out_residual = middle + gate_value[:, None] * mixture
    stored = SimpleNamespace(
        residual=residual, normed=normed, wide_in=wide_in, gate_in=gate_in, activated=activated,
        step_low=step_low, step_pre=step_pre, step_size=step_size, in_wide=in_wide,
        out_wide=out_wide, totals=totals, entry_state=entry_state, scanned=scanned,
        gated_out=gated_out, middle=middle, normed_two=normed_two, probability=probability,
        chosen=chosen, gate_value=gate_value, slot_index=slot_index, token_index=token_index,
        pre_act=pre_act, hidden=hidden, flat_rows=flat_rows, mixture=mixture,
        documents=documents, mark=mark,
    )
    return out_residual, stored


def layer_backward(grad_out, kept, small, big, section, earlier, pending, ranks):
    conv_part, gate_part, output_weight, up_weight, down_weight = big
    first = section == 0
    row_count, model_width = grad_out.shape
    tap_count = small.conv.shape[0]
    expert_count = small.router.shape[0]
    capacity = 2 * row_count // expert_count
    back_gate = jnp.sum(grad_out * kept.mixture, axis=1)
    back_result = (kept.gate_value[:, None] * grad_out).astype(jnp.bfloat16)
    padded = jnp.concatenate([back_result, jnp.zeros((1, model_width), jnp.bfloat16)], axis=0)
    back_outgoing = padded[kept.token_index].reshape(expert_count, capacity, model_width)
    back_arrived = lax.all_to_all(back_outgoing, "expert", split_axis=0, concat_axis=0, tiled=True)
    back_flat = back_arrived.reshape(-1, model_width)
    back_hidden = cross_cols(back_flat, down_weight)
    back_pre = jax.vjp(jax.nn.gelu, kept.pre_act)[1](back_hidden)[0].astype(jnp.bfloat16)
    back_expert = cross_cols(back_pre, up_weight).astype(jnp.bfloat16).reshape(back_arrived.shape)
    if earlier is not None:
        (back_expert,) = tie([back_expert], earlier.moving)
        earlier.advance()
    back_returned = lax.all_to_all(back_expert, "expert", split_axis=0, concat_axis=0, tiled=True)
    grad_down = joined(halves(kept.hidden, first, 1), lambda half: cross_rows(half, back_flat))
    grad_up = joined(halves(back_pre, first, 1), lambda half: cross_rows(half, kept.flat_rows))
    line = LineSum(grad_up, grad_down)
    line.advance()
    back_tokens = back_returned.reshape(-1, model_width)[kept.slot_index].astype(jnp.float32)
    back_logits = (
        (back_gate * kept.gate_value)[:, None]
        * (kept.chosen.astype(jnp.float32) - kept.probability)
    ).astype(jnp.bfloat16)
    grad_router = cross_rows(back_logits, kept.normed_two)
    back_normed_two = back_tokens + product(back_logits, small.router)
    back_mid_norm, grad_expert_gain = jax.vjp(norm_scale, kept.middle, small.expert_gain)[1](
        back_normed_two
    )
    back_middle = grad_out + back_mid_norm
    back_branch = back_middle.astype(jnp.bfloat16)
    gated_pair = halves(by_expert(kept.gated_out, 2), first, 1)
    grad_output = joined(gated_pair, lambda half: cross_rows(half, back_branch))
    back_gated = cross_cols(back_branch, output_weight)
    back_scanned, back_gate_in = jax.vjp(
        gate_product, kept.scanned, kept.gate_in.astype(jnp.float32)
    )[1](back_gated)
    normed_rows = by_expert(kept.normed, 1)
    back_gate_in = back_gate_in.astype(jnp.bfloat16)
    grad_gate = joined(halves(back_gate_in, first, 1), lambda half: cross_rows(normed_rows, half))
    late = (settle(grad_gate), settle(grad_output))
    (back_scanned,) = tie([back_scanned], (grad_up, grad_down, grad_gate, grad_output))
    rate = small.rate
    back_ends = entry_call(kept.step_size, kept.mark, kept.out_wide, rate, back_scanned)
    (adjoint,) = carry_call(back_ends, rate, kept.totals)
    back_act, back_step, grad_decay, back_in, back_out = back_call(
        kept.step_size, kept.activated, kept.mark, kept.in_wide, kept.out_wide,
        rate, kept.entry_state, adjoint, small.skip, back_scanned,
    )
    (back_step,) = tie(
        [back_step], line.moving + pending + (() if earlier is None else earlier.moving)
    )
    line.advance()
    act_float = kept.activated.astype(jnp.float32)
    grad_skip = jnp.sum(back_scanned * act_float, axis=0, keepdims=True)
    back_step_pre = back_step * jax.nn.sigmoid(kept.step_pre)
    grad_step_bias = jnp.sum(back_step_pre, axis=0, keepdims=True)
    back_step_low = back_step_pre.astype(jnp.bfloat16)
    grad_step = cross_rows(back_step_low, kept.step_low)
    back_rank = product(back_step_low, small.step)
    low_rank = ranks - 2 * rate.shape[0]
    maps = jnp.concatenate([jnp.sum(back_in, axis=2), jnp.sum(back_out, axis=2)], axis=1)
    back_projected = back_rank + jnp.pad(maps, ((0, 0), (low_rank, lanes - ranks)))
    back_projected = back_projected.astype(jnp.bfloat16)
    grad_select = cross_rows(kept.activated, back_projected)
    back_activated = back_act + cross_cols(back_projected, small.select)

    def conv_piece(wide_float, taps_in, bias_in):
        return conv_act(wide_float, taps_in, bias_in, kept.documents)

    back_wide, grad_conv, grad_conv_bias = jax.vjp(
        conv_piece, kept.wide_in.astype(jnp.float32), small.conv, small.conv_bias
    )[1](back_activated)
    rim_back = from_behind(back_wide[: tap_count - 1], "expert", -1)
    back_conv_in = back_wide[tap_count - 1 :] + jnp.pad(
        rim_back, ((row_count - tap_count + 1, 0), (0, 0))
    )
    back_conv_in = back_conv_in.astype(jnp.bfloat16)
    grad_taps_in = joined(halves(back_conv_in, first, 1), lambda half: cross_rows(normed_rows, half))
    back_normed = cross_cols(back_conv_in, conv_part) + cross_cols(back_gate_in, gate_part)
    back_residual_norm, grad_mixer_gain = jax.vjp(
        norm_scale, kept.residual, small.mixer_gain
    )[1](back_normed)
    back_residual = back_middle + back_residual_norm
    lines = jnp.concatenate(
        [grad_conv, grad_decay, grad_conv_bias[None], grad_step_bias, grad_skip], axis=0
    )
    model = jnp.concatenate([grad_mixer_gain[None], grad_expert_gain[None], grad_router], axis=0)
    small_grads = (grad_select, grad_step, lines, model)
    return back_residual, grad_taps_in, late, line, small_grads


def doc_marks(documents, tap_count):
    own = documents[tap_count - 1 :]
    begins = own != documents[tap_count - 2 : -1]
    return jnp.broadcast_to(jnp.where(begins, reset, 0.0)[:, None], (own.shape[0], lanes))


def shards(
    inputs,
    cotangent,
    routes,
    lengths,
    mixer_gain,
    input_weight,
    conv_weight,
    conv_bias,
    select_weight,
    step_weight,
    step_bias,
    decay_log,
    skip_gain,
    output_weight,
    expert_gain,
    router_weight,
    up_weight,
    down_weight,
):
    section = lax.axis_index("section")
    first = section == 0
    count = lax.axis_size("dp") * lax.axis_size("expert")
    row_count, model_width = inputs.shape[1:]
    tap_count = conv_weight.shape[1]
    chan = conv_bias.shape[1]
    low_rank = step_weight.shape[1]
    states = decay_log.shape[2]
    ranks = select_weight.shape[2]
    expert_count = router_weight.shape[2]

    thin = tap_count + states + 3
    packed = pack(
        select_weight[0],
        step_weight[0].T,
        jnp.concatenate(
            [conv_weight[0], decay_log[0].T, conv_bias, step_bias, skip_gain], axis=0
        ),
        jnp.concatenate([mixer_gain, expert_gain, router_weight[0].T], axis=0),
    )
    wide = input_weight.shape[2] // 2
    experts = expert_parts(up_weight[0, 0], down_weight[0, 0], first)
    early = gather_call(
        0,
        (
            packed.astype(jnp.bfloat16),
            input_weight[0, :, :wide].astype(jnp.bfloat16),
            input_weight[0, :, wide:].astype(jnp.bfloat16),
            output_weight[0].astype(jnp.bfloat16),
        ),
    )
    experts = tie(experts, early[:1])
    gathered = gather_call(1, (), early)
    gathered = (gathered[:4], gathered[4:])
    part = model_width // count

    def unpack(layer):
        select, step, rows = [
            gathered[layer][0][:, k].reshape(count * chan, lanes) for k in range(3)
        ]
        rows = rows.T[: thin + 2 + expert_count].astype(jnp.float32)
        model = rows[thin:].reshape(-1, count, chan)[:, :, :part].reshape(-1, model_width)
        return SimpleNamespace(
            select=select, step=step, conv=rows[:tap_count],
            rate=-jnp.exp(rows[tap_count : tap_count + states]),
            conv_bias=rows[thin - 3], step_bias=rows[thin - 2 : thin - 1],
            skip=rows[thin - 1 : thin], mixer_gain=model[0], expert_gain=model[1],
            router=model[2:].astype(jnp.bfloat16),
        )

    small = [unpack(0), unpack(1)]
    experts_two = [expert_spread(*experts[:2]), expert_spread(*experts[2:])]
    big = [
        (
            gathered[k][1].reshape(model_width, wide),
            gathered[k][2].reshape(model_width, wide),
            gathered[k][3].reshape(wide, model_width),
        )
        + experts_two[k]
        for k in range(2)
    ]

    own_routes, sent_routes = pick(first, routes[0, 0, :, 0], routes[0, 1, :, 0])
    routing = pick(first, own_routes, swap(sent_routes))
    lengths_row = lax.dynamic_index_in_dim(lengths[:, 0, :], section, 0, keepdims=False)
    positions = lax.axis_index("expert") * row_count + jnp.arange(
        1 - tap_count, row_count, dtype=jnp.int32
    )
    documents = doc_ids(lengths_row, positions)
    mark = doc_marks(documents, tap_count)

    residual = lax.dynamic_index_in_dim(inputs, section, 0, keepdims=False).astype(jnp.float32)
    outputs_seen = []
    kept = []
    for layer in range(2):
        out_residual, stored = layer_forward(
            residual, small[layer], big[layer], routing[layer], documents, mark, low_rank
        )
        outputs_seen.append(out_residual.astype(jnp.bfloat16))
        residual = outputs_seen[-1].astype(jnp.float32)
        kept.append(stored)

    grad_out = lax.dynamic_index_in_dim(cotangent, section, 0, keepdims=False).astype(jnp.float32)
    input_grads = [None, None]
    settled = [None, None]
    small_sums = [None, None]
    line, pending = None, ()
    for layer in (1, 0):
        earlier = line
        back_residual, grad_taps_in, late, line, small_grads = layer_backward(
            grad_out, kept[layer], small[layer], big[layer], section, earlier, pending, ranks
        )
        input_grads[layer] = back_residual
        grad_out = back_residual.astype(jnp.bfloat16).astype(jnp.float32)
        if layer == 1:
            pending = (settle(grad_taps_in),) + late
        else:
            settled[1] = pending + (earlier.total(),)
            final_late = late + (line.total(),)
        across, along = lax.axis_size("dp"), lax.axis_size("expert")
        grad_select, grad_step, rows, model = small_grads
        model = model.reshape(-1, count, part)
        model = jnp.pad(model, ((0, 0), (0, 0), (0, chan - part))).reshape(-1, count * chan)
        rows = widen(jnp.concatenate([rows, model], axis=0).T)
        whole = jnp.stack(
            [array.reshape(across, along, chan, lanes) for array in (grad_select, grad_step, rows)],
            axis=2,
        ).astype(jnp.bfloat16)
        small_sums[layer] = whole.transpose(1, 0, 2, 3, 4).reshape(count, -1, model_width)

    own_small, sent_small = pick(first, small_sums[0], small_sums[1])
    own_small = own_small.astype(jnp.float32) + swap(sent_small).astype(jnp.float32)
    last = jnp.concatenate(
        [grad_taps_in.reshape(count, part, -1), own_small.astype(jnp.bfloat16)], axis=1
    )
    last = settle_direct(last.reshape(-1, model_width))
    settled[0] = (last[:part],) + final_late
    total = last[part:].reshape(3, chan, lanes).astype(jnp.float32)
    rows = total[2].T
    model = rows[thin : thin + 2 + expert_count, :part]

    def whole_input():
        taps = hand_back((settled[0][0], settled[1][0]), first, 1)
        return jnp.concatenate([taps, hand_back((settled[0][1], settled[1][1]), first, 1)], axis=1)

    experts_back = hand_back((settled[0][3], settled[1][3]), first, 1)
    def both(array):
        mine, sent = pick(first, array[0], array[1])
        return jnp.stack(pick(first, mine, swap(sent)))[None]

    return (
        both(outputs_seen),
        both(input_grads),
        model[:1],
        whole_input()[None],
        rows[:tap_count][None],
        rows[thin - 3 : thin - 2],
        total[0, :, :ranks][None],
        total[1, :, :low_rank].T[None],
        rows[thin - 2 : thin - 1],
        rows[tap_count : tap_count + states].T[None],
        rows[thin - 1 : thin],
        hand_back((settled[0][2], settled[1][2]), first, 0)[None],
        model[1:2],
        model[2:].T[None],
        experts_back[0].T[None, None],
        experts_back[1][None, None],
    )


def solution(mesh):
    return jax.shard_map(
        shards,
        mesh=mesh,
        in_specs=(
            P(None, ("dp", "expert"), None),
            P(None, ("dp", "expert"), None),
            P("section", None, ("dp", "expert"), None),
            P(None, "dp", None),
            P("section", ("dp", "expert")),
            P("section", ("dp", "expert"), None),
            P("section", None, ("dp", "expert")),
            P("section", ("dp", "expert")),
            P("section", ("dp", "expert"), None),
            P("section", None, ("dp", "expert")),
            P("section", ("dp", "expert")),
            P("section", ("dp", "expert"), None),
            P("section", ("dp", "expert")),
            P("section", ("dp", "expert"), None),
            P("section", ("dp", "expert")),
            P("section", ("dp", "expert"), None),
            P("section", "expert", None, "dp"),
            P("section", "expert", "dp", None),
        ),
        out_specs=(
            P("section", None, ("dp", "expert"), None),
            P("section", None, ("dp", "expert"), None),
            P("section", ("dp", "expert")),
            P("section", ("dp", "expert"), None),
            P("section", None, ("dp", "expert")),
            P("section", ("dp", "expert")),
            P("section", ("dp", "expert"), None),
            P("section", None, ("dp", "expert")),
            P("section", ("dp", "expert")),
            P("section", ("dp", "expert"), None),
            P("section", ("dp", "expert")),
            P("section", ("dp", "expert"), None),
            P("section", ("dp", "expert")),
            P("section", ("dp", "expert"), None),
            P("section", "expert", None, "dp"),
            P("section", "expert", "dp", None),
        ),
        check_vma=False,
    )
```

time: 5920 us -> 1120 us (0.19)
  other arithmetic: 1700 us -> 119 us
  waiting for transfers between devices: 1610 us -> 148 us
  matrix products: 1070 us -> 223 us
  local copies, waits for them, and re-layouts: 752 us -> 141 us
  blocking collectives: 558 us -> 0 us
  Pallas kernels: 0 us -> 355 us
  loops' own time: 108 us -> 0 us
    reduce_scatter x9 -> x5, waiting for transfers between devices: 1380 us -> 0.03 us  [settle(): part = lax.psum_scatter(total, 'expert', scatter_dimension=0, tiled=True)]
    reduce_sum x230 -> x11, other arithmetic: 890 us -> 17.2 us  [the longest x1 4.7 us: conv_act(): summed = summed + taps_weight[start_row] * jnp.where(same_doc, lagged, 0.0)]
    dot_general x180 -> x0, matrix products: 759 us -> none  [the longest x108 705 us: one_block(): inside = jnp.einsum('tscn,tsn,sc->tc', weight, paired, drive_part)]
    all_gather x17 -> x0, blocking collectives: 391 us -> none  [the longest x6 62.3 us: prefix(): everything = jax.tree.map(lambda part: lax.all_gather(part, axis), array)]
    pallas_call x0 -> x20, Pallas kernels: none -> 355 us  [the longest x2 177 us: gather_call(): pl.pallas_call(body, in_specs=[pl.BlockSpec(memory_space=pltpu.HBM)] * le...]
    squeeze x432 -> x2, local copies, waits for them, and re-layouts: 304 us -> 0.1 us  [shards(): rows = total[2].T]
    dot_general x222 -> x0, other arithmetic: 285 us -> none  [the longest x144 189 us: one_block(): fresh_state = jnp.einsum('scn,sn,sc->cn', tail_weight, in_part, drive_part)]
    unnamed x2 -> x0, blocking collectives: 154 us -> none
where the time goes in v1:
time: 1120 us; the launch traced here: 1110 us
  Pallas kernels  355 us (32%)
  matrix products  223 us (20%)
  waiting for transfers between devices  148 us (13%)
  local copies, waits for them, and re-layouts  141 us (13%)
  other arithmetic  119 us (11%)
  starting transfers between devices  103 us (9%)
  between operations  18 us (2%)
    pallas_call x2, Pallas kernels, gather_call(): pl.pallas_call(body, in_specs=[pl.BlockSpec(memory_space=pltpu.HBM)] * le...  177 us
    dot_general x26, matrix products, cross_rows(): lax.dot_general(left, right, (((0,), (0,)), ((), ())), preferred_element_...  87.2 us
    pallas_call x2, Pallas kernels, back_call(): pl.pallas_call(back_kernel, grid=(width // block,), in_specs=[wide, wide,...  74.6 us
    dot_general x16, matrix products, cross_cols(): lax.dot_general(left, right, (((1,), (1,)), ((), ())), preferred_element_...  73.3 us
    dot_general x16, matrix products, product(): return jnp.dot(left, right, preferred_element_type=jnp.float32)  62 us
    unnamed x471, local copies, waits for them, and re-layouts  52.4 us
    ppermute x12, starting transfers between devices, advance(): moved.append(lax.ppermute(held.astype(jnp.bfloat16), 'dp', pairs))  47.1 us
    ppermute x3, waiting for transfers between devices, crossed(): return lax.ppermute(array, axis, [(i, i ^ mask) for i in range(length)])  44.4 us
  transfers between devices with their start and end apart: 64, of which 16 were waited for; matrix products, arithmetic and copies ran while one was open for 37% of the time, Pallas kernels for 32%

profile of v1, /device:TPU:0, one launch (start us, length us, event | category | flops | bytes accessed | tf_op | source)
XLA Modules:
  0.0 1106.6 jit_solution(12199505879155378146)
XLA Ops:
  18.4 94.2 %weights_along_dp.1 = (bf16[16,3,144,128]{3,2,1,0:T(8,128)(2,1)}, bf16[16,72,2304]{2,1,0:T(8,128)(2,1)}, bf16[16,72,2304]{2,1,0:T(8,128)(2,1)}, bf16[16,144,1152...) custom-call(bf16[3,144,128]{2,1,0:T(8,128)(2,1)} %pad_maximum_fusion, ...), custom_call_target="tpu_custom_call" | custom-call | bytes 262144000 | tf_op jit(solution)/shard_map/weights_along_dp/pallas_call | solution.py:599
  124.7 83.3 %weights_across.1 = (bf16[16,3,144,128]{3,2,1,0:T(8,128)(2,1)}, bf16[16,72,2304]{2,1,0:T(8,128)(2,1)}, bf16[16,72,2304]{2,1,0:T(8,128)(2,1)}, bf16[16,144,1152]{...) custom-call(bf16[16,3,144,128]{3,2,1,0:T(8,128)(2,1)} %get-tuple-ele, ...), custom_call_target="tpu_custom_call", output_to_operand_aliasing={{0}: (0, {}), {1}: (1, {}), {2}: (2, {}), {3}: (3, {}), {4}... | custom-call | bytes 262144000 | tf_op jit(solution)/shard_map/weights_across/pallas_call | solution.py:599
  210.1 4.1 convolution_convert_fusion.13
  228.3 8.8 state_end.2.refs_0_
  237.7 9.3 state_carry.2
  250.1 14.3 %state_scan.2 = f32[192,2304]{1,0:T(8,128)S(1)} custom-call(f32[192,2304]{1,0:T(8,128)S(1)} %copy-done.31, bf16[192,2304]{1,0:T(8,128)(2,1)S(1)} %get-tuple-element.239.act_ref, f32[192,128]{1,0:T(8,128)S(1)} %broadcast_in_dim.281.start_ref, f32[192,16,128]{2,1,0:T(8,128)S(1)} %broadcast_in_dim.282.in_ref, f32[192,16,128]{2,1,0:T(8,128)S(1)} %broadcast_in_dim.283.out_ref, ...), custom_call_target="tpu_custom_call" | custom-call | flops 84934656 | bytes 4423680 | tf_op jit(solution)/shard_map/state_scan/pallas_call | solution.py:241
  264.4 6.2 multiply_convert_fusion.4
  278.8 11.4 %all-to-all-done = bf16[4,96,1152]{2,1,0:T(8,128)(2,1)S(1)} async-done(((bf16[4,96,1152]{2,1,0:T(8,128)(2,1)}), bf16[4,96,1152]{2,1,0:T(8,128)(2,1)S(1)}, u32[]{:S(2)}, u32[]{:S(2)}) %all-to-all-start) | async-done | bytes 884768 | tf_op jit(solution)/shard_map/all_to_all | solution.py:891
  290.2 9.6 multiply_convert_fusion.1
  299.8 7.9 convolution_convert_fusion.21
  311.7 10.9 all-to-all-done.1
  341.4 8.8 state_end.3.refs_0_
  352.2 9.7 state_carry.3
  364.9 14.3 %state_scan.3 = f32[192,2304]{1,0:T(8,128)S(1)} custom-call(f32[192,2304]{1,0:T(8,128)S(1)} %copy-done.34, bf16[192,2304]{1,0:T(8,128)(2,1)S(1)} %get-tuple-element.235.act_ref, f32[192,128]{1,0:T(8,128)S(1)} %broadcast_in_dim.281.start_ref, f32[192,16,128]{2,1,0:T(8,128)S(1)} %broadcast_in_dim.287.in_ref, f32[192,16,128]{2,1,0:T(8,128)S(1)} %broadcast_in_dim.288.out_ref, ...), custom_call_target="tpu_custom_call" | custom-call | flops 84934656 | bytes 4423680 | tf_op jit(solution)/shard_map/state_scan/pallas_call | solution.py:241
  379.3 5.8 multiply_convert_fusion.2
  398.3 5.9 all-to-all-done.4
  407.9 9.5 fusion.243
  417.4 11.6 %fusion.13 = (bf16[384,3072]{1,0:T(8,128)(2,1)}, bf16[384,3072]{1,0:T(8,128)(2,1)S(1)}) fusion(f32[384,3072]{1,0:T(8,128)} %fusion.243, bf16[384,1152]{1,0:T(8,128)(2,1)S(1)} %bitcast.402, bf16[1152,3072]{1,0:T(8,128)(2,1)} %all-gather.9.cloned.1.call-done), kind=kOutput, calls=%fused_computation.47 | convolution fusion | flops 2743861248 | bytes 17399808 | tf_op jit(solution)/shard_map/dot_general | solution.py:307
  429.0 4.1 convolution_convert_fusion.20
  433.2 4.2 all-to-all-start.3
  437.4 7.9 convolution_convert_fusion.19
  463.6 5.7 fusion.164
  485.6 4.2 add_convert_fusion.9.refs_3_
  497.8 4.3 add_convert_fusion.3.refs_1_
  502.1 5.5 add_convert_fusion.2.refs_2_
  514.4 4.5 collective-permute-start.10
  526.8 4.3 add_convert_fusion.8.refs_4_
  535.7 8.4 adjoint_entry.2.refs_0_
  544.7 12.3 %adjoint_carry.2.adj_ref = f32[16,2304]{1,0:T(8,128)} custom-call(f32[16,2304]{1,0:T(8,128)} %copy-done.22, f32[4,1,2304]{2,1,0:T(1,128)} %get-tuple-element.72.refs_1_, f32[16,2304]{1,0:T(8,128)} %copy-done.18), custom_call_target="tpu_custom_call" | custom-call | tf_op jit(solution)/shard_map/adjoint_carry/pallas_call | solution.py:684
  557.1 37.3 %scan_back.2 = (f32[192,2304]{1,0:T(8,128)}, f32[192,2304]{1,0:T(8,128)}, f32[16,2304]{1,0:T(8,128)}, f32[192,16,128]{2,1,0:T(8,128)}, f32[192,16,128]{2,1,0:T(8,128)}) custom-call(f32[192,2304]{1,0:T(8,128)} %copy-done.33, bf16[192,2304]{1,0:T(8,128)(2,1)} %copy-done.4, f32[192,128]{1,0:T(8,128)} %copy-done.24, f32[192,16,128]{2,1,0:T(8,128)} %copy-done.13, ...), custom_call_target="tpu_custom_call" | custom-call | flops 283115520 | bytes 8847360 | tf_op jit(solution)/shard_map/scan_back/pallas_call | solution.py:275
  625.3 5.7 fusion.245
  636.9 4.3 add_convert_fusion.5
  642.4 4.9 fusion.79
  650.7 4.2 all-to-all-start.6
  660.9 12.4 %all-to-all-done.6 = bf16[4,96,1152]{2,1,0:T(8,128)(2,1)} async-done(((bf16[4,96,1152]{2,1,0:T(8,128)(2,1)}), bf16[4,96,1152]{2,1,0:T(8,128)(2,1)}, u32[]{:S(2)}, u32[]{:S(2)}) %all-to-all-start.6) | async-done | bytes 884768 | tf_op jit(solution)/shard_map/all_to_all | solution.py:922
  673.3 8.5 fusion.6
  681.8 8.1 convolution_convert_fusion.18
  693.9 6.0 convolution_convert_fusion.7
  700.0 5.1 convolution_convert_fusion.6
  713.5 5.8 fusion.163
  728.2 6.2 add_convert_fusion.refs_2_
  734.7 5.5 dynamic-slice_bitcast_fusion.10
  740.2 6.1 add_convert_fusion.1.refs_1_
  746.3 4.2 add_convert_fusion.7.refs_3_
  750.6 5.5 dynamic-slice_bitcast_fusion.11
  763.7 14.0 %collective-permute-start.19 = (bf16[2,384,1152]{2,1,0:T(8,128)(2,1)}, bf16[2,384,1152]{2,1,0:T(8,128)(2,1)}, u32[]{:S(2)}, u32[]{:S(2)}) collective-permute-start(bf16[2,384,1152]{2,1,0:T(8,128)(2,1)} %pad_maximum_fusion.3), channel_id=1, source_target_pairs={{0,4},{1,5},{2,6},{3,7},{16,20},{17,21},{18,22},{19,23}} | collective-permute-start | bytes 5308424 | tf_op jit(solution)/shard_map/ppermute | solution.py:785
  792.5 30.6 %collective-permute-done.19.refs_1_ = bf16[2,384,1152]{2,1,0:T(8,128)(2,1)} collective-permute-done((bf16[2,384,1152]{2,1,0:T(8,128)(2,1)}, bf16[2,384,1152]{2,1,0:T(8,128)(2,1)}, u32[]{:S(2)}, u32[]{:S(2)}) %collective-permute-start.19) | collective-permute-done | bytes 1769504 | tf_op jit(solution)/shard_map/ppermute | solution.py:785
  826.4 5.6 collective-permute-start.37
  837.5 5.3 fusion.247
  842.8 4.3 add_convert_fusion.6.refs_4_
  851.4 8.4 adjoint_entry.3.refs_0_
  860.5 8.4 adjoint_carry.3.adj_ref
  868.9 37.3 %scan_back.3 = (f32[192,2304]{1,0:T(8,128)}, f32[192,2304]{1,0:T(8,128)}, f32[16,2304]{1,0:T(8,128)}, f32[192,16,128]{2,1,0:T(8,128)}, f32[192,16,128]{2,1,0:T(8,128)}) custom-call(f32[192,2304]{1,0:T(8,128)} %copy-done.30, bf16[192,2304]{1,0:T(8,128)(2,1)} %copy-done.2, f32[192,128]{1,0:T(8,128)} %copy-done.24, f32[192,16,128]{2,1,0:T(8,128)} %copy-done.10, ...), custom_call_target="tpu_custom_call" | custom-call | flops 283115520 | bytes 8847360 | tf_op jit(solution)/shard_map/scan_back/pallas_call | solution.py:275
  920.2 7.4 collective-permute-start.38
  933.6 4.7 multiply_reduce_fusion.4
  950.2 4.8 fusion.97
  964.6 4.5 select_n.576
  970.0 6.3 broadcast_select_fusion.2
  981.1 4.8 reshape.689
  989.0 4.3 add_convert_fusion.16
  999.2 5.2 copy.231
  1019.4 20.0 %collective-permute-done.30 = bf16[480,1152]{1,0:T(8,128)(2,1)S(1)} collective-permute-done((bf16[480,1152]{1,0:T(8,128)(2,1)}, bf16[480,1152]{1,0:T(8,128)(2,1)S(1)}, u32[]{:S(2)}, u32[]{:S(2)}) %collective-permute-start.30) | collective-permute-done | bytes 1105952 | tf_op jit(solution)/shard_map/ppermute | solution.py:724
  1039.3 23.2 %collective-permute-done.29 = bf16[480,1152]{1,0:T(8,128)(2,1)} collective-permute-done((bf16[480,1152]{1,0:T(8,128)(2,1)}, bf16[480,1152]{1,0:T(8,128)(2,1)}, u32[]{:S(2)}, u32[]{:S(2)}) %collective-permute-start.29) | collective-permute-done | bytes 1105952 | tf_op jit(solution)/shard_map/ppermute | solution.py:724
  1075.9 17.6 %collective-permute-done.32 = bf16[120,1152]{1,0:T(8,128)(2,1)S(1)} collective-permute-done((bf16[120,1152]{1,0:T(8,128)(2,1)S(1)}, bf16[120,1152]{1,0:T(8,128)(2,1)S(1)}, u32[]{:S(2)}, u32[]{:S(2)}) %collective-permute-start.32) | collective-permute-done | bytes 276512 | tf_op jit(solution)/shard_map/ppermute | solution.py:719
  (892 shorter events, 351.5 us)
Async XLA Ops:
  7.2 283.0 %all-gather.5.cloned.1.call-start = ((), (), s32[]{:S(2)}) async-start(), calls=%async_computation.18 | async-start | bytes 7962624 | tf_op jit(solution)/shard_map/all_gather | solution.py:739
  10.9 101.6 %collective-permute-start.2 = (bf16[1152,384]{1,0:T(8,128)(2,1)}, bf16[1152,384]{1,0:T(8,128)(2,1)}, u32[]{:S(2)}, u32[]{:S(2)}) collective-permute-start(bf16[1152,384]{1,0:T(8,128)(2,1)} %broadcast_select_fusion.7), channel_id=1, source_target_pairs={{0,16},{16,0},{1,17},{17,1},{2,18},{18,2},{3,19},{19,3},{4,20},{20... | collective-permute-start | bytes 2654216 | tf_op jit(solution)/shard_map/ppermute | solution.py:703
  14.6 101.0 %collective-permute-start.3 = (bf16[384,1152]{1,0:T(8,128)(2,1)}, bf16[384,1152]{1,0:T(8,128)(2,1)S(1)}, u32[]{:S(2)}, u32[]{:S(2)}) collective-permute-start(bf16[384,1152]{1,0:T(8,128)(2,1)} %select_bitcast_fusion.3), channel_id=1, source_target_pairs={{0,16},{16,0},{1,17},{17,1},{2,18},{18,2},{3,19},{19,3},{4,20},{20... | collective-permute-start | bytes 2654216 | tf_op jit(solution)/shard_map/ppermute | solution.py:703
  117.1 182.7 %all-gather.7.cloned.1.call-start = ((), (), s32[]{:S(2)}) async-start(), calls=%async_computation.19 | async-start | bytes 7962624 | tf_op jit(solution)/shard_map/all_gather | solution.py:739
  117.8 290.1 %all-gather.11.cloned.1.call-start = ((), (), s32[]{:S(2)}) async-start(), calls=%async_computation.21 | async-start | bytes 7962624 | tf_op jit(solution)/shard_map/all_gather | solution.py:739
  118.6 298.8 %all-gather.9.cloned.1.call-start = ((), (), s32[]{:S(2)}) async-start(), calls=%async_computation.20 | async-start | bytes 7962624 | tf_op jit(solution)/shard_map/all_gather | solution.py:739
  118.6 2.1 collective-permute-start.1
  214.2 6.3 collective-permute-start
  275.0 15.2 %all-to-all-start = ((bf16[4,96,1152]{2,1,0:T(8,128)(2,1)}), bf16[4,96,1152]{2,1,0:T(8,128)(2,1)S(1)}, u32[]{:S(2)}, u32[]{:S(2)}) async-start(bf16[4,96,1152]{2,1,0:T(8,128)(2,1)} %bitcast.30), calls=%async_computation | async-start | bytes 1769472 | tf_op jit(solution)/shard_map/all_to_all | solution.py:891
  307.7 14.9 %all-to-all-start.1 = ((bf16[4,96,1152]{2,1,0:T(8,128)(2,1)}), bf16[4,96,1152]{2,1,0:T(8,128)(2,1)S(1)}, u32[]{:S(2)}, u32[]{:S(2)}) async-start(bf16[4,96,1152]{2,1,0:T(8,128)(2,1)} %bitcast.35), calls=%async_computation.1 | async-start | bytes 1769472 | tf_op jit(solution)/shard_map/all_to_all | solution.py:896
  328.4 5.2 collective-permute-start.4
  392.0 12.2 %all-to-all-start.4 = ((bf16[4,96,1152]{2,1,0:T(8,128)(2,1)}), bf16[4,96,1152]{2,1,0:T(8,128)(2,1)S(1)}, u32[]{:S(2)}, u32[]{:S(2)}) async-start(bf16[4,96,1152]{2,1,0:T(8,128)(2,1)} %bitcast.59), calls=%async_computation.4 | async-start | bytes 1769472 | tf_op jit(solution)/shard_map/all_to_all | solution.py:922
  404.2 13.2 %all-to-all-start.2 = ((bf16[4,96,1152]{2,1,0:T(8,128)(2,1)}), bf16[4,96,1152]{2,1,0:T(8,128)(2,1)S(1)}, u32[]{:S(2)}, u32[]{:S(2)}) async-start(bf16[4,96,1152]{2,1,0:T(8,128)(2,1)} %bitcast.48), calls=%async_computation.2 | async-start | bytes 1769472 | tf_op jit(solution)/shard_map/all_to_all | solution.py:891
  433.2 12.7 %all-to-all-start.3 = ((bf16[4,96,1152]{2,1,0:T(8,128)(2,1)}), bf16[4,96,1152]{2,1,0:T(8,128)(2,1)S(1)}, u32[]{:S(2)}, u32[]{:S(2)}) async-start(bf16[4,96,1152]{2,1,0:T(8,128)(2,1)} %bitcast.50), calls=%async_computation.3 | async-start | bytes 1769472 | tf_op jit(solution)/shard_map/all_to_all | solution.py:896
  445.9 12.2 %all-to-all-start.5 = ((bf16[4,96,1152]{2,1,0:T(8,128)(2,1)}), bf16[4,96,1152]{2,1,0:T(8,128)(2,1)S(1)}, u32[]{:S(2)}, u32[]{:S(2)}) async-start(bf16[4,96,1152]{2,1,0:T(8,128)(2,1)} %bitcast.405), calls=%async_computation.5 | async-start | bytes 1769472 | tf_op jit(solution)/shard_map/all_to_all | solution.py:930
  449.6 261.1 %reduce-scatter.23.cloned.1.call-start = ((), (), s32[]{:S(2)}) async-start(), calls=%async_computation.23 | async-start | bytes 3317760 | tf_op jit(solution)/shard_map/reduce_scatter | solution.py:809
  471.8 13.8 %collective-permute-start.8 = (bf16[1152,1152]{1,0:T(8,128)(2,1)}, bf16[1152,1152]{1,0:T(8,128)(2,1)}, u32[]{:S(2)}, u32[]{:S(2)}) collective-permute-start(bf16[1152,1152]{1,0:T(8,128)(2,1)} %convolution_convert_fusion.5), channel_id=1, source_target_pairs={{0,16},{16,0},{1,17},{17,1},{2,18},{18,2},{3,19},{19,3},{4,20},{20... | collective-permute-start | bytes 7962632 | tf_op jit(solution)/shard_map/ppermute | solution.py:703
  476.4 21.3 %collective-permute-start.6 = (bf16[1536,1152]{1,0:T(8,128)(2,1)}, bf16[1536,1152]{1,0:T(8,128)(2,1)}, u32[]{:S(2)}, u32[]{:S(2)}) collective-permute-start(bf16[1536,1152]{1,0:T(8,128)(2,1)} %convolution_convert_fusion.9), channel_id=1, source_target_pairs={{0,16},{16,0},{1,17},{17,1},{2,18},{18,2},{3,19},{19,3},{4,20},{20... | collective-permute-start | bytes 10616840 | tf_op jit(solution)/shard_map/ppermute | solution.py:703
  480.4 21.7 %collective-permute-start.7 = (bf16[1536,1152]{1,0:T(8,128)(2,1)}, bf16[1536,1152]{1,0:T(8,128)(2,1)}, u32[]{:S(2)}, u32[]{:S(2)}) collective-permute-start(bf16[1536,1152]{1,0:T(8,128)(2,1)} %convolution_convert_fusion.8), channel_id=1, source_target_pairs={{0,16},{16,0},{1,17},{17,1},{2,18},{18,2},{3,19},{19,3},{4,20},{20... | collective-permute-start | bytes 10616840 | tf_op jit(solution)/shard_map/ppermute | solution.py:703
  489.8 231.9 %reduce-scatter.25.cloned.1.call-start = ((), (), s32[]{:S(2)}) async-start(), calls=%async_computation.24 | async-start | bytes 3317760 | tf_op jit(solution)/shard_map/reduce_scatter | solution.py:809
  497.7 29.1 %collective-permute-start.9 = (bf16[1152,1152]{1,0:T(8,128)(2,1)}, bf16[1152,1152]{1,0:T(8,128)(2,1)}, u32[]{:S(2)}, u32[]{:S(2)}) collective-permute-start(bf16[1152,1152]{1,0:T(8,128)(2,1)} %convolution_convert_fusion.4), channel_id=1, source_target_pairs={{0,16},{16,0},{1,17},{17,1},{2,18},{18,2},{3,19},{19,3},{4,20},{20... | collective-permute-start | bytes 7962632 | tf_op jit(solution)/shard_map/ppermute | solution.py:703
  514.4 82.5 %collective-permute-start.10 = (bf16[2,384,1152]{2,1,0:T(8,128)(2,1)}, bf16[2,384,1152]{2,1,0:T(8,128)(2,1)}, u32[]{:S(2)}, u32[]{:S(2)}) collective-permute-start(bf16[2,384,1152]{2,1,0:T(8,128)(2,1)} %pad_maximum_fusion.1), channel_id=1, source_target_pairs={{0,4},{1,5},{2,6},{3,7},{16,20},{17,21},{18,22},{19,23}} | collective-permute-start | bytes 5308424 | tf_op jit(solution)/shard_map/ppermute | solution.py:785
  520.4 76.6 %collective-permute-start.11 = (bf16[2,384,1152]{2,1,0:T(8,128)(2,1)}, bf16[2,384,1152]{2,1,0:T(8,128)(2,1)}, u32[]{:S(2)}, u32[]{:S(2)}) collective-permute-start(bf16[2,384,1152]{2,1,0:T(8,128)(2,1)} %pad_maximum_fusion.2), channel_id=1, source_target_pairs={{12,8},{13,9},{14,10},{15,11},{28,24},{29,25},{30,26},{31,27}} | collective-permute-start | bytes 5308424 | tf_op jit(solution)/shard_map/ppermute | solution.py:785
  531.1 203.3 %reduce-scatter.21.cloned.1.call-start = ((), (), s32[]{:S(2)}) async-start(), calls=%async_computation.22 | async-start | bytes 3317760 | tf_op jit(solution)/shard_map/reduce_scatter | solution.py:809
  605.0 5.9 collective-permute-start.12
  613.5 23.3 %collective-permute-start.21 = (bf16[1152,1152]{1,0:T(8,128)(2,1)}, bf16[1152,1152]{1,0:T(8,128)(2,1)}, u32[]{:S(2)}, u32[]{:S(2)}) collective-permute-start(bf16[1152,1152]{1,0:T(8,128)(2,1)} %convolution_convert_fusion.1), channel_id=1, source_target_pairs={{0,16},{16,0},{1,17},{17,1},{2,18},{18,2},{3,19},{19,3},{4,20},{20... | collective-permute-start | bytes 7962632 | tf_op jit(solution)/shard_map/ppermute | solution.py:703
  624.9 96.9 %collective-permute-start.5 = (bf16[192,1152]{1,0:T(8,128)(2,1)}, bf16[192,1152]{1,0:T(8,128)(2,1)}, u32[]{:S(2)}, u32[]{:S(2)}) collective-permute-start(bf16[192,1152]{1,0:T(8,128)(2,1)} %get-tuple-element.233), channel_id=1, source_target_pairs={{0,16},{16,0},{1,17},{17,1},{2,18},{18,2},{3,19},{19,3},{4,20},{20... | collective-permute-start | bytes 1327112 | tf_op jit(solution)/shard_map/ppermute | solution.py:703
  634.2 55.8 %collective-permute-start.13 = (bf16[2,384,1152]{2,1,0:T(8,128)(2,1)}, bf16[2,384,1152]{2,1,0:T(8,128)(2,1)}, u32[]{:S(2)}, u32[]{:S(2)}) collective-permute-start(bf16[2,384,1152]{2,1,0:T(8,128)(2,1)} %add_convert_fusion.20), channel_id=1, source_target_pairs={{0,4},{4,8},{1,5},{5,9},{2,6},{6,10},{3,7},{7,11},{16,20},{20,24},... | collective-permute-start | bytes 5308424 | tf_op jit(solution)/shard_map/ppermute | solution.py:785
  650.7 22.5 %all-to-all-start.6 = ((bf16[4,96,1152]{2,1,0:T(8,128)(2,1)}), bf16[4,96,1152]{2,1,0:T(8,128)(2,1)}, u32[]{:S(2)}, u32[]{:S(2)}) async-start(bf16[4,96,1152]{2,1,0:T(8,128)(2,1)} %bitcast.379), calls=%async_computation.6 | async-start | bytes 1769472 | tf_op jit(solution)/shard_map/all_to_all | solution.py:922
  658.8 31.1 %collective-permute-start.14 = (bf16[2,384,1152]{2,1,0:T(8,128)(2,1)}, bf16[2,384,1152]{2,1,0:T(8,128)(2,1)}, u32[]{:S(2)}, u32[]{:S(2)}) collective-permute-start(bf16[2,384,1152]{2,1,0:T(8,128)(2,1)} %add_convert_fusion.19), channel_id=1, source_target_pairs={{8,4},{12,8},{9,5},{13,9},{10,6},{14,10},{11,7},{15,11},{24,20},{2... | collective-permute-start | bytes 5308424 | tf_op jit(solution)/shard_map/ppermute | solution.py:785
  689.9 15.9 %all-to-all-start.7 = ((bf16[4,96,1152]{2,1,0:T(8,128)(2,1)}), bf16[4,96,1152]{2,1,0:T(8,128)(2,1)S(1)}, u32[]{:S(2)}, u32[]{:S(2)}) async-start(bf16[4,96,1152]{2,1,0:T(8,128)(2,1)} %order.9), calls=%async_computation.7 | async-start | bytes 1769472 | tf_op jit(solution)/shard_map/all_to_all | solution.py:930
  693.5 234.2 %reduce-scatter.33.cloned.1.call-start = ((), (), s32[]{:S(2)}) async-start(), calls=%async_computation.28 | async-start | bytes 829440
  699.9 40.3 %collective-permute-start.15 = (bf16[1536,1152]{1,0:T(8,128)(2,1)}, bf16[1536,1152]{1,0:T(8,128)(2,1)}, u32[]{:S(2)}, u32[]{:S(2)}) collective-permute-start(bf16[1536,1152]{1,0:T(8,128)(2,1)} %convolution_convert_fusion.7), channel_id=1, source_target_pairs={{0,16},{16,0},{1,17},{17,1},{2,18},{18,2},{3,19},{19,3},{4,20},{20... | collective-permute-start | bytes 10616840 | tf_op jit(solution)/shard_map/ppermute | solution.py:703
  705.1 23.1 %collective-permute-start.16 = (bf16[1536,1152]{1,0:T(8,128)(2,1)}, bf16[1536,1152]{1,0:T(8,128)(2,1)}, u32[]{:S(2)}, u32[]{:S(2)}) collective-permute-start(bf16[1536,1152]{1,0:T(8,128)(2,1)} %convolution_convert_fusion.6), channel_id=1, source_target_pairs={{0,16},{16,0},{1,17},{17,1},{2,18},{18,2},{3,19},{19,3},{4,20},{20... | collective-permute-start | bytes 10616840 | tf_op jit(solution)/shard_map/ppermute | solution.py:703
  710.7 216.9 %reduce-scatter.35.cloned.1.call-start = ((), (), s32[]{:S(2)}) async-start(), calls=%async_computation.29 | async-start | bytes 829440
  721.7 24.6 %collective-permute-start.17 = (bf16[1152,1152]{1,0:T(8,128)(2,1)}, bf16[1152,1152]{1,0:T(8,128)(2,1)}, u32[]{:S(2)}, u32[]{:S(2)}) collective-permute-start(bf16[1152,1152]{1,0:T(8,128)(2,1)} %convolution_convert_fusion.3), channel_id=1, source_target_pairs={{0,16},{16,0},{1,17},{17,1},{2,18},{18,2},{3,19},{19,3},{4,20},{20... | collective-permute-start | bytes 7962632 | tf_op jit(solution)/shard_map/ppermute | solution.py:703
  721.7 206.0 %reduce-scatter.31.cloned.1.call-start = ((), (), s32[]{:S(2)}) async-start(), calls=%async_computation.27 | async-start | bytes 829440
  734.5 235.1 %reduce-scatter.27.cloned.1.call-start = ((), (), s32[]{:S(2)}) async-start(), calls=%async_computation.25 | async-start | bytes 3317760 | tf_op jit(solution)/shard_map/reduce_scatter | solution.py:809
  750.6 238.4 %reduce-scatter.29.cloned.1.call-start = ((), (), s32[]{:S(2)}) async-start(), calls=%async_computation.26 | async-start | bytes 3317760 | tf_op jit(solution)/shard_map/reduce_scatter | solution.py:809
  757.5 29.8 %collective-permute-start.20 = (bf16[2,384,1152]{2,1,0:T(8,128)(2,1)}, bf16[2,384,1152]{2,1,0:T(8,128)(2,1)}, u32[]{:S(2)}, u32[]{:S(2)}) collective-permute-start(bf16[2,384,1152]{2,1,0:T(8,128)(2,1)} %pad_maximum_fusion.4), channel_id=1, source_target_pairs={{12,8},{13,9},{14,10},{15,11},{28,24},{29,25},{30,26},{31,27}} | collective-permute-start | bytes 5308424 | tf_op jit(solution)/shard_map/ppermute | solution.py:785
  763.7 59.4 %collective-permute-start.19 = (bf16[2,384,1152]{2,1,0:T(8,128)(2,1)}, bf16[2,384,1152]{2,1,0:T(8,128)(2,1)}, u32[]{:S(2)}, u32[]{:S(2)}) collective-permute-start(bf16[2,384,1152]{2,1,0:T(8,128)(2,1)} %pad_maximum_fusion.3), channel_id=1, source_target_pairs={{0,4},{1,5},{2,6},{3,7},{16,20},{17,21},{18,22},{19,23}} | collective-permute-start | bytes 5308424 | tf_op jit(solution)/shard_map/ppermute | solution.py:785
  781.2 61.6 %collective-permute-start.18 = (bf16[1152,1152]{1,0:T(8,128)(2,1)}, bf16[1152,1152]{1,0:T(8,128)(2,1)}, u32[]{:S(2)}, u32[]{:S(2)}) collective-permute-start(bf16[1152,1152]{1,0:T(8,128)(2,1)} %convolution_convert_fusion.2), channel_id=1, source_target_pairs={{0,16},{16,0},{1,17},{17,1},{2,18},{18,2},{3,19},{19,3},{4,20},{20... | collective-permute-start | bytes 7962632 | tf_op jit(solution)/shard_map/ppermute | solution.py:703
  784.8 142.8 %collective-permute-start.22 = (bf16[2,384,1152]{2,1,0:T(8,128)(2,1)}, bf16[2,384,1152]{2,1,0:T(8,128)(2,1)}, u32[]{:S(2)}, u32[]{:S(2)}) collective-permute-start(bf16[2,384,1152]{2,1,0:T(8,128)(2,1)} %add_convert_fusion.18), channel_id=1, source_target_pairs={{0,4},{4,8},{8,12},{1,5},{5,9},{9,13},{2,6},{6,10},{10,14},{3,7},{... | collective-permute-start | bytes 5308424 | tf_op jit(solution)/shard_map/ppermute | solution.py:785
  790.6 121.1 %collective-permute-start.39 = (bf16[2,384,1152]{2,1,0:T(8,128)(2,1)}, bf16[2,384,1152]{2,1,0:T(8,128)(2,1)}, u32[]{:S(2)}, u32[]{:S(2)}) collective-permute-start(bf16[2,384,1152]{2,1,0:T(8,128)(2,1)} %add_convert_fusion.13), channel_id=1, source_target_pairs={{8,4},{12,8},{9,5},{13,9},{10,6},{14,10},{11,7},{15,11},{24,20},{2... | collective-permute-start | bytes 5308424 | tf_op jit(solution)/shard_map/ppermute | solution.py:785
  826.4 90.6 %collective-permute-start.37 = (bf16[2,384,1152]{2,1,0:T(8,128)(2,1)}, bf16[2,384,1152]{2,1,0:T(8,128)(2,1)}, u32[]{:S(2)}, u32[]{:S(2)}) collective-permute-start(bf16[2,384,1152]{2,1,0:T(8,128)(2,1)} %add_convert_fusion.15), channel_id=1, source_target_pairs={{0,4},{4,8},{1,5},{5,9},{2,6},{6,10},{3,7},{7,11},{16,20},{20,24},... | collective-permute-start | bytes 5308424 | tf_op jit(solution)/shard_map/ppermute | solution.py:785
  835.3 92.4 %collective-permute-start.23 = (bf16[2,384,1152]{2,1,0:T(8,128)(2,1)}, bf16[2,384,1152]{2,1,0:T(8,128)(2,1)}, u32[]{:S(2)}, u32[]{:S(2)}) collective-permute-start(bf16[2,384,1152]{2,1,0:T(8,128)(2,1)} %add_convert_fusion.17), channel_id=1, source_target_pairs={{4,0},{8,4},{12,8},{5,1},{9,5},{13,9},{6,2},{10,6},{14,10},{7,3},{... | collective-permute-start | bytes 5308424 | tf_op jit(solution)/shard_map/ppermute | solution.py:785
  911.7 103.7 %reduce-scatter.37.cloned.1.call-start = ((), (), s32[]{:S(2)}) async-start(), calls=%async_computation.30 | async-start | bytes 829440
  915.7 54.2 %collective-permute-start.40 = (bf16[2,384,1152]{2,1,0:T(8,128)(2,1)}, bf16[2,384,1152]{2,1,0:T(8,128)(2,1)}, u32[]{:S(2)}, u32[]{:S(2)}) collective-permute-start(bf16[2,384,1152]{2,1,0:T(8,128)(2,1)} %add_convert_fusion.12), channel_id=1, source_target_pairs={{4,0},{8,4},{12,8},{5,1},{9,5},{13,9},{6,2},{10,6},{14,10},{7,3},{... | collective-permute-start | bytes 5308424 | tf_op jit(solution)/shard_map/ppermute | solution.py:785
  920.2 49.8 %collective-permute-start.38 = (bf16[2,384,1152]{2,1,0:T(8,128)(2,1)}, bf16[2,384,1152]{2,1,0:T(8,128)(2,1)}, u32[]{:S(2)}, u32[]{:S(2)}) collective-permute-start(bf16[2,384,1152]{2,1,0:T(8,128)(2,1)} %add_convert_fusion.14), channel_id=1, source_target_pairs={{0,4},{4,8},{8,12},{1,5},{5,9},{9,13},{2,6},{6,10},{10,14},{3,7},{... | collective-permute-start | bytes 5308424 | tf_op jit(solution)/shard_map/ppermute | solution.py:785
  939.1 9.4 collective-permute-start.24
  956.3 30.0 %collective-permute-start.25 = (f32[192,1152]{1,0:T(8,128)}, f32[192,1152]{1,0:T(8,128)}, u32[]{:S(2)}, u32[]{:S(2)}) collective-permute-start(f32[192,1152]{1,0:T(8,128)} %get-tuple-element.227), channel_id=1, source_target_pairs={{0,16},{16,0},{1,17},{17,1},{2,18},{18,2},{3,19},{19,3},{4,20},{20... | collective-permute-start | bytes 2654216 | tf_op jit(solution)/shard_map/ppermute | solution.py:703
  969.1 19.9 %collective-permute-start.27 = (bf16[16,48,1152]{2,1,0:T(8,128)(2,1)}, bf16[16,48,1152]{2,1,0:T(8,128)(2,1)}, u32[]{:S(2)}, u32[]{:S(2)}) collective-permute-start(bf16[16,48,1152]{2,1,0:T(8,128)(2,1)} %select_n.576), channel_id=1, source_target_pairs={{0,16},{16,0},{1,17},{17,1},{2,18},{18,2},{3,19},{19,3},{4,20},{20... | collective-permute-start | bytes 5308424 | tf_op jit(solution)/shard_map/ppermute | solution.py:703
  969.6 48.6 %reduce-scatter.39.cloned.1.call-start = ((), (), s32[]{:S(2)}) async-start(), calls=%async_computation.31 | async-start | bytes 829440
  976.3 17.0 %collective-permute-start.41 = (bf16[2,384,1152]{2,1,0:T(8,128)(2,1)}, bf16[2,384,1152]{2,1,0:T(8,128)(2,1)}, u32[]{:S(2)}, u32[]{:S(2)}) collective-permute-start(bf16[2,384,1152]{2,1,0:T(8,128)(2,1)} %get-tuple-element.219), channel_id=1, source_target_pairs={{0,16},{16,0},{1,17},{17,1},{2,18},{18,2},{3,19},{19,3},{4,20},{20... | collective-permute-start | bytes 5308424 | tf_op jit(solution)/shard_map/ppermute | solution.py:703
  985.8 18.5 %collective-permute-start.26 = (bf16[1152,1152]{1,0:T(8,128)(2,1)}, bf16[1152,1152]{1,0:T(8,128)(2,1)}, u32[]{:S(2)}, u32[]{:S(2)}) collective-permute-start(bf16[1152,1152]{1,0:T(8,128)(2,1)} %convolution_convert_fusion), channel_id=1, source_target_pairs={{0,16},{16,0},{1,17},{17,1},{2,18},{18,2},{3,19},{19,3},{4,20},{20... | collective-permute-start | bytes 7962632 | tf_op jit(solution)/shard_map/ppermute | solution.py:703
  1010.3 29.1 %collective-permute-start.30 = (bf16[480,1152]{1,0:T(8,128)(2,1)}, bf16[480,1152]{1,0:T(8,128)(2,1)S(1)}, u32[]{:S(2)}, u32[]{:S(2)}) collective-permute-start(bf16[480,1152]{1,0:T(8,128)(2,1)} %get-tuple-element.248), channel_id=1, source_target_pairs={{0,3},{1,2},{2,1},{3,0},{4,7},{5,6},{6,5},{7,4},{8,11},{9,10},{10,... | collective-permute-start | bytes 3317768 | tf_op jit(solution)/shard_map/ppermute | solution.py:724
  1013.9 48.6 %collective-permute-start.29 = (bf16[480,1152]{1,0:T(8,128)(2,1)}, bf16[480,1152]{1,0:T(8,128)(2,1)}, u32[]{:S(2)}, u32[]{:S(2)}) collective-permute-start(bf16[480,1152]{1,0:T(8,128)(2,1)} %get-tuple-element.249), channel_id=1, source_target_pairs={{0,2},{1,3},{2,0},{3,1},{4,6},{5,7},{6,4},{7,5},{8,10},{9,11},{10,... | collective-permute-start | bytes 3317768 | tf_op jit(solution)/shard_map/ppermute | solution.py:724
  1014.4 49.3 %collective-permute-start.28 = (bf16[480,1152]{1,0:T(8,128)(2,1)S(1)}, bf16[480,1152]{1,0:T(8,128)(2,1)}, u32[]{:S(2)}, u32[]{:S(2)}) collective-permute-start(bf16[480,1152]{1,0:T(8,128)(2,1)S(1)} %get-tuple-element.247), channel_id=1, source_target_pairs={{0,1},{1,0},{2,3},{3,2},{4,5},{5,4},{6,7},{7,6},{8,9},{9,8},{10,11... | collective-permute-start | bytes 3317768 | tf_op jit(solution)/shard_map/ppermute | solution.py:724
  1015.4 3.0 collective-permute-start.35
  1018.3 53.5 %collective-permute-start.36 = (bf16[72,1152]{1,0:T(8,128)(2,1)S(1)}, bf16[72,1152]{1,0:T(8,128)(2,1)S(1)}, u32[]{:S(2)}, u32[]{:S(2)}) collective-permute-start(bf16[72,1152]{1,0:T(8,128)(2,1)S(1)} %broadcast_select_fusion.13), channel_id=1, source_target_pairs={{0,16},{16,0},{1,17},{17,1},{2,18},{18,2},{3,19},{19,3},{4,20},{20... | collective-permute-start | bytes 497672 | tf_op jit(solution)/shard_map/ppermute | solution.py:703
  1066.3 9.6 collective-permute-start.33
  1068.7 24.8 %collective-permute-start.32 = (bf16[120,1152]{1,0:T(8,128)(2,1)S(1)}, bf16[120,1152]{1,0:T(8,128)(2,1)S(1)}, u32[]{:S(2)}, u32[]{:S(2)}) collective-permute-start(bf16[120,1152]{1,0:T(8,128)(2,1)S(1)} %get-tuple-element.311), channel_id=1, source_target_pairs={{0,8},{4,12},{8,0},{12,4},{1,9},{5,13},{9,1},{13,5},{2,10},{6,14},... | collective-permute-start | bytes 829448 | tf_op jit(solution)/shard_map/ppermute | solution.py:719
  1069.8 23.6 %collective-permute-start.31 = (bf16[120,1152]{1,0:T(8,128)(2,1)S(1)}, bf16[120,1152]{1,0:T(8,128)(2,1)S(1)}, u32[]{:S(2)}, u32[]{:S(2)}) collective-permute-start(bf16[120,1152]{1,0:T(8,128)(2,1)S(1)} %get-tuple-element.309), channel_id=1, source_target_pairs={{0,4},{4,8},{8,12},{12,0},{1,5},{5,9},{9,13},{13,1},{2,6},{6,10},{... | collective-permute-start | bytes 829448 | tf_op jit(solution)/shard_map/ppermute | solution.py:719
  1096.8 1.5 collective-permute-start.34
  (230 other events, 3211.3 us)
Sparse Core Ops, SparseCore 0:
  117.2 70.8 all-gather.4
  190.2 69.5 all-gather.6
  261.4 69.8 all-gather.10
  333.3 69.7 all-gather.8
  489.9 38.5 reduce-scatter.22
  531.4 43.0 reduce-scatter.24
  641.3 47.9 reduce-scatter.20
  710.8 33.1 reduce-scatter.32
  746.5 21.2 reduce-scatter.34
  770.0 29.4 reduce-scatter.30
  802.8 39.1 reduce-scatter.26
  911.8 43.5 reduce-scatter.28
  969.7 24.9 reduce-scatter.36
  997.0 21.2 reduce-scatter.38

commit v2 on v1

--- a/solution.py
+++ b/solution.py
@@ -12,10 +12,30 @@
 lanes = 128
 group = 8
 reset = 1e30
+fold_order = (3, 7, 5, 1, 4, 0, 6, 2)
 
 
 def row_of(tile, index, states):
     return jnp.broadcast_to(tile[index : index + 1, :], (states, tile.shape[1]))
+
+
+def fold(parts, shift, rows):
+    count = len(parts)
+    if count == 1:
+        return parts[0]
+    span = group // count
+    left = fold(parts[: count // 2], shift, rows)
+    right = fold(parts[count // 2 :], shift + (span if count > 2 else 0), rows)
+    mask = ((rows - shift) & span) != 0
+    if count == 2:
+        mask = jnp.logical_not(mask)
+    return jnp.where(mask, left, right) + pltpu.roll(jnp.where(mask, right, left), span, 0)
+
+
+def state_sums(parts):
+    rows = lax.broadcasted_iota(jnp.int32, (group, lanes), 0)
+    halved = [part[:group] + part[group:] for part in parts]
+    return fold([halved[k] for k in fold_order], 0, rows)
 
 
 def end_kernel(step_ref, act_ref, start_ref, in_ref, rate_ref, end_ref):
@@ -54,7 +74,6 @@
     states = rate_ref.shape[0]
     tiles = width // lanes
     cols = [slice(j * lanes, (j + 1) * lanes) for j in range(tiles)]
-    which = lax.broadcasted_iota(jnp.int32, (group, lanes), 0)
 
     def body(g, state):
         at = pl.ds(pl.multiple_of(g * group, group), group)
@@ -66,13 +85,12 @@
             drive = step * act
             fall = step + begin
             rate = rate_ref[:, cols[j]]
-            y = skip_ref[:, cols[j]] * act
+            parts = []
             for i in range(group):
                 decay = jnp.exp(row_of(fall, i, states) * rate)
                 state[j] = decay * state[j] + row_of(drive, i, states) * in_ref[g * group + i]
-                part = jnp.sum(state[j] * out_ref[g * group + i], axis=0, keepdims=True)
-                y = y + jnp.where(which == i, part, 0.0)
-            y_ref[at, cols[j]] = y
+                parts.append(state[j] * out_ref[g * group + i])
+            y_ref[at, cols[j]] = skip_ref[:, cols[j]] * act + state_sums(parts)
         return tuple(state)
 
     lax.fori_loop(
@@ -116,7 +134,6 @@
     tiles = width // lanes
     cols = [slice(j * lanes, (j + 1) * lanes) for j in range(tiles)]
     groups = rows // group
-    which = lax.broadcasted_iota(jnp.int32, (group, lanes), 0)
 
     @pl.when(pl.program_id(0) == 0)
     def _():
@@ -158,21 +175,19 @@
             drive = step * act
             grad = grad_ref[at, cols[j]]
             rate = rate_ref[:, cols[j]]
-            back_drive = jnp.zeros((group, lanes), jnp.float32)
-            back_fall = jnp.zeros((group, lanes), jnp.float32)
+            drives, falls = [], []
             for i in reversed(range(group)):
                 t = g * group + i
                 grad_row = row_of(grad, i, states)
                 adj = flow[j] + grad_row * out_ref[t]
                 back_out[i] = back_out[i] + kept[t + 1, :, cols[j]] * grad_row
                 back_in[i] = back_in[i] + adj * row_of(drive, i, states)
-                part = jnp.sum(adj * in_ref[t], axis=0, keepdims=True)
-                back_drive = back_drive + jnp.where(which == i, part, 0.0)
+                drives.insert(0, adj * in_ref[t])
                 flow[j] = adj * decays[t, :, cols[j]]
                 turn = flow[j] * kept[t, :, cols[j]]
-                part = jnp.sum(turn * rate, axis=0, keepdims=True)
-                back_fall = back_fall + jnp.where(which == i, part, 0.0)
+                falls.insert(0, turn * rate)
                 slope[j] = slope[j] + row_of(step, i, states) * turn
+            back_drive, back_fall = state_sums(drives), state_sums(falls)
             back_act_ref[at, cols[j]] = step * back_drive + skip_ref[:, cols[j]] * grad
             back_step_ref[at, cols[j]] = act * back_drive + back_fall
         for i in range(group):
@@ -219,7 +234,7 @@
 def end_call(step, act, start, in_map, rate, block=None):
     rows, width = step.shape
     states = rate.shape[0]
-    block = block or block_of(width, 384)
+    block = block or block_of(width, 768)
     wide, mark, maps, held, line, total = specs(rows, states, block)
     return pl.pallas_call(
         end_kernel,
@@ -236,7 +251,7 @@
 def scan_call(step, act, start, in_map, out_map, rate, entry, skip, block=None):
     rows, width = step.shape
     states = rate.shape[0]
-    block = block or block_of(width, 384)
+    block = block or block_of(width, 768)
     wide, mark, maps, held, line, total = specs(rows, states, block)
     return pl.pallas_call(
         scan_kernel,
@@ -253,7 +268,7 @@
 def entry_call(step, start, out_map, rate, grad, block=None):
     rows, width = step.shape
     states = rate.shape[0]
-    block = block or block_of(width, 384)
+    block = block or block_of(width, 768)
     wide, mark, maps, held, line, total = specs(rows, states, block)
     return pl.pallas_call(
         entry_kernel,
@@ -270,7 +285,7 @@
 def back_call(step, act, start, in_map, out_map, rate, entry, adj, skip, grad, block=None):
     rows, width = step.shape
     states = rate.shape[0]
-    block = block or block_of(width, 384)
+    block = block or block_of(width, 768)
     wide, mark, maps, held, line, total = specs(rows, states, block)
     return pl.pallas_call(
         back_kernel,
@@ -805,9 +820,12 @@
     return parts.transpose(0, 3, 2, 1, 4).reshape(rows, width)
 
 
-def settle(total):
-    part = lax.psum_scatter(total, "expert", scatter_dimension=0, tiled=True)
-    return lax.psum_scatter(part, "dp", scatter_dimension=0, tiled=True)
+def settle_expert(total):
+    return lax.psum_scatter(total, "expert", scatter_dimension=0, tiled=True)
+
+
+def settle_dp(total):
+    return lax.psum_scatter(total, "dp", scatter_dimension=0, tiled=True)
 
 
 def settle_direct(total):
@@ -842,10 +860,20 @@
     return jnp.pad(array, ((0, 0), (0, lanes - array.shape[1])))
 
 
+def piled(parts):
+    total, at = None, 0
+    rows = sum(part.shape[0] for part in parts)
+    for part in parts:
+        padded = jnp.pad(part, ((at, rows - at - part.shape[0]), (0, 0)))
+        total = padded if total is None else total + padded
+        at += part.shape[0]
+    return total
+
+
 def pack(select, step, rows, model):
-    model = jnp.pad(model, ((0, 0), (0, rows.shape[1] - model.shape[1])))
-    thin = jnp.concatenate([rows, model], axis=0).T
-    return jnp.stack([widen(select), widen(step), widen(thin)])
+    model = jnp.pad(model, ((0, 0), (0, rows[0].shape[1] - model.shape[1])))
+    thin = piled(rows + [model]).T
+    return jnp.concatenate([widen(select), widen(step), widen(thin)], axis=1)
 
 
 def layer_forward(residual, small, big, routing, documents, mark, low_rank):
@@ -925,7 +953,7 @@
     back_pre = jax.vjp(jax.nn.gelu, kept.pre_act)[1](back_hidden)[0].astype(jnp.bfloat16)
     back_expert = cross_cols(back_pre, up_weight).astype(jnp.bfloat16).reshape(back_arrived.shape)
     if earlier is not None:
-        (back_expert,) = tie([back_expert], earlier.moving)
+        back_expert, *earlier.moving = tie([back_expert, *earlier.moving], ())
         earlier.advance()
     back_returned = lax.all_to_all(back_expert, "expert", split_axis=0, concat_axis=0, tiled=True)
     grad_down = joined(halves(kept.hidden, first, 1), lambda half: cross_rows(half, back_flat))
@@ -951,10 +979,17 @@
         gate_product, kept.scanned, kept.gate_in.astype(jnp.float32)
     )[1](back_gated)
     normed_rows = by_expert(kept.normed, 1)
+    part_rows = model_width // (lax.axis_size("dp") * lax.axis_size("expert"))
     back_gate_in = back_gate_in.astype(jnp.bfloat16)
     grad_gate = joined(halves(back_gate_in, first, 1), lambda half: cross_rows(normed_rows, half))
-    late = (settle(grad_gate), settle(grad_output))
-    (back_scanned,) = tie([back_scanned], (grad_up, grad_down, grad_gate, grad_output))
+    together = [part.reshape(-1, part_rows, model_width) for part in (grad_gate, grad_output)]
+    together = jnp.stack(together, axis=1).reshape(-1, model_width)
+    late = settle_expert(together)
+    ready = (grad_up, grad_down, together)
+    if earlier is None:
+        (back_scanned,) = tie([back_scanned], ready)
+    else:
+        back_scanned, *earlier.moving = tie([back_scanned, *earlier.moving], ready)
     rate = small.rate
     back_ends = entry_call(kept.step_size, kept.mark, kept.out_wide, rate, back_scanned)
     (adjoint,) = carry_call(back_ends, rate, kept.totals)
@@ -962,9 +997,7 @@
         kept.step_size, kept.activated, kept.mark, kept.in_wide, kept.out_wide,
         rate, kept.entry_state, adjoint, small.skip, back_scanned,
     )
-    (back_step,) = tie(
-        [back_step], line.moving + pending + (() if earlier is None else earlier.moving)
-    )
+    back_step, *line.moving = tie([back_step, *line.moving], pending)
     line.advance()
     act_float = kept.activated.astype(jnp.float32)
     grad_skip = jnp.sum(back_scanned * act_float, axis=0, keepdims=True)
@@ -997,12 +1030,44 @@
         norm_scale, kept.residual, small.mixer_gain
     )[1](back_normed)
     back_residual = back_middle + back_residual_norm
-    lines = jnp.concatenate(
-        [grad_conv, grad_decay, grad_conv_bias[None], grad_step_bias, grad_skip], axis=0
-    )
-    model = jnp.concatenate([grad_mixer_gain[None], grad_expert_gain[None], grad_router], axis=0)
+    lines = piled([grad_conv, grad_decay, grad_conv_bias[None], grad_step_bias, grad_skip])
+    model = piled([grad_mixer_gain[None], grad_expert_gain[None], grad_router])
     small_grads = (grad_select, grad_step, lines, model)
+    if earlier is not None:
+        small_grads = tie(list(small_grads), (grad_taps_in,))
     return back_residual, grad_taps_in, late, line, small_grads
+
+
+def small_outputs(total, taps, states, ranks, low_rank, expert_count, part):
+    chan = total.shape[1]
+    thin = taps + states + 3
+
+    def body(total_ref, *outs):
+        mixer, conv, conv_bias, select, step, step_bias, decay, skip, expert, router = outs
+        down = lax.broadcasted_iota(jnp.int32, (lanes, lanes), 0)
+        right = lax.broadcasted_iota(jnp.int32, (lanes, lanes), 1)
+        same = jnp.where(down == right, 1.0, 0.0).astype(jnp.bfloat16)
+        rows = cross_cols(same, total_ref[2])
+        select[0] = total_ref[0].astype(jnp.float32)[:, :ranks]
+        step[0] = cross_cols(same, total_ref[1])[:low_rank]
+        conv[0] = rows[:taps]
+        decay[0] = total_ref[2].astype(jnp.float32)[:, taps : taps + states]
+        for ref, at in ((conv_bias, thin - 3), (step_bias, thin - 2), (skip, thin - 1)):
+            ref[...] = rows[at : at + 1]
+        mixer[...] = rows[thin : thin + 1, :part]
+        expert[...] = rows[thin + 1 : thin + 2, :part]
+        whole = total_ref[2].astype(jnp.float32)
+        router[0] = whole[:part, thin + 2 : thin + 2 + expert_count]
+
+    line = f32(1, chan)
+    return pl.pallas_call(
+        body,
+        out_shape=[
+            f32(1, part), f32(1, taps, chan), line, f32(1, chan, ranks), f32(1, low_rank, chan),
+            line, f32(1, chan, states), line, f32(1, part), f32(1, part, expert_count),
+        ],
+        name="small_outputs",
+    )(total)
 
 
 def doc_marks(documents, tap_count):
@@ -1046,10 +1111,8 @@
     packed = pack(
         select_weight[0],
         step_weight[0].T,
-        jnp.concatenate(
-            [conv_weight[0], decay_log[0].T, conv_bias, step_bias, skip_gain], axis=0
-        ),
-        jnp.concatenate([mixer_gain, expert_gain, router_weight[0].T], axis=0),
+        [conv_weight[0], decay_log[0].T, conv_bias, step_bias, skip_gain],
+        piled([mixer_gain, expert_gain, router_weight[0].T]),
     )
     wide = input_weight.shape[2] // 2
     experts = expert_parts(up_weight[0, 0], down_weight[0, 0], first)
@@ -1068,9 +1131,8 @@
     part = model_width // count
 
     def unpack(layer):
-        select, step, rows = [
-            gathered[layer][0][:, k].reshape(count * chan, lanes) for k in range(3)
-        ]
+        whole = gathered[layer][0].reshape(count * chan, 3 * lanes)
+        select, step, rows = [whole[:, k * lanes : (k + 1) * lanes] for k in range(3)]
         rows = rows.T[: thin + 2 + expert_count].astype(jnp.float32)
         model = rows[thin:].reshape(-1, count, chan)[:, :, :part].reshape(-1, model_width)
         return SimpleNamespace(
@@ -1126,37 +1188,38 @@
         input_grads[layer] = back_residual
         grad_out = back_residual.astype(jnp.bfloat16).astype(jnp.float32)
         if layer == 1:
-            pending = (settle(grad_taps_in),) + late
+            pending = (settle_dp(settle_expert(grad_taps_in)), settle_dp(late))
         else:
             settled[1] = pending + (earlier.total(),)
-            final_late = late + (line.total(),)
+            final_late = (settle_dp(late), line.total())
         across, along = lax.axis_size("dp"), lax.axis_size("expert")
         grad_select, grad_step, rows, model = small_grads
         model = model.reshape(-1, count, part)
         model = jnp.pad(model, ((0, 0), (0, 0), (0, chan - part))).reshape(-1, count * chan)
-        rows = widen(jnp.concatenate([rows, model], axis=0).T)
+        rows = widen(piled([rows, model]).T)
         whole = jnp.stack(
-            [array.reshape(across, along, chan, lanes) for array in (grad_select, grad_step, rows)],
+            [
+                array.astype(jnp.bfloat16).reshape(across, along, chan, lanes)
+                for array in (grad_select, grad_step, rows)
+            ],
             axis=2,
-        ).astype(jnp.bfloat16)
-        small_sums[layer] = whole.transpose(1, 0, 2, 3, 4).reshape(count, -1, model_width)
+        )
+        small_sums[layer] = whole.transpose(1, 0, 2, 3, 4).reshape(-1, lanes)
 
     own_small, sent_small = pick(first, small_sums[0], small_sums[1])
     own_small = own_small.astype(jnp.float32) + swap(sent_small).astype(jnp.float32)
-    last = jnp.concatenate(
-        [grad_taps_in.reshape(count, part, -1), own_small.astype(jnp.bfloat16)], axis=1
-    )
-    last = settle_direct(last.reshape(-1, model_width))
-    settled[0] = (last[:part],) + final_late
-    total = last[part:].reshape(3, chan, lanes).astype(jnp.float32)
-    rows = total[2].T
-    model = rows[thin : thin + 2 + expert_count, :part]
+    total = settle_direct(own_small.astype(jnp.bfloat16))
+    small_out = small_outputs(
+        total.reshape(3, chan, lanes), tap_count, states, ranks, low_rank, expert_count, part
+    )
+    settled[0] = (settle_direct(grad_taps_in),) + final_late
+    both_late = [(late_one[1][:part], late_one[1][part:]) for late_one in settled]
 
     def whole_input():
         taps = hand_back((settled[0][0], settled[1][0]), first, 1)
-        return jnp.concatenate([taps, hand_back((settled[0][1], settled[1][1]), first, 1)], axis=1)
-
-    experts_back = hand_back((settled[0][3], settled[1][3]), first, 1)
+        return jnp.concatenate([taps, hand_back([pair[0] for pair in both_late], first, 1)], axis=1)
+
+    experts_back = hand_back((settled[0][2], settled[1][2]), first, 1)
     def both(array):
         mine, sent = pick(first, array[0], array[1])
         return jnp.stack(pick(first, mine, swap(sent)))[None]
@@ -1164,18 +1227,11 @@
     return (
         both(outputs_seen),
         both(input_grads),
-        model[:1],
+        small_out[0],
         whole_input()[None],
-        rows[:tap_count][None],
-        rows[thin - 3 : thin - 2],
-        total[0, :, :ranks][None],
-        total[1, :, :low_rank].T[None],
-        rows[thin - 2 : thin - 1],
-        rows[tap_count : tap_count + states].T[None],
-        rows[thin - 1 : thin],
-        hand_back((settled[0][2], settled[1][2]), first, 0)[None],
-        model[1:2],
-        model[2:].T[None],
+        *small_out[1:8],
+        hand_back([pair[1] for pair in both_late], first, 0)[None],
+        *small_out[8:],
         experts_back[0].T[None, None],
         experts_back[1][None, None],
     )

time: 1120 us -> 1040 us (0.929)
  matrix products: 223 us -> 192 us
  Pallas kernels: 355 us -> 338 us
  starting transfers between devices: 103 us -> 90.6 us
  local copies, waits for them, and re-layouts: 141 us -> 129 us
    dot_general x26, matrix products: 87.2 us -> 67.6 us  [cross_rows(): lax.dot_general(left, right, (((0,), (0,)), ((), ())), preferred_element_...]
    ppermute x12, starting transfers between devices: 47.1 us -> 29.4 us  [advance(): moved.append(lax.ppermute(held.astype(jnp.bfloat16), 'dp', pairs))]
    unnamed x471 -> x570, local copies, waits for them, and re-layouts: 52.4 us -> 70.1 us
    ppermute x12, waiting for transfers between devices: 30.6 us -> 16.6 us  [advance(): moved.append(lax.ppermute(held.astype(jnp.bfloat16), 'dp', pairs))]
    ppermute x3 -> x6, waiting for transfers between devices: 44.4 us -> 36.8 us  [crossed(): return lax.ppermute(array, axis, [(i, i ^ mask) for i in range(length)])]
    select_n x16 -> x14, other arithmetic: 22.7 us -> 21.1 us  [pick(): return (jnp.where(first, left, right), jnp.where(first, right, left))]
  transfers between devices with their start and end apart: 64 -> 66, of which waited for: 16 -> 18; matrix products, arithmetic and copies ran while one was open for 37% -> 35% of each run, Pallas kernels for 32% -> 33%
where the time goes in v2:
time: 1040 us; the launch traced here: 1030 us
  Pallas kernels  338 us (32%)
  matrix products  192 us (18%)
  waiting for transfers between devices  139 us (13%)
  local copies, waits for them, and re-layouts  129 us (12%)
  other arithmetic  126 us (12%)
  starting transfers between devices  90.6 us (9%)
  between operations  18.4 us (2%)
    pallas_call x2, Pallas kernels, gather_call(): pl.pallas_call(body, in_specs=[pl.BlockSpec(memory_space=pltpu.HBM)] * le...  178 us
    unnamed x570, local copies, waits for them, and re-layouts  70.1 us
    dot_general x26, matrix products, cross_rows(): lax.dot_general(left, right, (((0,), (0,)), ((), ())), preferred_element_...  67.6 us
    pallas_call x2, Pallas kernels, back_call(): pl.pallas_call(back_kernel, grid=(width // block,), in_specs=[wide, wide,...  66.9 us
    dot_general x16, matrix products, cross_cols(): lax.dot_general(left, right, (((1,), (1,)), ((), ())), preferred_element_...  64 us
    dot_general x16, matrix products, product(): return jnp.dot(left, right, preferred_element_type=jnp.float32)  60.4 us
    pallas_call x4, Pallas kernels, carry_call(): pl.pallas_call(functools.partial(carry_kernel, count, backward), in_specs...  38.3 us
    ppermute x6, waiting for transfers between devices, crossed(): return lax.ppermute(array, axis, [(i, i ^ mask) for i in range(length)])  36.8 us
  transfers between devices with their start and end apart: 66, of which 18 were waited for; matrix products, arithmetic and copies ran while one was open for 35% of the time, Pallas kernels for 33%

profile of v2, /device:TPU:0, one launch (start us, length us, event | category | flops | bytes accessed | tf_op | source)
XLA Modules:
  0.0 1032.7 jit_solution(15503421300713656421)
XLA Ops:
  33.2 94.2 %weights_along_dp.1 = (bf16[16,144,384]{2,1,0:T(8,128)(2,1)}, bf16[16,72,2304]{2,1,0:T(8,128)(2,1)}, bf16[16,72,2304]{2,1,0:T(8,128)(2,1)}, bf16[16,144,1152]{2,...) custom-call(bf16[144,384]{1,0:T(8,128)(2,1)} %fusion.190.refs_0_, ...), custom_call_target="tpu_custom_call" | custom-call | bytes 262144000 | tf_op jit(solution)/shard_map/weights_along_dp/pallas_call | solution.py:614
  141.0 83.3 %weights_across.1 = (bf16[16,144,384]{2,1,0:T(8,128)(2,1)}, bf16[16,72,2304]{2,1,0:T(8,128)(2,1)}, bf16[16,72,2304]{2,1,0:T(8,128)(2,1)}, bf16[16,144,1152]{2,1,...) custom-call(bf16[16,144,384]{2,1,0:T(8,128)(2,1)} %get-tuple-element, ...), custom_call_target="tpu_custom_call", output_to_operand_aliasing={{0}: (0, {}), {1}: (1, {}), {2}: (2, {}), {3}: (3, {}), {4}... | custom-call | bytes 262144000 | tf_op jit(solution)/shard_map/weights_across/pallas_call | solution.py:614
  226.0 4.0 convolution_convert_fusion.13
  241.6 7.8 state_end.2.refs_0_
  250.1 9.9 state_carry.2
  263.1 11.5 %state_scan.2 = f32[192,2304]{1,0:T(8,128)S(1)} custom-call(f32[192,2304]{1,0:T(8,128)S(1)} %copy-done.32, bf16[192,2304]{1,0:T(8,128)(2,1)S(1)} %get-tuple-element.293.act_ref, f32[192,128]{1,0:T(8,128)S(1)} %broadcast_in_dim.263.start_ref, f32[192,16,128]{2,1,0:T(8,128)S(1)} %broadcast_in_dim.264.in_ref, f32[192,16,128]{2,1,0:T(8,128)S(1)} %broadcast_in_dim.265.out_ref, ...), custom_call_target="tpu_custom_call" | custom-call | flops 84934656 | bytes 4423680 | tf_op jit(solution)/shard_map/state_scan/pallas_call | solution.py:256
  274.6 5.8 multiply_convert_fusion.4
  284.9 4.0 all-to-all-start
  289.0 11.1 %all-to-all-done = bf16[4,96,1152]{2,1,0:T(8,128)(2,1)S(1)} async-done(((bf16[4,96,1152]{2,1,0:T(8,128)(2,1)}), bf16[4,96,1152]{2,1,0:T(8,128)(2,1)S(1)}, u32[]{:S(2)}, u32[]{:S(2)}) %all-to-all-start) | async-done | bytes 884768 | tf_op jit(solution)/shard_map/all_to_all | solution.py:919
  300.1 9.7 multiply_convert_fusion.1
  309.8 7.9 convolution_convert_fusion.19
  321.6 11.0 %all-to-all-done.1 = bf16[4,96,1152]{2,1,0:T(8,128)(2,1)S(1)} async-done(((bf16[4,96,1152]{2,1,0:T(8,128)(2,1)}), bf16[4,96,1152]{2,1,0:T(8,128)(2,1)S(1)}, u32[]{:S(2)}, u32[]{:S(2)}) %all-to-all-start.1) | async-done | bytes 884768 | tf_op jit(solution)/shard_map/all_to_all | solution.py:924
  334.7 3.8 convolution_convert_fusion.11
  349.9 7.8 state_end.3.refs_0_
  359.7 10.1 state_carry.3
  372.9 11.5 %state_scan.3 = f32[192,2304]{1,0:T(8,128)S(1)} custom-call(f32[192,2304]{1,0:T(8,128)S(1)} %copy-done.35, bf16[192,2304]{1,0:T(8,128)(2,1)S(1)} %get-tuple-element.289.act_ref, f32[192,128]{1,0:T(8,128)S(1)} %broadcast_in_dim.263.start_ref, f32[192,16,128]{2,1,0:T(8,128)S(1)} %broadcast_in_dim.269.in_ref, f32[192,16,128]{2,1,0:T(8,128)S(1)} %broadcast_in_dim.270.out_ref, ...), custom_call_target="tpu_custom_call" | custom-call | flops 84934656 | bytes 4423680 | tf_op jit(solution)/shard_map/state_scan/pallas_call | solution.py:256
  384.4 5.9 multiply_convert_fusion.2
  396.4 4.4 all-to-all-start.4
  410.1 3.7 all-to-all-start.2
  413.9 8.8 fusion.247
  422.7 11.7 %fusion.13 = (bf16[384,3072]{1,0:T(8,128)(2,1)}, bf16[384,3072]{1,0:T(8,128)(2,1)S(1)}) fusion(f32[384,3072]{1,0:T(8,128)} %fusion.247, bf16[384,1152]{1,0:T(8,128)(2,1)S(1)} %bitcast.392, bf16[1152,3072]{1,0:T(8,128)(2,1)} %all-gather.9.cloned.1.call-done), kind=kOutput, calls=%fused_computation.49 | convolution fusion | flops 2743861248 | bytes 17399808 | tf_op jit(solution)/shard_map/dot_general | solution.py:322
  434.4 6.0 convolution_convert_fusion.8
  440.4 4.1 convolution_convert_fusion.18
  444.6 4.2 all-to-all-start.3
  448.8 7.9 convolution_convert_fusion.17
  457.3 3.5 all-to-all-start.5
  467.7 5.9 convolution_convert_fusion.9
  486.3 5.7 fusion.178
  494.0 4.5 add_convert_fusion.2.refs_2_
  502.7 4.4 add_convert_fusion.3.refs_1_
  527.1 7.4 adjoint_entry.2.refs_0_
  535.2 9.2 adjoint_carry.2.adj_ref
  544.4 33.4 %scan_back.2 = (f32[192,2304]{1,0:T(8,128)}, f32[192,2304]{1,0:T(8,128)}, f32[16,2304]{1,0:T(8,128)}, f32[192,16,128]{2,1,0:T(8,128)}, f32[192,16,128]{2,1,0:T(8,128)}) custom-call(f32[192,2304]{1,0:T(8,128)} %copy-done.34, bf16[192,2304]{1,0:T(8,128)(2,1)} %copy-done.4, f32[192,128]{1,0:T(8,128)} %copy-done.25, f32[192,16,128]{2,1,0:T(8,128)} %copy-done.13, ...), custom_call_target="tpu_custom_call" | custom-call | flops 283115520 | bytes 8847360 | tf_op jit(solution)/shard_map/scan_back/pallas_call | solution.py:290
  591.0 3.8 collective-permute-done.12
  596.0 4.9 collective-permute-done.23
  616.8 5.5 fusion.248
  626.0 4.1 add_convert_fusion.19
  632.7 3.7 add_convert_fusion.18
  646.5 4.1 all-to-all-start.6
  653.7 18.0 %all-to-all-done.6 = bf16[4,96,1152]{2,1,0:T(8,128)(2,1)S(1)} async-done(((bf16[4,96,1152]{2,1,0:T(8,128)(2,1)}), bf16[4,96,1152]{2,1,0:T(8,128)(2,1)S(1)}, u32[]{:S(2)}, u32[]{:S(2)}) %all-to-all-start.6) | async-done | bytes 884768 | tf_op jit(solution)/shard_map/all_to_all | solution.py:950
  671.7 10.5 %fusion.6 = bf16[384,3072]{1,0:T(8,128)(2,1)S(1)} fusion(f32[384,3072]{1,0:T(8,128)} %get-tuple-element.402, bf16[384,1152]{1,0:T(8,128)(2,1)S(1)} %bitcast.389, bf16[3072,1152]{1,0:T(8,128)(2,1)} %all-gather.7.cloned.1.call-done), kind=kOutput, calls=%fused_computation.42 | convolution fusion | flops 2741501952 | bytes 15040512 | tf_op jit(solution)/shard_map/dot_general | solution.py:332
  682.3 4.0 convolution_convert_fusion.7
  686.3 4.0 convolution_convert_fusion.6
  690.8 4.3 convolution_convert_fusion.16
  695.1 3.6 all-to-all-start.7
  709.3 11.5 %all-to-all-done.7 = bf16[4,96,1152]{2,1,0:T(8,128)(2,1)S(1)} async-done(((bf16[4,96,1152]{2,1,0:T(8,128)(2,1)}), bf16[4,96,1152]{2,1,0:T(8,128)(2,1)S(1)}, u32[]{:S(2)}, u32[]{:S(2)}) %all-to-all-start.7) | async-done | bytes 884768 | tf_op jit(solution)/shard_map/all_to_all | solution.py:958
  727.3 5.8 fusion.177
  736.6 4.2 add_convert_fusion.refs_4_
  745.1 4.2 add_convert_fusion.1.refs_3_
  760.1 5.3 fusion.249
  778.3 7.4 adjoint_entry.3.refs_0_
  786.4 9.2 adjoint_carry.3.adj_ref
  795.5 33.5 %scan_back.3 = (f32[192,2304]{1,0:T(8,128)}, f32[192,2304]{1,0:T(8,128)}, f32[16,2304]{1,0:T(8,128)}, f32[192,16,128]{2,1,0:T(8,128)}, f32[192,16,128]{2,1,0:T(8,128)}) custom-call(f32[192,2304]{1,0:T(8,128)} %copy-done.31, bf16[192,2304]{1,0:T(8,128)(2,1)} %copy-done.2, f32[192,128]{1,0:T(8,128)} %copy-done.25, f32[192,16,128]{2,1,0:T(8,128)} %copy-done.10, ...), custom_call_target="tpu_custom_call" | custom-call | flops 283115520 | bytes 8847360 | tf_op jit(solution)/shard_map/scan_back/pallas_call | solution.py:290
  838.7 4.8 multiply_reduce_fusion.4
  878.0 16.6 %collective-permute-done.43 = bf16[2,384,1152]{2,1,0:T(8,128)(2,1)} collective-permute-done((bf16[2,384,1152]{2,1,0:T(8,128)(2,1)}, bf16[2,384,1152]{2,1,0:T(8,128)(2,1)}, u32[]{:S(2)}, u32[]{:S(2)}) %collective-permute-start.43) | collective-permute-done | bytes 1769504 | tf_op jit(solution)/shard_map/ppermute | solution.py:800
  897.9 5.5 collective-permute-start.44
  919.1 8.3 collective-permute-done.36
  927.5 11.8 %collective-permute-done.35 = bf16[288,1152]{1,0:T(8,128)(2,1)} collective-permute-done((bf16[288,1152]{1,0:T(8,128)(2,1)}, bf16[288,1152]{1,0:T(8,128)(2,1)}, u32[]{:S(2)}, u32[]{:S(2)}) %collective-permute-start.35) | collective-permute-done | bytes 663584 | tf_op jit(solution)/shard_map/ppermute | solution.py:739
  948.4 5.2 broadcast_select_fusion.2
  962.8 6.5 collective-permute-done.30
  969.3 9.1 collective-permute-done.29
  984.4 5.4 collective-permute-done.33
  989.8 11.1 %collective-permute-done.32 = bf16[432,128]{1,0:T(8,128)(2,1)S(1)} collective-permute-done((bf16[432,128]{1,0:T(8,128)(2,1)S(1)}, bf16[432,128]{1,0:T(8,128)(2,1)S(1)}, u32[]{:S(2)}, u32[]{:S(2)}) %collective-permute-start.32) | collective-permute-done | bytes 110624 | tf_op jit(solution)/shard_map/ppermute | solution.py:734
  1013.9 5.3 slice_bitcast_fusion
  (975 shorter events, 349.3 us)
Async XLA Ops:
  7.2 292.9 %all-gather.5.cloned.1.call-start = ((), (), s32[]{:S(2)}) async-start(), calls=%async_computation.14 | async-start | bytes 7962624 | tf_op jit(solution)/shard_map/all_gather | solution.py:754
  10.4 116.9 %collective-permute-start.2 = (bf16[1152,384]{1,0:T(8,128)(2,1)}, bf16[1152,384]{1,0:T(8,128)(2,1)}, u32[]{:S(2)}, u32[]{:S(2)}) collective-permute-start(bf16[1152,384]{1,0:T(8,128)(2,1)} %broadcast_select_fusion.7), channel_id=1, source_target_pairs={{0,16},{16,0},{1,17},{17,1},{2,18},{18,2},{3,19},{19,3},{4,20},{20... | collective-permute-start | bytes 2654216 | tf_op jit(solution)/shard_map/ppermute | solution.py:718
  14.1 115.9 %collective-permute-start.3 = (bf16[384,1152]{1,0:T(8,128)(2,1)}, bf16[384,1152]{1,0:T(8,128)(2,1)}, u32[]{:S(2)}, u32[]{:S(2)}) collective-permute-start(bf16[384,1152]{1,0:T(8,128)(2,1)} %select_bitcast_fusion.3), channel_id=1, source_target_pairs={{0,16},{16,0},{1,17},{17,1},{2,18},{18,2},{3,19},{19,3},{4,20},{20... | collective-permute-start | bytes 2654216 | tf_op jit(solution)/shard_map/ppermute | solution.py:718
  132.7 177.1 %all-gather.7.cloned.1.call-start = ((), (), s32[]{:S(2)}) async-start(), calls=%async_computation.15 | async-start | bytes 7962624 | tf_op jit(solution)/shard_map/all_gather | solution.py:754
  133.5 280.4 %all-gather.11.cloned.1.call-start = ((), (), s32[]{:S(2)}) async-start(), calls=%async_computation.17 | async-start | bytes 7962624 | tf_op jit(solution)/shard_map/all_gather | solution.py:754
  134.2 288.5 %all-gather.9.cloned.1.call-start = ((), (), s32[]{:S(2)}) async-start(), calls=%async_computation.16 | async-start | bytes 7962624 | tf_op jit(solution)/shard_map/all_gather | solution.py:754
  284.9 15.1 %all-to-all-start = ((bf16[4,96,1152]{2,1,0:T(8,128)(2,1)}), bf16[4,96,1152]{2,1,0:T(8,128)(2,1)S(1)}, u32[]{:S(2)}, u32[]{:S(2)}) async-start(bf16[4,96,1152]{2,1,0:T(8,128)(2,1)} %bitcast.25), calls=%async_computation | async-start | bytes 1769472 | tf_op jit(solution)/shard_map/all_to_all | solution.py:919
  317.6 15.0 %all-to-all-start.1 = ((bf16[4,96,1152]{2,1,0:T(8,128)(2,1)}), bf16[4,96,1152]{2,1,0:T(8,128)(2,1)S(1)}, u32[]{:S(2)}, u32[]{:S(2)}) async-start(bf16[4,96,1152]{2,1,0:T(8,128)(2,1)} %bitcast.396), calls=%async_computation.1 | async-start | bytes 1769472 | tf_op jit(solution)/shard_map/all_to_all | solution.py:924
  338.7 4.8 collective-permute-start.4
  396.4 13.7 %all-to-all-start.4 = ((bf16[4,96,1152]{2,1,0:T(8,128)(2,1)}), bf16[4,96,1152]{2,1,0:T(8,128)(2,1)}, u32[]{:S(2)}, u32[]{:S(2)}) async-start(bf16[4,96,1152]{2,1,0:T(8,128)(2,1)} %bitcast.52), calls=%async_computation.4 | async-start | bytes 1769472 | tf_op jit(solution)/shard_map/all_to_all | solution.py:950
  410.1 12.6 %all-to-all-start.2 = ((bf16[4,96,1152]{2,1,0:T(8,128)(2,1)}), bf16[4,96,1152]{2,1,0:T(8,128)(2,1)S(1)}, u32[]{:S(2)}, u32[]{:S(2)}) async-start(bf16[4,96,1152]{2,1,0:T(8,128)(2,1)} %bitcast.374), calls=%async_computation.2 | async-start | bytes 1769472 | tf_op jit(solution)/shard_map/all_to_all | solution.py:919
  444.6 12.7 %all-to-all-start.3 = ((bf16[4,96,1152]{2,1,0:T(8,128)(2,1)}), bf16[4,96,1152]{2,1,0:T(8,128)(2,1)S(1)}, u32[]{:S(2)}, u32[]{:S(2)}) async-start(bf16[4,96,1152]{2,1,0:T(8,128)(2,1)} %bitcast.43), calls=%async_computation.3 | async-start | bytes 1769472 | tf_op jit(solution)/shard_map/all_to_all | solution.py:924
  448.7 44.6 %collective-permute-start.7 = (bf16[1536,1152]{1,0:T(8,128)(2,1)}, bf16[1536,1152]{1,0:T(8,128)(2,1)}, u32[]{:S(2)}, u32[]{:S(2)}) collective-permute-start(bf16[1536,1152]{1,0:T(8,128)(2,1)} %convolution_convert_fusion.8), channel_id=1, source_target_pairs={{0,16},{16,0},{1,17},{17,1},{2,18},{18,2},{3,19},{19,3},{4,20},{20... | collective-permute-start | bytes 10616840 | tf_op jit(solution)/shard_map/ppermute | solution.py:718
  457.3 21.0 %all-to-all-start.5 = ((bf16[4,96,1152]{2,1,0:T(8,128)(2,1)}), bf16[4,96,1152]{2,1,0:T(8,128)(2,1)S(1)}, u32[]{:S(2)}, u32[]{:S(2)}) async-start(bf16[4,96,1152]{2,1,0:T(8,128)(2,1)} %bitcast.395), calls=%async_computation.5 | async-start | bytes 1769472 | tf_op jit(solution)/shard_map/all_to_all | solution.py:958
  460.8 275.6 %reduce-scatter.9.cloned.1.call-start = ((), (), s32[]{:S(2)}) async-start(), calls=%async_computation.18 | async-start | bytes 3317760 | tf_op jit(solution)/shard_map/reduce_scatter | solution.py:824
  473.6 28.6 %collective-permute-start.6 = (bf16[1536,1152]{1,0:T(8,128)(2,1)}, bf16[1536,1152]{1,0:T(8,128)(2,1)}, u32[]{:S(2)}, u32[]{:S(2)}) collective-permute-start(bf16[1536,1152]{1,0:T(8,128)(2,1)} %convolution_convert_fusion.9), channel_id=1, source_target_pairs={{0,16},{16,0},{1,17},{17,1},{2,18},{18,2},{3,19},{19,3},{4,20},{20... | collective-permute-start | bytes 10616840 | tf_op jit(solution)/shard_map/ppermute | solution.py:718
  485.0 33.8 %collective-permute-start.9 = (bf16[1152,1152]{1,0:T(8,128)(2,1)S(1)}, bf16[1152,1152]{1,0:T(8,128)(2,1)S(1)}, u32[]{:S(2)}, u32[]{:S(2)}) collective-permute-start(bf16[1152,1152]{1,0:T(8,128)(2,1)S(1)} %convolution_convert_fusion.4), channel_id=1, source_target_pairs={{0,16},{16,0},{1,17},{17,1},{2,18},{18,2},{3,19},{19,3},{4,20},{20... | collective-permute-start | bytes 7962632 | tf_op jit(solution)/shard_map/ppermute | solution.py:718
  492.9 24.9 %collective-permute-start.8 = (bf16[1152,1152]{1,0:T(8,128)(2,1)S(1)}, bf16[1152,1152]{1,0:T(8,128)(2,1)S(1)}, u32[]{:S(2)}, u32[]{:S(2)}) collective-permute-start(bf16[1152,1152]{1,0:T(8,128)(2,1)S(1)} %convolution_convert_fusion.5), channel_id=1, source_target_pairs={{0,16},{16,0},{1,17},{17,1},{2,18},{18,2},{3,19},{19,3},{4,20},{20... | collective-permute-start | bytes 7962632 | tf_op jit(solution)/shard_map/ppermute | solution.py:718
  511.7 68.7 %collective-permute-start.10 = (bf16[2,384,1152]{2,1,0:T(8,128)(2,1)}, bf16[2,384,1152]{2,1,0:T(8,128)(2,1)}, u32[]{:S(2)}, u32[]{:S(2)}) collective-permute-start(bf16[2,384,1152]{2,1,0:T(8,128)(2,1)} %pad_maximum_fusion.2), channel_id=1, source_target_pairs={{0,4},{1,5},{2,6},{3,7},{16,20},{17,21},{18,22},{19,23}} | collective-permute-start | bytes 5308424 | tf_op jit(solution)/shard_map/ppermute | solution.py:800
  515.9 64.5 %collective-permute-start.11 = (bf16[2,384,1152]{2,1,0:T(8,128)(2,1)}, bf16[2,384,1152]{2,1,0:T(8,128)(2,1)}, u32[]{:S(2)}, u32[]{:S(2)}) collective-permute-start(bf16[2,384,1152]{2,1,0:T(8,128)(2,1)} %pad_maximum_fusion.3), channel_id=1, source_target_pairs={{12,8},{13,9},{14,10},{15,11},{28,24},{29,25},{30,26},{31,27}} | collective-permute-start | bytes 5308424 | tf_op jit(solution)/shard_map/ppermute | solution.py:800
  589.0 5.9 collective-permute-start.12
  596.0 5.0 collective-permute-start.23
  603.5 145.8 %reduce-scatter.11.cloned.1.call-start = ((), (), s32[]{:S(2)}) async-start(), calls=%async_computation.19 | async-start | bytes 6635520 | tf_op jit(solution)/shard_map/reduce_scatter | solution.py:824
  615.1 7.1 collective-permute-start.5
  630.1 65.0 %collective-permute-start.13 = (bf16[2,384,1152]{2,1,0:T(8,128)(2,1)}, bf16[2,384,1152]{2,1,0:T(8,128)(2,1)}, u32[]{:S(2)}, u32[]{:S(2)}) collective-permute-start(bf16[2,384,1152]{2,1,0:T(8,128)(2,1)} %add_convert_fusion.19), channel_id=1, source_target_pairs={{0,4},{4,8},{1,5},{5,9},{2,6},{6,10},{3,7},{7,11},{16,20},{20,24},... | collective-permute-start | bytes 5308424 | tf_op jit(solution)/shard_map/ppermute | solution.py:800
  636.4 58.7 %collective-permute-start.14 = (bf16[2,384,1152]{2,1,0:T(8,128)(2,1)}, bf16[2,384,1152]{2,1,0:T(8,128)(2,1)}, u32[]{:S(2)}, u32[]{:S(2)}) collective-permute-start(bf16[2,384,1152]{2,1,0:T(8,128)(2,1)} %add_convert_fusion.18), channel_id=1, source_target_pairs={{8,4},{12,8},{9,5},{13,9},{10,6},{14,10},{11,7},{15,11},{24,20},{2... | collective-permute-start | bytes 5308424 | tf_op jit(solution)/shard_map/ppermute | solution.py:800
  646.5 25.2 %all-to-all-start.6 = ((bf16[4,96,1152]{2,1,0:T(8,128)(2,1)}), bf16[4,96,1152]{2,1,0:T(8,128)(2,1)S(1)}, u32[]{:S(2)}, u32[]{:S(2)}) async-start(bf16[4,96,1152]{2,1,0:T(8,128)(2,1)} %bitcast.71), calls=%async_computation.6 | async-start | bytes 1769472 | tf_op jit(solution)/shard_map/all_to_all | solution.py:950
  686.3 58.8 %collective-permute-start.17 = (bf16[1536,1152]{1,0:T(8,128)(2,1)}, bf16[1536,1152]{1,0:T(8,128)(2,1)}, u32[]{:S(2)}, u32[]{:S(2)}) collective-permute-start(bf16[1536,1152]{1,0:T(8,128)(2,1)} %convolution_convert_fusion.7), channel_id=1, source_target_pairs={{0,16},{16,0},{1,17},{17,1},{2,18},{18,2},{3,19},{19,3},{4,20},{20... | collective-permute-start | bytes 10616840 | tf_op jit(solution)/shard_map/ppermute | solution.py:718
  690.3 46.2 %collective-permute-start.18 = (bf16[1536,1152]{1,0:T(8,128)(2,1)}, bf16[1536,1152]{1,0:T(8,128)(2,1)}, u32[]{:S(2)}, u32[]{:S(2)}) collective-permute-start(bf16[1536,1152]{1,0:T(8,128)(2,1)} %convolution_convert_fusion.6), channel_id=1, source_target_pairs={{0,16},{16,0},{1,17},{17,1},{2,18},{18,2},{3,19},{19,3},{4,20},{20... | collective-permute-start | bytes 10616840 | tf_op jit(solution)/shard_map/ppermute | solution.py:718
  695.1 25.8 %all-to-all-start.7 = ((bf16[4,96,1152]{2,1,0:T(8,128)(2,1)}), bf16[4,96,1152]{2,1,0:T(8,128)(2,1)S(1)}, u32[]{:S(2)}, u32[]{:S(2)}) async-start(bf16[4,96,1152]{2,1,0:T(8,128)(2,1)} %get-tuple-element.106), calls=%async_computation.7 | async-start | bytes 1769472 | tf_op jit(solution)/shard_map/all_to_all | solution.py:958
  698.8 134.6 %reduce-scatter.19.cloned.1.call-start = ((), (), s32[]{:S(2)}) async-start(), calls=%async_computation.23 | async-start | bytes 829440
  702.3 71.6 %collective-permute-start.15 = (bf16[2,384,1152]{2,1,0:T(8,128)(2,1)}, bf16[2,384,1152]{2,1,0:T(8,128)(2,1)}, u32[]{:S(2)}, u32[]{:S(2)}) collective-permute-start(bf16[2,384,1152]{2,1,0:T(8,128)(2,1)} %add_convert_fusion.17), channel_id=1, source_target_pairs={{0,4},{4,8},{8,12},{1,5},{5,9},{9,13},{2,6},{6,10},{10,14},{3,7},{... | collective-permute-start | bytes 5308424 | tf_op jit(solution)/shard_map/ppermute | solution.py:800
  707.9 66.0 %collective-permute-start.16 = (bf16[2,384,1152]{2,1,0:T(8,128)(2,1)}, bf16[2,384,1152]{2,1,0:T(8,128)(2,1)}, u32[]{:S(2)}, u32[]{:S(2)}) collective-permute-start(bf16[2,384,1152]{2,1,0:T(8,128)(2,1)} %add_convert_fusion.16), channel_id=1, source_target_pairs={{4,0},{8,4},{12,8},{5,1},{9,5},{13,9},{6,2},{10,6},{14,10},{7,3},{... | collective-permute-start | bytes 5308424 | tf_op jit(solution)/shard_map/ppermute | solution.py:800
  726.7 41.6 %collective-permute-start.20 = (bf16[1152,1152]{1,0:T(8,128)(2,1)}, bf16[1152,1152]{1,0:T(8,128)(2,1)}, u32[]{:S(2)}, u32[]{:S(2)}) collective-permute-start(bf16[1152,1152]{1,0:T(8,128)(2,1)} %convolution_convert_fusion.2), channel_id=1, source_target_pairs={{0,16},{16,0},{1,17},{17,1},{2,18},{18,2},{3,19},{19,3},{4,20},{20... | collective-permute-start | bytes 7962632 | tf_op jit(solution)/shard_map/ppermute | solution.py:718
  736.5 96.9 %reduce-scatter.13.cloned.1.call-start = ((), (), s32[]{:S(2)}) async-start(), calls=%async_computation.20 | async-start | bytes 1658880 | tf_op jit(solution)/shard_map/reduce_scatter | solution.py:828
  736.5 21.3 %collective-permute-start.19 = (bf16[1152,1152]{1,0:T(8,128)(2,1)}, bf16[1152,1152]{1,0:T(8,128)(2,1)}, u32[]{:S(2)}, u32[]{:S(2)}) collective-permute-start(bf16[1152,1152]{1,0:T(8,128)(2,1)} %convolution_convert_fusion.3), channel_id=1, source_target_pairs={{0,16},{16,0},{1,17},{17,1},{2,18},{18,2},{3,19},{19,3},{4,20},{20... | collective-permute-start | bytes 7962632 | tf_op jit(solution)/shard_map/ppermute | solution.py:718
  749.4 213.4 %reduce-scatter.15.cloned.1.call-start = ((), (), s32[]{:S(2)}) async-start(), calls=%async_computation.21 | async-start | bytes 6635520 | tf_op jit(solution)/shard_map/reduce_scatter | solution.py:824
  753.9 79.4 %collective-permute-start.21 = (bf16[2,384,1152]{2,1,0:T(8,128)(2,1)}, bf16[2,384,1152]{2,1,0:T(8,128)(2,1)}, u32[]{:S(2)}, u32[]{:S(2)}) collective-permute-start(bf16[2,384,1152]{2,1,0:T(8,128)(2,1)} %pad_maximum_fusion.4), channel_id=1, source_target_pairs={{0,4},{1,5},{2,6},{3,7},{16,20},{17,21},{18,22},{19,23}} | collective-permute-start | bytes 5308424 | tf_op jit(solution)/shard_map/ppermute | solution.py:800
  757.9 75.4 %collective-permute-start.22 = (bf16[2,384,1152]{2,1,0:T(8,128)(2,1)}, bf16[2,384,1152]{2,1,0:T(8,128)(2,1)}, u32[]{:S(2)}, u32[]{:S(2)}) collective-permute-start(bf16[2,384,1152]{2,1,0:T(8,128)(2,1)} %pad_maximum_fusion.5), channel_id=1, source_target_pairs={{12,8},{13,9},{14,10},{15,11},{28,24},{29,25},{30,26},{31,27}} | collective-permute-start | bytes 5308424 | tf_op jit(solution)/shard_map/ppermute | solution.py:800
  833.2 178.4 %reduce-scatter.17.cloned.1.call-start = ((), (), s32[]{:S(2)}) async-start(), calls=%async_computation.22 | async-start | bytes 1658880 | tf_op jit(solution)/shard_map/reduce_scatter | solution.py:828
  844.8 14.2 %collective-permute-start.24 = (f32[3,2304]{1,0:T(4,128)S(1)}, f32[3,2304]{1,0:T(4,128)S(1)}, u32[]{:S(2)}, u32[]{:S(2)}) collective-permute-start(f32[3,2304]{1,0:T(4,128)S(1)} %pad_add_fusion.5), channel_id=1, source_target_pairs={{1,0},{2,1},{3,2},{5,4},{6,5},{7,6},{9,8},{10,9},{11,10},{13,12},{... | collective-permute-start | bytes 82952 | tf_op jit(solution)/shard_map/ppermute | solution.py:312
  849.9 23.3 %collective-permute-start.45 = (bf16[2,384,1152]{2,1,0:T(8,128)(2,1)}, bf16[2,384,1152]{2,1,0:T(8,128)(2,1)}, u32[]{:S(2)}, u32[]{:S(2)}) collective-permute-start(bf16[2,384,1152]{2,1,0:T(8,128)(2,1)} %add_convert_fusion.13), channel_id=1, source_target_pairs={{8,4},{12,8},{9,5},{13,9},{10,6},{14,10},{11,7},{15,11},{24,20},{2... | collective-permute-start | bytes 5308424 | tf_op jit(solution)/shard_map/ppermute | solution.py:800
  855.1 39.5 %collective-permute-start.43 = (bf16[2,384,1152]{2,1,0:T(8,128)(2,1)}, bf16[2,384,1152]{2,1,0:T(8,128)(2,1)}, u32[]{:S(2)}, u32[]{:S(2)}) collective-permute-start(bf16[2,384,1152]{2,1,0:T(8,128)(2,1)} %add_convert_fusion.15), channel_id=1, source_target_pairs={{0,4},{4,8},{1,5},{5,9},{2,6},{6,10},{3,7},{7,11},{16,20},{20,24},... | collective-permute-start | bytes 5308424 | tf_op jit(solution)/shard_map/ppermute | solution.py:800
  863.5 8.1 collective-permute-start.25
  866.0 37.4 %collective-permute-start.26 = (bf16[1152,1152]{1,0:T(8,128)(2,1)}, bf16[1152,1152]{1,0:T(8,128)(2,1)}, u32[]{:S(2)}, u32[]{:S(2)}) collective-permute-start(bf16[1152,1152]{1,0:T(8,128)(2,1)} %convolution_convert_fusion), channel_id=1, source_target_pairs={{0,16},{16,0},{1,17},{17,1},{2,18},{18,2},{3,19},{19,3},{4,20},{20... | collective-permute-start | bytes 7962632 | tf_op jit(solution)/shard_map/ppermute | solution.py:718
  876.7 69.7 %collective-permute-start.46 = (bf16[2,384,1152]{2,1,0:T(8,128)(2,1)}, bf16[2,384,1152]{2,1,0:T(8,128)(2,1)}, u32[]{:S(2)}, u32[]{:S(2)}) collective-permute-start(bf16[2,384,1152]{2,1,0:T(8,128)(2,1)} %add_convert_fusion.12), channel_id=1, source_target_pairs={{4,0},{8,4},{12,8},{5,1},{9,5},{13,9},{6,2},{10,6},{14,10},{7,3},{... | collective-permute-start | bytes 5308424 | tf_op jit(solution)/shard_map/ppermute | solution.py:800
  897.9 50.5 %collective-permute-start.44 = (bf16[2,384,1152]{2,1,0:T(8,128)(2,1)}, bf16[2,384,1152]{2,1,0:T(8,128)(2,1)}, u32[]{:S(2)}, u32[]{:S(2)}) collective-permute-start(bf16[2,384,1152]{2,1,0:T(8,128)(2,1)} %add_convert_fusion.14), channel_id=1, source_target_pairs={{0,4},{4,8},{8,12},{1,5},{5,9},{9,13},{2,6},{6,10},{10,14},{3,7},{... | collective-permute-start | bytes 5308424 | tf_op jit(solution)/shard_map/ppermute | solution.py:800
  908.3 19.2 %collective-permute-start.36 = (bf16[288,1152]{1,0:T(8,128)(2,1)}, bf16[288,1152]{1,0:T(8,128)(2,1)}, u32[]{:S(2)}, u32[]{:S(2)}) collective-permute-start(bf16[288,1152]{1,0:T(8,128)(2,1)} %get-tuple-element.336), channel_id=1, source_target_pairs={{0,3},{1,2},{2,1},{3,0},{4,7},{5,6},{6,5},{7,4},{8,11},{9,10},{10,... | collective-permute-start | bytes 1990664 | tf_op jit(solution)/shard_map/ppermute | solution.py:739
  911.3 28.0 %collective-permute-start.35 = (bf16[288,1152]{1,0:T(8,128)(2,1)}, bf16[288,1152]{1,0:T(8,128)(2,1)}, u32[]{:S(2)}, u32[]{:S(2)}) collective-permute-start(bf16[288,1152]{1,0:T(8,128)(2,1)} %get-tuple-element.337), channel_id=1, source_target_pairs={{0,2},{1,3},{2,0},{3,1},{4,6},{5,7},{6,4},{7,5},{8,10},{9,11},{10,... | collective-permute-start | bytes 1990664 | tf_op jit(solution)/shard_map/ppermute | solution.py:739
  911.8 28.7 %collective-permute-start.34 = (bf16[288,1152]{1,0:T(8,128)(2,1)}, bf16[288,1152]{1,0:T(8,128)(2,1)}, u32[]{:S(2)}, u32[]{:S(2)}) collective-permute-start(bf16[288,1152]{1,0:T(8,128)(2,1)} %get-tuple-element.335), channel_id=1, source_target_pairs={{0,1},{1,0},{2,3},{3,2},{4,5},{5,4},{6,7},{7,6},{8,9},{9,8},{10,11... | collective-permute-start | bytes 1990664 | tf_op jit(solution)/shard_map/ppermute | solution.py:739
  927.5 26.1 %collective-permute-start.27 = (bf16[6912,128]{1,0:T(8,128)(2,1)S(1)}, bf16[6912,128]{1,0:T(8,128)(2,1)S(1)}, u32[]{:S(2)}, u32[]{:S(2)}) collective-permute-start(bf16[6912,128]{1,0:T(8,128)(2,1)S(1)} %bitcast.383), channel_id=1, source_target_pairs={{0,16},{16,0},{1,17},{17,1},{2,18},{18,2},{3,19},{19,3},{4,20},{20... | collective-permute-start | bytes 5308424 | tf_op jit(solution)/shard_map/ppermute | solution.py:718
  942.6 13.9 %collective-permute-start.39 = (bf16[72,1152]{1,0:T(8,128)(2,1)S(1)}, bf16[72,1152]{1,0:T(8,128)(2,1)S(1)}, u32[]{:S(2)}, u32[]{:S(2)}) collective-permute-start(bf16[72,1152]{1,0:T(8,128)(2,1)S(1)} %get-tuple-element.369), channel_id=1, source_target_pairs={{0,12},{4,0},{8,4},{12,8},{1,13},{5,1},{9,5},{13,9},{2,14},{6,2},{... | collective-permute-start | bytes 497672 | tf_op jit(solution)/shard_map/ppermute | solution.py:734
  945.4 14.8 %collective-permute-start.38 = (bf16[72,1152]{1,0:T(8,128)(2,1)S(1)}, bf16[72,1152]{1,0:T(8,128)(2,1)S(1)}, u32[]{:S(2)}, u32[]{:S(2)}) collective-permute-start(bf16[72,1152]{1,0:T(8,128)(2,1)S(1)} %get-tuple-element.370), channel_id=1, source_target_pairs={{0,8},{4,12},{8,0},{12,4},{1,9},{5,13},{9,1},{13,5},{2,10},{6,14},... | collective-permute-start | bytes 497672 | tf_op jit(solution)/shard_map/ppermute | solution.py:734
  946.4 15.5 %collective-permute-start.37 = (bf16[72,1152]{1,0:T(8,128)(2,1)S(1)}, bf16[72,1152]{1,0:T(8,128)(2,1)S(1)}, u32[]{:S(2)}, u32[]{:S(2)}) collective-permute-start(bf16[72,1152]{1,0:T(8,128)(2,1)S(1)} %get-tuple-element.368), channel_id=1, source_target_pairs={{0,4},{4,8},{8,12},{12,0},{1,5},{5,9},{9,13},{13,1},{2,6},{6,10},{... | collective-permute-start | bytes 497672 | tf_op jit(solution)/shard_map/ppermute | solution.py:734
  953.5 52.8 %collective-permute-start.47 = (bf16[2,384,1152]{2,1,0:T(8,128)(2,1)}, bf16[2,384,1152]{2,1,0:T(8,128)(2,1)}, u32[]{:S(2)}, u32[]{:S(2)}) collective-permute-start(bf16[2,384,1152]{2,1,0:T(8,128)(2,1)} %get-tuple-element.271), channel_id=1, source_target_pairs={{0,16},{16,0},{1,17},{17,1},{2,18},{18,2},{3,19},{19,3},{4,20},{20... | collective-permute-start | bytes 5308424 | tf_op jit(solution)/shard_map/ppermute | solution.py:718
  955.1 14.2 %collective-permute-start.30 = (bf16[1728,128]{1,0:T(8,128)(2,1)}, bf16[1728,128]{1,0:T(8,128)(2,1)}, u32[]{:S(2)}, u32[]{:S(2)}) collective-permute-start(bf16[1728,128]{1,0:T(8,128)(2,1)} %get-tuple-element.345), channel_id=1, source_target_pairs={{0,3},{1,2},{2,1},{3,0},{4,7},{5,6},{6,5},{7,4},{8,11},{9,10},{10,... | collective-permute-start | bytes 1327112 | tf_op jit(solution)/shard_map/ppermute | solution.py:739
  956.5 21.9 %collective-permute-start.29 = (bf16[1728,128]{1,0:T(8,128)(2,1)}, bf16[1728,128]{1,0:T(8,128)(2,1)}, u32[]{:S(2)}, u32[]{:S(2)}) collective-permute-start(bf16[1728,128]{1,0:T(8,128)(2,1)} %get-tuple-element.346), channel_id=1, source_target_pairs={{0,2},{1,3},{2,0},{3,1},{4,6},{5,7},{6,4},{7,5},{8,10},{9,11},{10,... | collective-permute-start | bytes 1327112 | tf_op jit(solution)/shard_map/ppermute | solution.py:739
  960.2 18.2 %collective-permute-start.28 = (bf16[1728,128]{1,0:T(8,128)(2,1)}, bf16[1728,128]{1,0:T(8,128)(2,1)}, u32[]{:S(2)}, u32[]{:S(2)}) collective-permute-start(bf16[1728,128]{1,0:T(8,128)(2,1)} %get-tuple-element.344), channel_id=1, source_target_pairs={{0,1},{1,0},{2,3},{3,2},{4,5},{5,4},{6,7},{7,6},{8,9},{9,8},{10,11... | collective-permute-start | bytes 1327112 | tf_op jit(solution)/shard_map/ppermute | solution.py:739
  962.8 19.9 %collective-permute-start.40 = (bf16[72,1152]{1,0:T(8,128)(2,1)}, bf16[72,1152]{1,0:T(8,128)(2,1)}, u32[]{:S(2)}, u32[]{:S(2)}) collective-permute-start(bf16[72,1152]{1,0:T(8,128)(2,1)} %get-tuple-element.274), channel_id=1, source_target_pairs={{0,16},{16,0},{1,17},{17,1},{2,18},{18,2},{3,19},{19,3},{4,20},{20... | collective-permute-start | bytes 497672 | tf_op jit(solution)/shard_map/ppermute | solution.py:718
  979.9 9.8 collective-permute-start.33
  981.9 19.0 %collective-permute-start.32 = (bf16[432,128]{1,0:T(8,128)(2,1)S(1)}, bf16[432,128]{1,0:T(8,128)(2,1)S(1)}, u32[]{:S(2)}, u32[]{:S(2)}) collective-permute-start(bf16[432,128]{1,0:T(8,128)(2,1)S(1)} %get-tuple-element.377), channel_id=1, source_target_pairs={{0,8},{4,12},{8,0},{12,4},{1,9},{5,13},{9,1},{13,5},{2,10},{6,14},... | collective-permute-start | bytes 331784 | tf_op jit(solution)/shard_map/ppermute | solution.py:734
  982.0 18.9 %collective-permute-start.31 = (bf16[432,128]{1,0:T(8,128)(2,1)S(1)}, bf16[432,128]{1,0:T(8,128)(2,1)S(1)}, u32[]{:S(2)}, u32[]{:S(2)}) collective-permute-start(bf16[432,128]{1,0:T(8,128)(2,1)S(1)} %get-tuple-element.375), channel_id=1, source_target_pairs={{0,4},{4,8},{8,12},{12,0},{1,5},{5,9},{9,13},{13,1},{2,6},{6,10},{... | collective-permute-start | bytes 331784 | tf_op jit(solution)/shard_map/ppermute | solution.py:734
  1013.4 8.8 collective-permute-start.42
  1013.4 8.8 collective-permute-start.41
  (276 other events, 3567.2 us)
Sparse Core Ops, SparseCore 0:
  132.8 70.3 all-gather.4
  204.8 70.1 all-gather.6
  277.2 69.8 all-gather.10
  349.1 69.7 all-gather.8
  603.6 40.4 reduce-scatter.8
  647.0 79.2 reduce-scatter.10
  736.6 27.5 reduce-scatter.18
  766.7 53.5 reduce-scatter.12
  833.4 62.5 reduce-scatter.14
  962.9 36.7 reduce-scatter.16

commit v3 on v2

--- a/solution.py
+++ b/solution.py
@@ -379,6 +379,168 @@
     return (slot_index, token_index)
 
 
+def rows_rows(left, right):
+    return lax.dot_general(
+        left, right, (((0,), (0,)), ((), ())), preferred_element_type=jnp.float32
+    )
+
+
+def expert_kernel(x_ref, up_ref, down_ref, pre_ref, hidden_ref, out_ref, total):
+    step = pl.program_id(0)
+    pre = product(x_ref[...], up_ref[...])
+    pre_ref[...] = pre
+    hidden = jax.nn.gelu(pre).astype(jnp.bfloat16)
+    hidden_ref[...] = hidden
+    part = product(hidden, down_ref[...])
+
+    @pl.when(step == 0)
+    def _():
+        total[...] = part
+
+    @pl.when(step > 0)
+    def _():
+        total[...] += part
+
+    @pl.when(step == pl.num_programs(0) - 1)
+    def _():
+        out_ref[...] = total[...].astype(jnp.bfloat16)
+
+
+def expert_back_kernel(back_ref, up_ref, down_ref, pre_ref, back_pre_ref, out_ref, total):
+    step = pl.program_id(0)
+    back_hidden = cross_cols(back_ref[...], down_ref[...])
+    back_pre = jax.vjp(jax.nn.gelu, pre_ref[...])[1](back_hidden)[0].astype(jnp.bfloat16)
+    back_pre_ref[...] = back_pre
+    part = cross_cols(back_pre, up_ref[...])
+
+    @pl.when(step == 0)
+    def _():
+        total[...] = part
+
+    @pl.when(step > 0)
+    def _():
+        total[...] += part
+
+    @pl.when(step == pl.num_programs(0) - 1)
+    def _():
+        out_ref[...] = total[...].astype(jnp.bfloat16)
+
+
+def expert_call(rows_in, up, down, pre=None):
+    rows, width = rows_in.shape
+    hidden_width = up.shape[1]
+    block = 512
+    fixed = pl.BlockSpec((rows, width), lambda i: (0, 0))
+    wide = pl.BlockSpec((rows, block), lambda i: (0, i))
+    first = pl.BlockSpec((width, block), lambda i: (0, i))
+    second = pl.BlockSpec((block, width), lambda i: (i, 0))
+    low = jax.ShapeDtypeStruct((rows, hidden_width), jnp.bfloat16)
+    out = jax.ShapeDtypeStruct((rows, width), jnp.bfloat16)
+    forward = pre is None
+    return pl.pallas_call(
+        expert_kernel if forward else expert_back_kernel,
+        grid=(hidden_width // block,),
+        in_specs=[fixed, first, second] + ([] if forward else [wide]),
+        out_specs=[wide, wide, fixed] if forward else [wide, fixed],
+        out_shape=[f32(rows, hidden_width), low, out] if forward else [low, out],
+        scratch_shapes=[pltpu.VMEM((rows, width), jnp.float32)],
+        compiler_params=params(40),
+        cost_estimate=pl.CostEstimate(
+            flops=4 * rows * width * hidden_width,
+            bytes_accessed=4 * width * hidden_width + 6 * rows * hidden_width,
+            transcendentals=rows * hidden_width,
+        ),
+        name="expert_rows" if forward else "expert_rows_back",
+    )(rows_in, up, down, *(() if forward else (pre,)))
+
+
+def expert_grads(part, hidden, back_pre, back_flat, flat_rows, received=()):
+    rows, width = back_flat.shape
+    half = hidden.shape[1] // 2
+    block = 384
+    steps = half // block
+
+    def body(part_ref, hidden_ref, back_ref, flat_ref, x_ref, *refs):
+        del part_ref
+        outs = refs[len(received) :]
+        for k, (left, right) in enumerate(((back_ref, x_ref), (hidden_ref, flat_ref))):
+            total = rows_rows(left[...], right[...])
+            if received:
+                total = total + refs[k][...].astype(jnp.float32)
+            outs[k][...] = total.astype(jnp.bfloat16)
+
+    wide = pl.BlockSpec((rows, block), lambda i, part_ref: (0, part_ref[0] * steps + i))
+    fixed = pl.BlockSpec((rows, width), lambda i, part_ref: (0, 0))
+    tall = pl.BlockSpec((block, width), lambda i, part_ref: (i, 0))
+    out = jax.ShapeDtypeStruct((half, width), jnp.bfloat16)
+    return pl.pallas_call(
+        body,
+        grid_spec=pltpu.PrefetchScalarGridSpec(
+            num_scalar_prefetch=1,
+            grid=(steps,),
+            in_specs=[wide, wide, fixed, fixed] + [tall] * len(received),
+            out_specs=[tall, tall],
+        ),
+        out_shape=[out, out],
+        compiler_params=params(40),
+        cost_estimate=pl.CostEstimate(
+            flops=4 * rows * width * half, bytes_accessed=8 * half * width, transcendentals=0
+        ),
+        name="expert_grads",
+    )(part, hidden, back_pre, back_flat, flat_rows, *received)
+
+
+def pack_small(masters):
+    mixer, conv, conv_bias, select, step, step_bias, decay, skip, expert, router = masters
+    chan, states = decay.shape[1:]
+    taps, ranks, low_rank = conv.shape[1], select.shape[2], step.shape[1]
+    part, expert_count = router.shape[1:]
+    thin = taps + states + 3
+
+    def body(mixer_ref, conv_ref, conv_bias_ref, select_ref, step_ref, step_bias_ref, decay_ref,
+             skip_ref, expert_ref, router_ref, out_ref, rows, columns):
+        def shift(by):
+            down = lax.broadcasted_iota(jnp.int32, (lanes, lanes), 0)
+            right = lax.broadcasted_iota(jnp.int32, (lanes, lanes), 1)
+            return jnp.where(right == down + by, 1.0, 0.0).astype(jnp.bfloat16)
+
+        across = lax.broadcasted_iota(jnp.int32, (chan, chan), 0)
+        along = lax.broadcasted_iota(jnp.int32, (chan, chan), 1)
+        same = jnp.where(across == along, 1.0, 0.0).astype(jnp.bfloat16)
+        rows[...] = jnp.zeros_like(rows)
+        rows[:taps] = conv_ref[0]
+        rows[thin - 3 : thin - 2] = conv_bias_ref[...]
+        rows[thin - 2 : thin - 1] = step_bias_ref[...]
+        rows[thin - 1 : thin] = skip_ref[...]
+        rows[thin : thin + 1, :part] = mixer_ref[...]
+        rows[thin + 1 : thin + 2, :part] = expert_ref[...]
+        total = cross_cols(same, rows[...].astype(jnp.bfloat16))
+        columns[...] = jnp.zeros_like(columns)
+        columns[:, :states] = decay_ref[0]
+        total = total + product(columns[...].astype(jnp.bfloat16), shift(taps))
+        columns[...] = jnp.zeros_like(columns)
+        columns[:part, :expert_count] = router_ref[0]
+        total = total + product(columns[...].astype(jnp.bfloat16), shift(thin + 2))
+        out_ref[:, 2 * lanes :] = total.astype(jnp.bfloat16)
+        columns[...] = jnp.zeros_like(columns)
+        columns[:, :ranks] = select_ref[0]
+        out_ref[:, :lanes] = columns[...].astype(jnp.bfloat16)
+        rows[...] = jnp.zeros_like(rows)
+        rows[:low_rank] = step_ref[0]
+        total = cross_cols(same, rows[...].astype(jnp.bfloat16))
+        out_ref[:, lanes : 2 * lanes] = total.astype(jnp.bfloat16)
+
+    return pl.pallas_call(
+        body,
+        out_shape=jax.ShapeDtypeStruct((chan, 3 * lanes), jnp.bfloat16),
+        scratch_shapes=[
+            pltpu.VMEM((lanes, chan), jnp.float32),
+            pltpu.VMEM((chan, lanes), jnp.float32),
+        ],
+        name="pack_small",
+    )(*masters)
+
+
 def gather_kernel(
     phase, along_dp, along_expert, own_refs, layer_refs,
     here_sem, z_send, z_recv, xy_send, xy_recv, c_send, c_recv,
@@ -714,6 +876,138 @@
     return out
 
 
+def settle_kernel(along_dp, along_expert, taps_ref, small_ref, taps_out, small_out,
+                  taps_held, small_held, taps_part, small_part, taps_last, small_last,
+                  xy_send, xy_recv, z_send, z_recv):
+    section = lax.axis_index("section")
+    d = lax.axis_index("dp")
+    e = lax.axis_index("expert")
+    mesh_id = pl.DeviceIdType.MESH
+    pairs = ((taps_ref, taps_held, taps_part, taps_last, taps_out),
+             (small_ref, small_held, small_part, small_last, small_out))
+
+    barrier = pltpu.get_barrier_semaphore()
+    peers = [(section, d, e ^ m) for m in range(1, along_expert)]
+    peers += [(section, lax.rem(d + k, along_dp), e) for k in range(1, along_dp)]
+    for peer in peers:
+        pl.semaphore_signal(barrier, inc=1, device_id=peer, device_id_type=mesh_id)
+    pl.semaphore_wait(barrier, len(peers))
+
+    def across(m, a):
+        return pltpu.make_async_remote_copy(
+            src_ref=pairs[a][0].at[e ^ m], dst_ref=pairs[a][1].at[m - 1],
+            send_sem=xy_send.at[m - 1, a], recv_sem=xy_recv.at[m - 1, a],
+            device_id=(section, d, e ^ m), device_id_type=mesh_id,
+        )
+
+    def along(k, a):
+        there = lax.rem(d + k, along_dp)
+        return pltpu.make_async_remote_copy(
+            src_ref=pairs[a][2].at[there], dst_ref=pairs[a][3].at[k - 1],
+            send_sem=z_send.at[k - 1, a], recv_sem=z_recv.at[k - 1, a],
+            device_id=(section, there, e), device_id_type=mesh_id,
+        )
+
+    def landed(ref, sem):
+        pltpu.make_async_copy(ref, ref, sem).wait()
+
+    for a in range(2):
+        for m in range(1, along_expert):
+            across(m, a).start()
+    for a, (own, held, part, last, out) in enumerate(pairs):
+        for m in range(1, along_expert):
+            landed(held.at[m - 1], xy_recv.at[m - 1, a])
+        for k in range(along_dp):
+            total = own[e, k].astype(jnp.float32)
+            for m in range(1, along_expert):
+                total = total + held[m - 1, k].astype(jnp.float32)
+            part[k] = total.astype(jnp.bfloat16)
+        for k in range(1, along_dp):
+            along(k, a).start()
+    for a, (own, held, part, last, out) in enumerate(pairs):
+        total = part[d].astype(jnp.float32)
+        for k in range(1, along_dp):
+            landed(last.at[k - 1], z_recv.at[k - 1, a])
+            total = total + last[k - 1].astype(jnp.float32)
+        out[...] = total.astype(jnp.bfloat16)
+    for a in range(2):
+        for m in range(1, along_expert):
+            across(m, a).wait_send()
+        for k in range(1, along_dp):
+            along(k, a).wait_send()
+
+
+def settle_call(taps, small):
+    along_dp, along_expert = lax.axis_size("dp"), lax.axis_size("expert")
+    vmem = pl.BlockSpec(memory_space=pltpu.VMEM)
+    dma = pltpu.SemaphoreType.DMA
+    arrays = (taps, small)
+
+    def room(*lead):
+        return [pltpu.VMEM(lead + array.shape[2:], jnp.bfloat16) for array in arrays]
+
+    return pl.pallas_call(
+        functools.partial(settle_kernel, along_dp, along_expert),
+        in_specs=[vmem] * 2,
+        out_specs=[vmem] * 2,
+        out_shape=[jax.ShapeDtypeStruct(array.shape[2:], jnp.bfloat16) for array in arrays],
+        scratch_shapes=room(along_expert - 1, along_dp)
+        + room(along_dp)
+        + room(along_dp - 1)
+        + [dma((along_expert - 1, 2))] * 2
+        + [dma((along_dp - 1, 2))] * 2,
+        compiler_params=pltpu.CompilerParams(
+            collective_id=4, has_side_effects=True, vmem_limit_bytes=40 * 2**20
+        ),
+        cost_estimate=pl.CostEstimate(flops=0, bytes_accessed=200 * 2**20, transcendentals=0),
+        name="last_settle",
+    )(*arrays)
+
+
+def small_grads_call(select, step, conv, decay, lines, models, router, ranks, low_rank):
+    across, along = lax.axis_size("dp"), lax.axis_size("expert")
+    count = across * along
+    chan = select.shape[0] // count
+    part = router.shape[1] // count
+    taps, states = conv.shape[0], decay.shape[0]
+
+    def body(select_ref, step_ref, conv_ref, decay_ref, a_ref, b_ref, c_ref, mixer_ref, expert_ref,
+             router_ref, out_ref, rows, models_rows):
+        down = lax.broadcasted_iota(jnp.int32, (lanes, lanes), 0)
+        right = lax.broadcasted_iota(jnp.int32, (lanes, lanes), 1)
+        same = jnp.where(down == right, 1.0, 0.0).astype(jnp.bfloat16)
+        rows[...] = jnp.zeros_like(rows)
+        rows[ranks : ranks + taps] = conv_ref[...]
+        rows[ranks + taps : ranks + taps + states] = decay_ref[...]
+        at = ranks + taps + states
+        for k, ref in enumerate((a_ref, b_ref, c_ref)):
+            rows[at + k : at + k + 1] = ref[...]
+        models_rows[...] = jnp.zeros_like(models_rows)
+        models_rows[low_rank : low_rank + 1] = mixer_ref[...]
+        models_rows[low_rank + 1 : low_rank + 2] = expert_ref[...]
+        models_rows[low_rank + 2 : low_rank + 2 + router_ref.shape[0]] = router_ref[...]
+        first = rows_rows(rows[...].astype(jnp.bfloat16), same) + select_ref[...]
+        second = step_ref[...]
+        model = rows_rows(models_rows[...].astype(jnp.bfloat16), same)
+        for j in range(count):
+            spot = (j % along) * across + j // along
+            out_ref[spot, 0] = first[j * chan : (j + 1) * chan].astype(jnp.bfloat16)
+            block = second[j * chan : (j + 1) * chan]
+            top = block[:part] + model[j * part : (j + 1) * part]
+            out_ref[spot, 1] = jnp.concatenate([top, block[part:]], axis=0).astype(jnp.bfloat16)
+
+    return pl.pallas_call(
+        body,
+        out_shape=jax.ShapeDtypeStruct((count, 2, chan, lanes), jnp.bfloat16),
+        scratch_shapes=[
+            pltpu.VMEM((lanes, count * chan), jnp.float32),
+            pltpu.VMEM((lanes, router.shape[1]), jnp.float32),
+        ],
+        compiler_params=pltpu.CompilerParams(vmem_limit_bytes=40 * 2**20),
+        name="small_gradients",
+    )(select, step, conv, decay, *lines, *models, router)
+
+
 def swap(array):
     return lax.ppermute(array, "section", [(0, 1), (1, 0)])
 
@@ -870,13 +1164,15 @@
     return total
 
 
-def pack(select, step, rows, model):
-    model = jnp.pad(model, ((0, 0), (0, rows[0].shape[1] - model.shape[1])))
-    thin = piled(rows + [model]).T
-    return jnp.concatenate([widen(select), widen(step), widen(thin)], axis=1)
-
-
-def layer_forward(residual, small, big, routing, documents, mark, low_rank):
+def dispatch_back(grad_out, gate_value, token_index, expert_count, capacity):
+    back_result = (gate_value[:, None] * grad_out).astype(jnp.bfloat16)
+    none = jnp.zeros((1, grad_out.shape[1]), jnp.bfloat16)
+    padded = jnp.concatenate([back_result, none], axis=0)
+    outgoing = padded[token_index].reshape(expert_count, capacity, -1)
+    return lax.all_to_all(outgoing, "expert", split_axis=0, concat_axis=0, tiled=True)
+
+
+def layer_forward(residual, small, big, routing, documents, mark, low_rank, grad_out):
     conv_part, gate_part, output_weight, up_weight, down_weight = big
     row_count, model_width = residual.shape
     tap_count = small.conv.shape[0]
@@ -918,9 +1214,12 @@
     outgoing = padded[token_index].reshape(expert_count, capacity, model_width)
     arrived = lax.all_to_all(outgoing, "expert", split_axis=0, concat_axis=0, tiled=True)
     flat_rows = arrived.reshape(-1, model_width)
-    pre_act = product(flat_rows, up_weight)
-    hidden = jax.nn.gelu(pre_act).astype(jnp.bfloat16)
-    result = product(hidden, down_weight).astype(jnp.bfloat16).reshape(arrived.shape)
+    back_arrived = None
+    if grad_out is not None:
+        back_arrived = dispatch_back(grad_out, gate_value, token_index, expert_count, capacity)
+        (flat_rows,) = tie([flat_rows], (back_arrived,))
+    pre_act, hidden, result = expert_call(flat_rows, up_weight, down_weight)
+    result = result.reshape(arrived.shape)
     returned = lax.all_to_all(result, "expert", split_axis=0, concat_axis=0, tiled=True)
     mixture = returned.reshape(-1, model_width)[slot_index].astype(jnp.float32)
     out_residual = middle + gate_value[:, None] * mixture
@@ -931,7 +1230,7 @@
         gated_out=gated_out, middle=middle, normed_two=normed_two, probability=probability,
         chosen=chosen, gate_value=gate_value, slot_index=slot_index, token_index=token_index,
         pre_act=pre_act, hidden=hidden, flat_rows=flat_rows, mixture=mixture,
-        documents=documents, mark=mark,
+        documents=documents, mark=mark, back_arrived=back_arrived,
     )
     return out_residual, stored
 
@@ -944,20 +1243,22 @@
     expert_count = small.router.shape[0]
     capacity = 2 * row_count // expert_count
     back_gate = jnp.sum(grad_out * kept.mixture, axis=1)
-    back_result = (kept.gate_value[:, None] * grad_out).astype(jnp.bfloat16)
-    padded = jnp.concatenate([back_result, jnp.zeros((1, model_width), jnp.bfloat16)], axis=0)
-    back_outgoing = padded[kept.token_index].reshape(expert_count, capacity, model_width)
-    back_arrived = lax.all_to_all(back_outgoing, "expert", split_axis=0, concat_axis=0, tiled=True)
+    back_arrived = kept.back_arrived
+    if back_arrived is None:
+        back_arrived = dispatch_back(
+            grad_out, kept.gate_value, kept.token_index, expert_count, capacity
+        )
     back_flat = back_arrived.reshape(-1, model_width)
-    back_hidden = cross_cols(back_flat, down_weight)
-    back_pre = jax.vjp(jax.nn.gelu, kept.pre_act)[1](back_hidden)[0].astype(jnp.bfloat16)
-    back_expert = cross_cols(back_pre, up_weight).astype(jnp.bfloat16).reshape(back_arrived.shape)
+    back_pre, back_expert = expert_call(back_flat, up_weight, down_weight, kept.pre_act)
+    back_expert = back_expert.reshape(back_arrived.shape)
     if earlier is not None:
         back_expert, *earlier.moving = tie([back_expert, *earlier.moving], ())
         earlier.advance()
     back_returned = lax.all_to_all(back_expert, "expert", split_axis=0, concat_axis=0, tiled=True)
-    grad_down = joined(halves(kept.hidden, first, 1), lambda half: cross_rows(half, back_flat))
-    grad_up = joined(halves(back_pre, first, 1), lambda half: cross_rows(half, kept.flat_rows))
+    sources = (kept.hidden, back_pre, back_flat, kept.flat_rows)
+    own_part, sent_part = jnp.reshape(section, (1,)), jnp.reshape(1 - section, (1,))
+    received = [swap(part) for part in expert_grads(sent_part, *sources)]
+    grad_up, grad_down = expert_grads(own_part, *sources, received)
     line = LineSum(grad_up, grad_down)
     line.advance()
     back_tokens = back_returned.reshape(-1, model_width)[kept.slot_index].astype(jnp.float32)
@@ -985,11 +1286,7 @@
     together = [part.reshape(-1, part_rows, model_width) for part in (grad_gate, grad_output)]
     together = jnp.stack(together, axis=1).reshape(-1, model_width)
     late = settle_expert(together)
-    ready = (grad_up, grad_down, together)
-    if earlier is None:
-        (back_scanned,) = tie([back_scanned], ready)
-    else:
-        back_scanned, *earlier.moving = tie([back_scanned, *earlier.moving], ready)
+    (back_scanned,) = tie([back_scanned], (grad_up, grad_down, together))
     rate = small.rate
     back_ends = entry_call(kept.step_size, kept.mark, kept.out_wide, rate, back_scanned)
     (adjoint,) = carry_call(back_ends, rate, kept.totals)
@@ -997,7 +1294,11 @@
         kept.step_size, kept.activated, kept.mark, kept.in_wide, kept.out_wide,
         rate, kept.entry_state, adjoint, small.skip, back_scanned,
     )
-    back_step, *line.moving = tie([back_step, *line.moving], pending)
+    moving = list(line.moving) + ([] if earlier is None else list(earlier.moving))
+    back_step, *moving = tie([back_step, *moving], pending)
+    line.moving = tuple(moving[:2])
+    if earlier is not None:
+        earlier.moving = tuple(moving[2:])
     line.advance()
     act_float = kept.activated.astype(jnp.float32)
     grad_skip = jnp.sum(back_scanned * act_float, axis=0, keepdims=True)
@@ -1030,11 +1331,13 @@
         norm_scale, kept.residual, small.mixer_gain
     )[1](back_normed)
     back_residual = back_middle + back_residual_norm
-    lines = piled([grad_conv, grad_decay, grad_conv_bias[None], grad_step_bias, grad_skip])
-    model = piled([grad_mixer_gain[None], grad_expert_gain[None], grad_router])
-    small_grads = (grad_select, grad_step, lines, model)
     if earlier is not None:
-        small_grads = tie(list(small_grads), (grad_taps_in,))
+        grad_select, grad_step = tie([grad_select, grad_step], (grad_taps_in,))
+    small_grads = small_grads_call(
+        grad_select, grad_step, grad_conv, grad_decay,
+        (grad_conv_bias[None], grad_step_bias, grad_skip),
+        (grad_mixer_gain[None], grad_expert_gain[None]), grad_router, ranks, ranks - 2 * rate.shape[0],
+    )
     return back_residual, grad_taps_in, late, line, small_grads
 
 
@@ -1047,17 +1350,18 @@
         down = lax.broadcasted_iota(jnp.int32, (lanes, lanes), 0)
         right = lax.broadcasted_iota(jnp.int32, (lanes, lanes), 1)
         same = jnp.where(down == right, 1.0, 0.0).astype(jnp.bfloat16)
-        rows = cross_cols(same, total_ref[2])
+        rows = cross_cols(same, total_ref[0])
+        others = cross_cols(same, total_ref[1])
         select[0] = total_ref[0].astype(jnp.float32)[:, :ranks]
-        step[0] = cross_cols(same, total_ref[1])[:low_rank]
-        conv[0] = rows[:taps]
-        decay[0] = total_ref[2].astype(jnp.float32)[:, taps : taps + states]
+        step[0] = others[:low_rank]
+        conv[0] = rows[ranks : ranks + taps]
+        decay[0] = total_ref[0].astype(jnp.float32)[:, ranks + taps : ranks + taps + states]
         for ref, at in ((conv_bias, thin - 3), (step_bias, thin - 2), (skip, thin - 1)):
-            ref[...] = rows[at : at + 1]
-        mixer[...] = rows[thin : thin + 1, :part]
-        expert[...] = rows[thin + 1 : thin + 2, :part]
-        whole = total_ref[2].astype(jnp.float32)
-        router[0] = whole[:part, thin + 2 : thin + 2 + expert_count]
+            ref[...] = rows[ranks + at : ranks + at + 1]
+        mixer[...] = others[low_rank : low_rank + 1, :part]
+        expert[...] = others[low_rank + 1 : low_rank + 2, :part]
+        whole = total_ref[1].astype(jnp.float32)
+        router[0] = whole[:part, low_rank + 2 : low_rank + 2 + expert_count]
 
     line = f32(1, chan)
     return pl.pallas_call(
@@ -1108,18 +1412,18 @@
     expert_count = router_weight.shape[2]
 
     thin = tap_count + states + 3
-    packed = pack(
-        select_weight[0],
-        step_weight[0].T,
-        [conv_weight[0], decay_log[0].T, conv_bias, step_bias, skip_gain],
-        piled([mixer_gain, expert_gain, router_weight[0].T]),
+    packed = pack_small(
+        (
+            mixer_gain, conv_weight, conv_bias, select_weight, step_weight, step_bias, decay_log,
+            skip_gain, expert_gain, router_weight,
+        )
     )
     wide = input_weight.shape[2] // 2
     experts = expert_parts(up_weight[0, 0], down_weight[0, 0], first)
     early = gather_call(
         0,
         (
-            packed.astype(jnp.bfloat16),
+            packed,
             input_weight[0, :, :wide].astype(jnp.bfloat16),
             input_weight[0, :, wide:].astype(jnp.bfloat16),
             output_weight[0].astype(jnp.bfloat16),
@@ -1165,17 +1469,19 @@
     mark = doc_marks(documents, tap_count)
 
     residual = lax.dynamic_index_in_dim(inputs, section, 0, keepdims=False).astype(jnp.float32)
+    grad_last = lax.dynamic_index_in_dim(cotangent, section, 0, keepdims=False)
+    grad_last = grad_last.astype(jnp.float32)
     outputs_seen = []
     kept = []
     for layer in range(2):
         out_residual, stored = layer_forward(
-            residual, small[layer], big[layer], routing[layer], documents, mark, low_rank
+            residual, small[layer], big[layer], routing[layer], documents, mark, low_rank, grad_last if layer else None
         )
         outputs_seen.append(out_residual.astype(jnp.bfloat16))
         residual = outputs_seen[-1].astype(jnp.float32)
         kept.append(stored)
 
-    grad_out = lax.dynamic_index_in_dim(cotangent, section, 0, keepdims=False).astype(jnp.float32)
+    grad_out = grad_last
     input_grads = [None, None]
     settled = [None, None]
     small_sums = [None, None]
@@ -1191,35 +1497,28 @@
             pending = (settle_dp(settle_expert(grad_taps_in)), settle_dp(late))
         else:
             settled[1] = pending + (earlier.total(),)
-            final_late = (settle_dp(late), line.total())
-        across, along = lax.axis_size("dp"), lax.axis_size("expert")
-        grad_select, grad_step, rows, model = small_grads
-        model = model.reshape(-1, count, part)
-        model = jnp.pad(model, ((0, 0), (0, 0), (0, chan - part))).reshape(-1, count * chan)
-        rows = widen(piled([rows, model]).T)
-        whole = jnp.stack(
-            [
-                array.astype(jnp.bfloat16).reshape(across, along, chan, lanes)
-                for array in (grad_select, grad_step, rows)
-            ],
-            axis=2,
-        )
-        small_sums[layer] = whole.transpose(1, 0, 2, 3, 4).reshape(-1, lanes)
-
+            final_late = settle_dp(late)
+        small_sums[layer] = small_grads
+
+    across, along = lax.axis_size("dp"), lax.axis_size("expert")
     own_small, sent_small = pick(first, small_sums[0], small_sums[1])
     own_small = own_small.astype(jnp.float32) + swap(sent_small).astype(jnp.float32)
-    total = settle_direct(own_small.astype(jnp.bfloat16))
+    last, small_last = settle_call(
+        grad_taps_in.reshape(along, across, part, model_width),
+        own_small.astype(jnp.bfloat16).reshape(along, across, 2, chan, lanes),
+    )
+    settled[0] = (last, final_late, line.total())
     small_out = small_outputs(
-        total.reshape(3, chan, lanes), tap_count, states, ranks, low_rank, expert_count, part
-    )
-    settled[0] = (settle_direct(grad_taps_in),) + final_late
+        small_last, tap_count, states, ranks, low_rank, expert_count, part
+    )
+    experts_back = hand_back((settled[0][2], settled[1][2]), first, 1)
+    up_back, down_back = experts_back[0].T, experts_back[1]
     both_late = [(late_one[1][:part], late_one[1][part:]) for late_one in settled]
 
     def whole_input():
         taps = hand_back((settled[0][0], settled[1][0]), first, 1)
         return jnp.concatenate([taps, hand_back([pair[0] for pair in both_late], first, 1)], axis=1)
 
-    experts_back = hand_back((settled[0][2], settled[1][2]), first, 1)
     def both(array):
         mine, sent = pick(first, array[0], array[1])
         return jnp.stack(pick(first, mine, swap(sent)))[None]
@@ -1232,8 +1531,8 @@
         *small_out[1:8],
         hand_back([pair[1] for pair in both_late], first, 0)[None],
         *small_out[8:],
-        experts_back[0].T[None, None],
-        experts_back[1][None, None],
+        up_back[None, None],
+        down_back[None, None],
     )
 
 

time: 1040 us -> 1030 us (level)
  Pallas kernels: 338 us -> 472 us
  matrix products: 192 us -> 92.4 us
  waiting for transfers between devices: 139 us -> 106 us
  other arithmetic: 126 us -> 103 us
  starting transfers between devices: 90.6 us -> 73.4 us
  blocking collectives: 0 us -> 12.8 us
    pallas_call x0 -> x12, Pallas kernels: none -> 135 us  [the longest x1 56 us: settle_call(): pl.pallas_call(functools.partial(settle_kernel, along_dp, along_expert),...]
    ppermute x12 -> x0, waiting for transfers between devices: 56.4 us -> none  [the longest x6 36.8 us: crossed(): return lax.ppermute(array, axis, [(i, i ^ mask) for i in range(length)])]
    ppermute x12, waiting for transfers between devices: 16.6 us -> 51.7 us  [advance(): moved.append(lax.ppermute(held.astype(jnp.bfloat16), 'dp', pairs))]
    dot_general x26 -> x18, matrix products: 67.6 us -> 33.1 us  [cross_rows(): lax.dot_general(left, right, (((0,), (0,)), ((), ())), preferred_element_...]
    dot_general x16 -> x12, matrix products: 60.4 us -> 26.8 us  [product(): return jnp.dot(left, right, preferred_element_type=jnp.float32)]
    dot_general x16 -> x12, matrix products: 64 us -> 32.5 us  [cross_cols(): lax.dot_general(left, right, (((1,), (1,)), ((), ())), preferred_element_...]
    ppermute x12 -> x0, starting transfers between devices: 16.7 us -> none  [the longest x6 8.46 us: turned(): lax.ppermute(array, axis, [(i, (i + hop) % length) for i in range(length)])]
    all_to_all x0 -> x1, blocking collectives: none -> 12.8 us  [layer_forward(): lax.all_to_all(outgoing, 'expert', split_axis=0, concat_axis=0, tiled=True)]
  transfers between devices with their start and end apart: 66 -> 53, of which waited for: 18 -> 13; matrix products, arithmetic and copies ran while one was open for 35% -> 25% of each run, Pallas kernels for 33% -> 44%
where the time goes in v3:
time: 1030 us; the launch traced here: 1020 us
  Pallas kernels  472 us (46%)
  local copies, waits for them, and re-layouts  139 us (13%)
  waiting for transfers between devices  106 us (10%)
  other arithmetic  103 us (10%)
  matrix products  92.4 us (9%)
  starting transfers between devices  73.4 us (7%)
  between operations  18.6 us (2%)
  blocking collectives  12.8 us (1%)
    pallas_call x2, Pallas kernels, gather_call(): pl.pallas_call(body, in_specs=[pl.BlockSpec(memory_space=pltpu.HBM)] * le...  177 us
    unnamed x579, local copies, waits for them, and re-layouts  80.4 us
    pallas_call x2, Pallas kernels, back_call(): pl.pallas_call(back_kernel, grid=(width // block,), in_specs=[wide, wide,...  66.9 us
    pallas_call x1, Pallas kernels, settle_call(): pl.pallas_call(functools.partial(settle_kernel, along_dp, along_expert),...  56 us
    ppermute x12, waiting for transfers between devices, advance(): moved.append(lax.ppermute(held.astype(jnp.bfloat16), 'dp', pairs))  51.7 us
    pallas_call x4, Pallas kernels, expert_call(): pl.pallas_call(expert_kernel if forward else expert_back_kernel, grid=(hi...  50.9 us
    pallas_call x4, Pallas kernels, carry_call(): pl.pallas_call(functools.partial(carry_kernel, count, backward), in_specs...  38.1 us
    ppermute x12, starting transfers between devices, advance(): moved.append(lax.ppermute(held.astype(jnp.bfloat16), 'dp', pairs))  33.4 us
  transfers between devices with their start and end apart: 53, of which 13 were waited for; matrix products, arithmetic and copies ran while one was open for 25% of the time, Pallas kernels for 44%

profile of v3, /device:TPU:0, one launch (start us, length us, event | category | flops | bytes accessed | tf_op | source)
XLA Modules:
  0.0 1017.1 jit_solution(17427341810738120900)
XLA Ops:
  22.5 94.2 %weights_along_dp.1 = (bf16[16,144,384]{2,1,0:T(8,128)(2,1)}, bf16[16,72,2304]{2,1,0:T(8,128)(2,1)}, bf16[16,72,2304]{2,1,0:T(8,128)(2,1)}, bf16[16,144,1152]{2,...) custom-call(bf16[144,384]{1,0:T(8,128)(2,1)} %pack_small.1.refs_0_, ...), custom_call_target="tpu_custom_call" | custom-call | bytes 262144000 | tf_op jit(solution)/shard_map/weights_along_dp/pallas_call | solution.py:776
  130.2 83.1 %weights_across.1 = (bf16[16,144,384]{2,1,0:T(8,128)(2,1)}, bf16[16,72,2304]{2,1,0:T(8,128)(2,1)}, bf16[16,72,2304]{2,1,0:T(8,128)(2,1)}, bf16[16,144,1152]{2,1,...) custom-call(bf16[16,144,384]{2,1,0:T(8,128)(2,1)} %get-tuple-element, ...), custom_call_target="tpu_custom_call", output_to_operand_aliasing={{0}: (0, {}), {1}: (1, {}), {2}: (2, {}), {3}: (3, {}), {4}... | custom-call | bytes 262144000 | tf_op jit(solution)/shard_map/weights_across/pallas_call | solution.py:776
  215.0 4.0 convolution_convert_fusion.9
  230.8 7.8 state_end.2.refs_0_
  239.3 9.7 state_carry.2
  252.0 11.5 %state_scan.2 = f32[192,2304]{1,0:T(8,128)S(1)} custom-call(f32[192,2304]{1,0:T(8,128)S(1)} %copy-done.78, bf16[192,2304]{1,0:T(8,128)(2,1)S(1)} %get-tuple-element.309.act_ref, f32[192,128]{1,0:T(8,128)S(1)} %broadcast_in_dim.263.start_ref, f32[192,16,128]{2,1,0:T(8,128)S(1)} %broadcast_in_dim.264.in_ref, f32[192,16,128]{2,1,0:T(8,128)S(1)} %broadcast_in_dim.265.out_ref, ...), custom_call_target="tpu_custom_call" | custom-call | flops 84934656 | bytes 4423680 | tf_op jit(solution)/shard_map/state_scan/pallas_call | solution.py:256
  263.6 5.8 multiply_convert_fusion.2
  273.9 3.5 all-to-all-start
  277.4 11.2 %all-to-all-done = bf16[4,96,1152]{2,1,0:T(8,128)(2,1)S(1)} async-done(((bf16[4,96,1152]{2,1,0:T(8,128)(2,1)}), bf16[4,96,1152]{2,1,0:T(8,128)(2,1)S(1)}, u32[]{:S(2)}, u32[]{:S(2)}) %all-to-all-start) | async-done | bytes 884768 | tf_op jit(solution)/shard_map/all_to_all | solution.py:1215
  288.6 12.8 %expert_rows.2 = (f32[384,3072]{1,0:T(8,128)S(1)}, bf16[384,3072]{1,0:T(8,128)(2,1)S(1)}, bf16[384,1152]{1,0:T(8,128)(2,1)}) custom-call(bf16[384,1152]{1,0:T(8,128)(2,1)S(1)} %bitcast.269, bf16[1152,3072]{1,0:T(8,128)(2,1)} %all-gather.5.cloned.1.call-done.up_ref, bf16[3072,1152]{1,0:T(8,128)(2,1)} %all-gather.7.cloned.1.call-done.down_ref), custom_call_target="tpu_custom_call" | custom-call | flops 5435817984 | bytes 21233664 | tf_op jit(solution)/shard_map/expert_rows/pallas_call | solution.py:440
  305.0 4.0 all-to-all-start.1
  310.1 10.3 %all-to-all-done.1 = bf16[4,96,1152]{2,1,0:T(8,128)(2,1)S(1)} async-done(((bf16[4,96,1152]{2,1,0:T(8,128)(2,1)}), bf16[4,96,1152]{2,1,0:T(8,128)(2,1)S(1)}, u32[]{:S(2)}, u32[]{:S(2)}) %all-to-all-start.1) | async-done | bytes 884768 | tf_op jit(solution)/shard_map/all_to_all | solution.py:1223
  323.0 3.9 convolution_convert_fusion.7
  326.9 3.3 collective-permute-start.4
  338.3 7.8 state_end.3.refs_0_
  348.0 10.1 state_carry.3
  361.2 11.5 %state_scan.3 = f32[192,2304]{1,0:T(8,128)S(1)} custom-call(f32[192,2304]{1,0:T(8,128)S(1)} %copy-done.81, bf16[192,2304]{1,0:T(8,128)(2,1)S(1)} %get-tuple-element.305.act_ref, f32[192,128]{1,0:T(8,128)S(1)} %copy-done.61, f32[192,16,128]{2,1,0:T(8,128)S(1)} %broadcast_in_dim.269.in_ref, f32[192,16,128]{2,1,0:T(8,128)S(1)} %broadcast_in_dim.270.out_ref, ...), custom_call_target="tpu_custom_call" | custom-call | flops 84934656 | bytes 4423680 | tf_op jit(solution)/shard_map/state_scan/pallas_call | solution.py:256
  372.7 5.8 multiply_convert_fusion
  384.6 3.5 all-to-all-start.3
  390.4 7.1 all-to-all-done.3.refs_1_
  397.4 12.8 %all_to_all.40 = bf16[4,96,1152]{2,1,0:T(8,128)(2,1)} all-to-all(bf16[4,96,1152]{2,1,0:T(8,128)(2,1)S(1)} %bitcast.332), channel_id=1, replica_groups=mesh['section'=2,'dp'=4,'expert'=4] {'expert'}, dimensions={0} | all-to-all | bytes 1769472 | tf_op jit(solution)/shard_map/all_to_all | solution.py:1215
  411.5 12.3 %expert_rows.3 = (f32[384,3072]{1,0:T(8,128)S(1)}, bf16[384,3072]{1,0:T(8,128)(2,1)S(1)}, bf16[384,1152]{1,0:T(8,128)(2,1)}) custom-call(bf16[384,1152]{1,0:T(8,128)(2,1)S(1)} %copy-done.12, bf16[1152,3072]{1,0:T(8,128)(2,1)} %all-gather.9.cloned.1.call-done.up_ref, bf16[3072,1152]{1,0:T(8,128)(2,1)} %all-gather.11.cloned.1.call-done.down_ref), custom_call_target="tpu_custom_call" | custom-call | flops 5435817984 | bytes 21233664 | tf_op jit(solution)/shard_map/expert_rows/pallas_call | solution.py:440
  425.3 13.4 %expert_rows_back.2 = (bf16[384,3072]{1,0:T(8,128)(2,1)S(1)}, bf16[384,1152]{1,0:T(8,128)(2,1)}) custom-call(bf16[384,1152]{1,0:T(8,128)(2,1)S(1)} %bitcast.264, bf16[1152,3072]{1,0:T(8,128)(2,1)} %all-gather.9.cloned.1.call-done.up_ref, bf16[3072,1152]{1,0:T(8,128)(2,1)} %all-gather.11.cloned.1.call-done.down_ref, f32[384,3072]{1,0:T(8,128)S(1)} %get-tuple-element.117.pre_ref), custom_call_target="tpu_custom_call" | custom-call | flops 5435817984 | bytes 21233664 | tf_op jit(solution)/shard_map/expert_rows_back/pallas_call | solution.py:440
  440.1 3.6 all-to-all-start.5
  447.1 6.0 expert_grads.4
  454.0 3.7 all-to-all-start.4
  477.5 5.7 fusion.120
  488.8 6.7 expert_grads.5
  506.7 3.0 collective-permute-start.10
  511.7 3.0 pad_maximum_fusion
  519.0 7.4 adjoint_entry.2.refs_0_
  527.1 8.8 adjoint_carry.2.adj_ref
  535.9 33.5 %scan_back.2 = (f32[192,2304]{1,0:T(8,128)}, f32[192,2304]{1,0:T(8,128)}, f32[16,2304]{1,0:T(8,128)}, f32[192,16,128]{2,1,0:T(8,128)}, f32[192,16,128]{2,1,0:T(8,128)}) custom-call(f32[192,2304]{1,0:T(8,128)} %copy-done.80, bf16[192,2304]{1,0:T(8,128)(2,1)} %copy-done.18, f32[192,128]{1,0:T(8,128)} %copy-done.60, f32[192,16,128]{2,1,0:T(8,128)} %copy-done.46, ...), custom_call_target="tpu_custom_call" | custom-call | flops 283115520 | bytes 8847360 | tf_op jit(solution)/shard_map/scan_back/pallas_call | solution.py:290
  581.9 4.0 collective-permute-done.12
  587.1 4.9 collective-permute-done.23
  607.5 4.7 fusion.179
  614.5 3.3 add_convert_fusion.14
  619.7 3.2 add_convert_fusion.15
  633.3 3.7 all-to-all-start.6
  642.5 11.7 %all-to-all-done.6 = bf16[4,96,1152]{2,1,0:T(8,128)(2,1)S(1)} async-done(((bf16[4,96,1152]{2,1,0:T(8,128)(2,1)}), bf16[4,96,1152]{2,1,0:T(8,128)(2,1)S(1)}, u32[]{:S(2)}, u32[]{:S(2)}) %all-to-all-start.6) | async-done | bytes 884768 | tf_op jit(solution)/shard_map/all_to_all | solution.py:1172
  657.0 12.4 %expert_rows_back.3 = (bf16[384,3072]{1,0:T(8,128)(2,1)S(1)}, bf16[384,1152]{1,0:T(8,128)(2,1)S(1)}) custom-call(bf16[384,1152]{1,0:T(8,128)(2,1)S(1)} %bitcast.272, bf16[1152,3072]{1,0:T(8,128)(2,1)} %all-gather.5.cloned.1.call-done.up_ref, bf16[3072,1152]{1,0:T(8,128)(2,1)} %all-gather.7.cloned.1.call-done.down_ref, f32[384,3072]{1,0:T(8,128)S(1)} %copy-done.76), custom_call_target="tpu_custom_call" | custom-call | flops 5435817984 | bytes 21233664 | tf_op jit(solution)/shard_map/expert_rows_back/pallas_call | solution.py:440
  671.8 3.6 all-to-all-start.7
  679.1 5.9 expert_grads.6
  685.6 3.2 add_convert_fusion.12
  695.2 5.9 fusion.119
  703.7 3.3 add_convert_fusion.13
  707.0 5.6 collective-permute-start.21
  716.1 6.7 expert_grads.7
  728.3 5.2 dynamic-slice_bitcast_fusion.10
  741.1 5.3 fusion.180
  759.6 7.4 adjoint_entry.3.refs_0_
  767.7 9.6 adjoint_carry.3.adj_ref
  777.2 33.4 %scan_back.3 = (f32[192,2304]{1,0:T(8,128)}, f32[192,2304]{1,0:T(8,128)}, f32[16,2304]{1,0:T(8,128)}, f32[192,16,128]{2,1,0:T(8,128)}, f32[192,16,128]{2,1,0:T(8,128)}) custom-call(f32[192,2304]{1,0:T(8,128)} %copy-done.77, bf16[192,2304]{1,0:T(8,128)(2,1)} %copy-done.15, f32[192,128]{1,0:T(8,128)} %copy-done.60, f32[192,16,128]{2,1,0:T(8,128)} %copy-done.43, ...), custom_call_target="tpu_custom_call" | custom-call | flops 283115520 | bytes 8847360 | tf_op jit(solution)/shard_map/scan_back/pallas_call | solution.py:290
  813.5 6.9 collective-permute-done.19.refs_1_
  824.1 4.4 collective-permute-start.31
  835.3 3.5 multiply_reduce_fusion.4
  849.5 16.7 %collective-permute-done.31 = bf16[2,384,1152]{2,1,0:T(8,128)(2,1)S(1)} collective-permute-done((bf16[2,384,1152]{2,1,0:T(8,128)(2,1)S(1)}, bf16[2,384,1152]{2,1,0:T(8,128)(2,1)S(1)}, u32[]{:S(2)}, u32[]{:S(2)}) %collective-permute-start.31) | collective-permute-done | bytes 1769504 | tf_op jit(solution)/shard_map/ppermute | solution.py:1094
  867.8 5.7 collective-permute-start.32
  888.6 20.9 %collective-permute-done.32 = bf16[2,384,1152]{2,1,0:T(8,128)(2,1)} collective-permute-done((bf16[2,384,1152]{2,1,0:T(8,128)(2,1)}, bf16[2,384,1152]{2,1,0:T(8,128)(2,1)}, u32[]{:S(2)}, u32[]{:S(2)}) %collective-permute-start.32) | collective-permute-done | bytes 1769504 | tf_op jit(solution)/shard_map/ppermute | solution.py:1094
  909.5 7.2 collective-permute-done.34
  916.7 5.5 broadcast_select_fusion.2
  927.0 56.0 %last_settle.1 = (bf16[72,1152]{1,0:T(8,128)(2,1)S(1)}, bf16[2,144,128]{2,1,0:T(8,128)(2,1)S(1)}) custom-call(bf16[4,4,72,1152]{3,2,1,0:T(8,128)(2,1)S(1)} %bitcast.263, bf16[4,4,2,144,128]{4,3,2,1,0:T(8,128)(2,1)S(1)} %bitcast.268), custom_call_target="tpu_custom_call" | custom-call | bytes 209715200 | tf_op jit(solution)/shard_map/last_settle/pallas_call | solution.py:949
  991.9 3.4 maximum_convert_fusion
  998.0 5.3 slice_bitcast_fusion
  (926 shorter events, 289.0 us)
Async XLA Ops:
  7.2 116.8 %copy-start = (s32[2,1,4]{2,1,0:T(1,128)S(1)}, s32[2,1,4]{2,1,0:T(1,128)}, u32[]{:S(2)}) copy-start(s32[2,1,4]{2,1,0:T(1,128)} %param.21) | copy-start | bytes 100
  7.2 281.4 %all-gather.5.cloned.1.call-start = ((), (), s32[]{:S(2)}) async-start(), calls=%async_computation.14 | async-start | bytes 7962624 | tf_op jit(solution)/shard_map/all_gather | solution.py:1048
  10.5 106.3 %collective-permute-start.3 = (bf16[384,1152]{1,0:T(8,128)(2,1)}, bf16[384,1152]{1,0:T(8,128)(2,1)}, u32[]{:S(2)}, u32[]{:S(2)}) collective-permute-start(bf16[384,1152]{1,0:T(8,128)(2,1)} %select_bitcast_fusion.2), channel_id=1, source_target_pairs={{0,16},{16,0},{1,17},{17,1},{2,18},{18,2},{3,19},{19,3},{4,20},{20... | collective-permute-start | bytes 2654216 | tf_op jit(solution)/shard_map/ppermute | solution.py:1012
  14.1 105.2 %collective-permute-start.2 = (bf16[1152,384]{1,0:T(8,128)(2,1)}, bf16[1152,384]{1,0:T(8,128)(2,1)}, u32[]{:S(2)}, u32[]{:S(2)}) collective-permute-start(bf16[1152,384]{1,0:T(8,128)(2,1)} %broadcast_select_fusion.8), channel_id=1, source_target_pairs={{0,16},{16,0},{1,17},{17,1},{2,18},{18,2},{3,19},{19,3},{4,20},{20... | collective-permute-start | bytes 2654216 | tf_op jit(solution)/shard_map/ppermute | solution.py:1012
  122.0 166.7 %all-gather.7.cloned.1.call-start = ((), (), s32[]{:S(2)}) async-start(), calls=%async_computation.15 | async-start | bytes 7962624 | tf_op jit(solution)/shard_map/all_gather | solution.py:1048
  122.7 287.5 %all-gather.11.cloned.1.call-start = ((), (), s32[]{:S(2)}) async-start(), calls=%async_computation.17 | async-start | bytes 7962624 | tf_op jit(solution)/shard_map/all_gather | solution.py:1048
  123.5 286.8 %all-gather.9.cloned.1.call-start = ((), (), s32[]{:S(2)}) async-start(), calls=%async_computation.16 | async-start | bytes 7962624 | tf_op jit(solution)/shard_map/all_gather | solution.py:1048
  123.5 1.6 collective-permute-start.1
  124.9 138.6 %copy-start.240 = (f32[192]{0:T(256)}, f32[192]{0:T(256)S(1)}, u32[]{:S(2)}) copy-start(f32[192]{0:T(256)S(1)} %fusion.140) | copy-start | bytes 2308
  125.0 98.9 %copy-start.228 = (pred[192]{0:T(512)(128)(4,1)}, pred[192]{0:T(512)(128)(4,1)S(1)}, u32[]{:S(2)}) copy-start(pred[192]{0:T(512)(128)(4,1)S(1)} %get-tuple-element.392) | copy-start | bytes 580
  125.0 98.9 %copy-start.232 = (pred[192]{0:T(512)(128)(4,1)}, pred[192]{0:T(512)(128)(4,1)S(1)}, u32[]{:S(2)}) copy-start(pred[192]{0:T(512)(128)(4,1)S(1)} %get-tuple-element.393) | copy-start | bytes 580
  125.1 98.9 %copy-start.236 = (pred[192]{0:T(512)(128)(4,1)}, pred[192]{0:T(512)(128)(4,1)S(1)}, u32[]{:S(2)}) copy-start(pred[192]{0:T(512)(128)(4,1)S(1)} %get-tuple-element.394) | copy-start | bytes 580
  125.1 102.1 %copy-start.267 = (pred[128]{0:T(512)(128)(4,1)}, pred[128]{0:T(512)(128)(4,1)S(1)}, u32[]{:S(2)}) copy-start(pred[128]{0:T(512)(128)(4,1)S(1)} %iota_compare_fusion.8) | copy-start | bytes 388
  125.1 184.9 %copy-start.219 = (s32[192]{0:T(256)}, s32[192]{0:T(256)S(1)}, u32[]{:S(2)}) copy-start(s32[192]{0:T(256)S(1)} %get-tuple-element.389) | copy-start | bytes 2308
  129.1 142.1 %copy-start.245 = (s32[1024]{0:T(1024)}, s32[1024]{0:T(1024)S(1)}, u32[]{:S(2)}) copy-start(s32[1024]{0:T(1024)S(1)} %pad_clamp_fusion.3) | copy-start | bytes 12292
  129.6 190.7 %copy-start.258 = (s32[1024]{0:T(1024)}, s32[1024]{0:T(1024)S(1)}, u32[]{:S(2)}) copy-start(s32[1024]{0:T(1024)S(1)} %pad_clamp_fusion.2) | copy-start | bytes 12292
  219.0 4.7 collective-permute-start
  223.5 86.2 %copy-start.213 = (bf16[4,1152]{1,0:T(4,128)(2,1)}, bf16[4,1152]{1,0:T(4,128)(2,1)S(1)}, u32[]{:S(2)}) copy-start(bf16[4,1152]{1,0:T(4,128)(2,1)S(1)} %convert_element_type.455) | copy-start | bytes 27652
  223.7 85.3 %copy-start.191 = (f32[6,16,144]{2,1,0:T(8,128)}, f32[6,16,144]{2,1,0:T(8,128)S(1)}, u32[]{:S(2)}) copy-start(f32[6,16,144]{2,1,0:T(8,128)S(1)} %reshape.637) | copy-start | bytes 165892
  273.9 14.8 %all-to-all-start = ((bf16[4,96,1152]{2,1,0:T(8,128)(2,1)}), bf16[4,96,1152]{2,1,0:T(8,128)(2,1)S(1)}, u32[]{:S(2)}, u32[]{:S(2)}) async-start(bf16[4,96,1152]{2,1,0:T(8,128)(2,1)} %bitcast.16), calls=%async_computation | async-start | bytes 1769472 | tf_op jit(solution)/shard_map/all_to_all | solution.py:1215
  305.0 15.4 %all-to-all-start.1 = ((bf16[4,96,1152]{2,1,0:T(8,128)(2,1)}), bf16[4,96,1152]{2,1,0:T(8,128)(2,1)S(1)}, u32[]{:S(2)}, u32[]{:S(2)}) async-start(bf16[4,96,1152]{2,1,0:T(8,128)(2,1)} %bitcast.21), calls=%async_computation.1 | async-start | bytes 1769472 | tf_op jit(solution)/shard_map/all_to_all | solution.py:1223
  326.9 4.8 collective-permute-start.4
  384.6 12.9 %all-to-all-start.3 = ((bf16[4,96,1152]{2,1,0:T(8,128)(2,1)}), bf16[4,96,1152]{2,1,0:T(8,128)(2,1)S(1)}, u32[]{:S(2)}, u32[]{:S(2)}) async-start(bf16[4,96,1152]{2,1,0:T(8,128)(2,1)} %bitcast.331), calls=%async_computation.3 | async-start | bytes 1769472 | tf_op jit(solution)/shard_map/all_to_all | solution.py:1172
  440.1 13.9 %all-to-all-start.5 = ((bf16[4,96,1152]{2,1,0:T(8,128)(2,1)}), bf16[4,96,1152]{2,1,0:T(8,128)(2,1)S(1)}, u32[]{:S(2)}, u32[]{:S(2)}) async-start(bf16[4,96,1152]{2,1,0:T(8,128)(2,1)} %bitcast.45), calls=%async_computation.5 | async-start | bytes 1769472 | tf_op jit(solution)/shard_map/all_to_all | solution.py:1257
  453.0 35.7 %collective-permute-start.6 = (bf16[1536,1152]{1,0:T(8,128)(2,1)}, bf16[1536,1152]{1,0:T(8,128)(2,1)}, u32[]{:S(2)}, u32[]{:S(2)}) collective-permute-start(bf16[1536,1152]{1,0:T(8,128)(2,1)} %get-tuple-element.121), channel_id=1, source_target_pairs={{0,16},{16,0},{1,17},{17,1},{2,18},{18,2},{3,19},{19,3},{4,20},{20... | collective-permute-start | bytes 10616840 | tf_op jit(solution)/shard_map/ppermute | solution.py:1012
  453.0 35.7 %collective-permute-start.7 = (bf16[1536,1152]{1,0:T(8,128)(2,1)}, bf16[1536,1152]{1,0:T(8,128)(2,1)}, u32[]{:S(2)}, u32[]{:S(2)}) collective-permute-start(bf16[1536,1152]{1,0:T(8,128)(2,1)} %get-tuple-element.122), channel_id=1, source_target_pairs={{0,16},{16,0},{1,17},{17,1},{2,18},{18,2},{3,19},{19,3},{4,20},{20... | collective-permute-start | bytes 10616840 | tf_op jit(solution)/shard_map/ppermute | solution.py:1012
  454.0 16.6 %all-to-all-start.4 = ((bf16[4,96,1152]{2,1,0:T(8,128)(2,1)}), bf16[4,96,1152]{2,1,0:T(8,128)(2,1)S(1)}, u32[]{:S(2)}, u32[]{:S(2)}) async-start(bf16[4,96,1152]{2,1,0:T(8,128)(2,1)} %bitcast.36), calls=%async_computation.4 | async-start | bytes 1769472 | tf_op jit(solution)/shard_map/all_to_all | solution.py:1223
  457.7 245.9 %reduce-scatter.9.cloned.1.call-start = ((), (), s32[]{:S(2)}) async-start(), calls=%async_computation.18 | async-start | bytes 3317760 | tf_op jit(solution)/shard_map/reduce_scatter | solution.py:1118
  485.7 24.0 %collective-permute-start.8 = (bf16[1152,1152]{1,0:T(8,128)(2,1)}, bf16[1152,1152]{1,0:T(8,128)(2,1)S(1)}, u32[]{:S(2)}, u32[]{:S(2)}) collective-permute-start(bf16[1152,1152]{1,0:T(8,128)(2,1)} %convolution_convert_fusion.5), channel_id=1, source_target_pairs={{0,16},{16,0},{1,17},{17,1},{2,18},{18,2},{3,19},{19,3},{4,20},{20... | collective-permute-start | bytes 7962632 | tf_op jit(solution)/shard_map/ppermute | solution.py:1012
  488.3 22.4 %collective-permute-start.9 = (bf16[1152,1152]{1,0:T(8,128)(2,1)}, bf16[1152,1152]{1,0:T(8,128)(2,1)S(1)}, u32[]{:S(2)}, u32[]{:S(2)}) collective-permute-start(bf16[1152,1152]{1,0:T(8,128)(2,1)} %convolution_convert_fusion.4), channel_id=1, source_target_pairs={{0,16},{16,0},{1,17},{17,1},{2,18},{18,2},{3,19},{19,3},{4,20},{20... | collective-permute-start | bytes 7962632 | tf_op jit(solution)/shard_map/ppermute | solution.py:1012
  503.4 68.6 %collective-permute-start.11 = (bf16[2,384,1152]{2,1,0:T(8,128)(2,1)}, bf16[2,384,1152]{2,1,0:T(8,128)(2,1)}, u32[]{:S(2)}, u32[]{:S(2)}) collective-permute-start(bf16[2,384,1152]{2,1,0:T(8,128)(2,1)} %pad_maximum_fusion.3), channel_id=1, source_target_pairs={{12,8},{13,9},{14,10},{15,11},{28,24},{29,25},{30,26},{31,27}} | collective-permute-start | bytes 5308424 | tf_op jit(solution)/shard_map/ppermute | solution.py:1094
  506.7 65.3 %collective-permute-start.10 = (bf16[2,384,1152]{2,1,0:T(8,128)(2,1)}, bf16[2,384,1152]{2,1,0:T(8,128)(2,1)}, u32[]{:S(2)}, u32[]{:S(2)}) collective-permute-start(bf16[2,384,1152]{2,1,0:T(8,128)(2,1)} %pad_maximum_fusion.2), channel_id=1, source_target_pairs={{0,4},{1,5},{2,6},{3,7},{16,20},{17,21},{18,22},{19,23}} | collective-permute-start | bytes 5308424 | tf_op jit(solution)/shard_map/ppermute | solution.py:1094
  580.0 5.9 collective-permute-start.12
  587.0 5.0 collective-permute-start.23
  594.6 133.7 %reduce-scatter.11.cloned.1.call-start = ((), (), s32[]{:S(2)}) async-start(), calls=%async_computation.19 | async-start | bytes 6635520 | tf_op jit(solution)/shard_map/reduce_scatter | solution.py:1118
  606.4 5.7 collective-permute-start.5
  617.8 54.0 %collective-permute-start.14 = (bf16[2,384,1152]{2,1,0:T(8,128)(2,1)}, bf16[2,384,1152]{2,1,0:T(8,128)(2,1)}, u32[]{:S(2)}, u32[]{:S(2)}) collective-permute-start(bf16[2,384,1152]{2,1,0:T(8,128)(2,1)} %add_convert_fusion.14), channel_id=1, source_target_pairs={{8,4},{12,8},{9,5},{13,9},{10,6},{14,10},{11,7},{15,11},{24,20},{2... | collective-permute-start | bytes 5308424 | tf_op jit(solution)/shard_map/ppermute | solution.py:1094
  622.9 48.9 %collective-permute-start.13 = (bf16[2,384,1152]{2,1,0:T(8,128)(2,1)}, bf16[2,384,1152]{2,1,0:T(8,128)(2,1)}, u32[]{:S(2)}, u32[]{:S(2)}) collective-permute-start(bf16[2,384,1152]{2,1,0:T(8,128)(2,1)} %add_convert_fusion.15), channel_id=1, source_target_pairs={{0,4},{4,8},{1,5},{5,9},{2,6},{6,10},{3,7},{7,11},{16,20},{20,24},... | collective-permute-start | bytes 5308424 | tf_op jit(solution)/shard_map/ppermute | solution.py:1094
  633.3 20.9 %all-to-all-start.6 = ((bf16[4,96,1152]{2,1,0:T(8,128)(2,1)}), bf16[4,96,1152]{2,1,0:T(8,128)(2,1)S(1)}, u32[]{:S(2)}, u32[]{:S(2)}) async-start(bf16[4,96,1152]{2,1,0:T(8,128)(2,1)} %bitcast.64), calls=%async_computation.6 | async-start | bytes 1769472 | tf_op jit(solution)/shard_map/all_to_all | solution.py:1172
  671.8 18.3 %all-to-all-start.7 = ((bf16[4,96,1152]{2,1,0:T(8,128)(2,1)}), bf16[4,96,1152]{2,1,0:T(8,128)(2,1)S(1)}, u32[]{:S(2)}, u32[]{:S(2)}) async-start(bf16[4,96,1152]{2,1,0:T(8,128)(2,1)} %get-tuple-element.135), calls=%async_computation.7 | async-start | bytes 1769472 | tf_op jit(solution)/shard_map/all_to_all | solution.py:1257
  675.5 144.9 %reduce-scatter.19.cloned.1.call-start = ((), (), s32[]{:S(2)}) async-start(), calls=%async_computation.23 | async-start | bytes 829440
  685.0 30.7 %collective-permute-start.15 = (bf16[1536,1152]{1,0:T(8,128)(2,1)}, bf16[1536,1152]{1,0:T(8,128)(2,1)}, u32[]{:S(2)}, u32[]{:S(2)}) collective-permute-start(bf16[1536,1152]{1,0:T(8,128)(2,1)} %get-tuple-element.138), channel_id=1, source_target_pairs={{0,16},{16,0},{1,17},{17,1},{2,18},{18,2},{3,19},{19,3},{4,20},{20... | collective-permute-start | bytes 10616840 | tf_op jit(solution)/shard_map/ppermute | solution.py:1012
  685.0 31.0 %collective-permute-start.16 = (bf16[1536,1152]{1,0:T(8,128)(2,1)}, bf16[1536,1152]{1,0:T(8,128)(2,1)}, u32[]{:S(2)}, u32[]{:S(2)}) collective-permute-start(bf16[1536,1152]{1,0:T(8,128)(2,1)} %get-tuple-element.139), channel_id=1, source_target_pairs={{0,16},{16,0},{1,17},{17,1},{2,18},{18,2},{3,19},{19,3},{4,20},{20... | collective-permute-start | bytes 10616840 | tf_op jit(solution)/shard_map/ppermute | solution.py:1012
  688.8 124.6 %collective-permute-start.22 = (bf16[2,384,1152]{2,1,0:T(8,128)(2,1)}, bf16[2,384,1152]{2,1,0:T(8,128)(2,1)}, u32[]{:S(2)}, u32[]{:S(2)}) collective-permute-start(bf16[2,384,1152]{2,1,0:T(8,128)(2,1)} %add_convert_fusion.12), channel_id=1, source_target_pairs={{4,0},{8,4},{12,8},{5,1},{9,5},{13,9},{6,2},{10,6},{14,10},{7,3},{... | collective-permute-start | bytes 5308424 | tf_op jit(solution)/shard_map/ppermute | solution.py:1094
  703.6 34.7 %collective-permute-start.17 = (bf16[1152,1152]{1,0:T(8,128)(2,1)}, bf16[1152,1152]{1,0:T(8,128)(2,1)}, u32[]{:S(2)}, u32[]{:S(2)}) collective-permute-start(bf16[1152,1152]{1,0:T(8,128)(2,1)} %convolution_convert_fusion.3), channel_id=1, source_target_pairs={{0,16},{16,0},{1,17},{17,1},{2,18},{18,2},{3,19},{19,3},{4,20},{20... | collective-permute-start | bytes 7962632 | tf_op jit(solution)/shard_map/ppermute | solution.py:1012
  703.6 116.8 %reduce-scatter.13.cloned.1.call-start = ((), (), s32[]{:S(2)}) async-start(), calls=%async_computation.20 | async-start | bytes 1658880 | tf_op jit(solution)/shard_map/reduce_scatter | solution.py:1122
  707.0 106.4 %collective-permute-start.21 = (bf16[2,384,1152]{2,1,0:T(8,128)(2,1)}, bf16[2,384,1152]{2,1,0:T(8,128)(2,1)}, u32[]{:S(2)}, u32[]{:S(2)}) collective-permute-start(bf16[2,384,1152]{2,1,0:T(8,128)(2,1)} %add_convert_fusion.13), channel_id=1, source_target_pairs={{0,4},{4,8},{8,12},{1,5},{5,9},{9,13},{2,6},{6,10},{10,14},{3,7},{... | collective-permute-start | bytes 5308424 | tf_op jit(solution)/shard_map/ppermute | solution.py:1094
  715.8 33.5 %collective-permute-start.18 = (bf16[1152,1152]{1,0:T(8,128)(2,1)}, bf16[1152,1152]{1,0:T(8,128)(2,1)}, u32[]{:S(2)}, u32[]{:S(2)}) collective-permute-start(bf16[1152,1152]{1,0:T(8,128)(2,1)} %convolution_convert_fusion.2), channel_id=1, source_target_pairs={{0,16},{16,0},{1,17},{17,1},{2,18},{18,2},{3,19},{19,3},{4,20},{20... | collective-permute-start | bytes 7962632 | tf_op jit(solution)/shard_map/ppermute | solution.py:1012
  728.3 196.5 %reduce-scatter.15.cloned.1.call-start = ((), (), s32[]{:S(2)}) async-start(), calls=%async_computation.21 | async-start | bytes 6635520 | tf_op jit(solution)/shard_map/reduce_scatter | solution.py:1118
  735.0 78.5 %collective-permute-start.20 = (bf16[2,384,1152]{2,1,0:T(8,128)(2,1)}, bf16[2,384,1152]{2,1,0:T(8,128)(2,1)}, u32[]{:S(2)}, u32[]{:S(2)}) collective-permute-start(bf16[2,384,1152]{2,1,0:T(8,128)(2,1)} %pad_maximum_fusion.5), channel_id=1, source_target_pairs={{12,8},{13,9},{14,10},{15,11},{28,24},{29,25},{30,26},{31,27}} | collective-permute-start | bytes 5308424 | tf_op jit(solution)/shard_map/ppermute | solution.py:1094
  738.2 82.2 %collective-permute-start.19 = (bf16[2,384,1152]{2,1,0:T(8,128)(2,1)}, bf16[2,384,1152]{2,1,0:T(8,128)(2,1)}, u32[]{:S(2)}, u32[]{:S(2)}) collective-permute-start(bf16[2,384,1152]{2,1,0:T(8,128)(2,1)} %pad_maximum_fusion.4), channel_id=1, source_target_pairs={{0,4},{1,5},{2,6},{3,7},{16,20},{17,21},{18,22},{19,23}} | collective-permute-start | bytes 5308424 | tf_op jit(solution)/shard_map/ppermute | solution.py:1094
  755.0 240.3 %reduce-scatter.17.cloned.1.call-start = ((), (), s32[]{:S(2)}) async-start(), calls=%async_computation.22 | async-start | bytes 1658880 | tf_op jit(solution)/shard_map/reduce_scatter | solution.py:1122
  824.1 42.1 %collective-permute-start.31 = (bf16[2,384,1152]{2,1,0:T(8,128)(2,1)S(1)}, bf16[2,384,1152]{2,1,0:T(8,128)(2,1)S(1)}, u32[]{:S(2)}, u32[]{:S(2)}) collective-permute-start(bf16[2,384,1152]{2,1,0:T(8,128)(2,1)S(1)} %add_convert_fusion.11), channel_id=1, source_target_pairs={{0,4},{4,8},{1,5},{5,9},{2,6},{6,10},{3,7},{7,11},{16,20},{20,24},... | collective-permute-start | bytes 5308424 | tf_op jit(solution)/shard_map/ppermute | solution.py:1094
  830.7 42.9 %collective-permute-start.33 = (bf16[2,384,1152]{2,1,0:T(8,128)(2,1)S(1)}, bf16[2,384,1152]{2,1,0:T(8,128)(2,1)S(1)}, u32[]{:S(2)}, u32[]{:S(2)}) collective-permute-start(bf16[2,384,1152]{2,1,0:T(8,128)(2,1)S(1)} %add_convert_fusion.9), channel_id=1, source_target_pairs={{8,4},{12,8},{9,5},{13,9},{10,6},{14,10},{11,7},{15,11},{24,20},{2... | collective-permute-start | bytes 5308424 | tf_op jit(solution)/shard_map/ppermute | solution.py:1094
  839.7 6.3 collective-permute-start.24
  847.2 33.3 %collective-permute-start.26 = (bf16[1152,1152]{1,0:T(8,128)(2,1)S(1)}, bf16[1152,1152]{1,0:T(8,128)(2,1)S(1)}, u32[]{:S(2)}, u32[]{:S(2)}) collective-permute-start(bf16[1152,1152]{1,0:T(8,128)(2,1)S(1)} %convolution_convert_fusion), channel_id=1, source_target_pairs={{0,16},{16,0},{1,17},{17,1},{2,18},{18,2},{3,19},{19,3},{4,20},{20... | collective-permute-start | bytes 7962632 | tf_op jit(solution)/shard_map/ppermute | solution.py:1012
  867.8 41.7 %collective-permute-start.32 = (bf16[2,384,1152]{2,1,0:T(8,128)(2,1)}, bf16[2,384,1152]{2,1,0:T(8,128)(2,1)}, u32[]{:S(2)}, u32[]{:S(2)}) collective-permute-start(bf16[2,384,1152]{2,1,0:T(8,128)(2,1)} %add_convert_fusion.10), channel_id=1, source_target_pairs={{0,4},{4,8},{8,12},{1,5},{5,9},{9,13},{2,6},{6,10},{10,14},{3,7},{... | collective-permute-start | bytes 5308424 | tf_op jit(solution)/shard_map/ppermute | solution.py:1094
  875.3 41.4 %collective-permute-start.34 = (bf16[2,384,1152]{2,1,0:T(8,128)(2,1)}, bf16[2,384,1152]{2,1,0:T(8,128)(2,1)}, u32[]{:S(2)}, u32[]{:S(2)}) collective-permute-start(bf16[2,384,1152]{2,1,0:T(8,128)(2,1)} %add_convert_fusion.8), channel_id=1, source_target_pairs={{4,0},{8,4},{12,8},{5,1},{9,5},{13,9},{6,2},{10,6},{14,10},{7,3},{... | collective-permute-start | bytes 5308424 | tf_op jit(solution)/shard_map/ppermute | solution.py:1094
  880.5 41.8 %collective-permute-start.25 = (f32[192,1152]{1,0:T(8,128)}, f32[192,1152]{1,0:T(8,128)}, u32[]{:S(2)}, u32[]{:S(2)}) collective-permute-start(f32[192,1152]{1,0:T(8,128)} %get-tuple-element.297), channel_id=1, source_target_pairs={{0,16},{16,0},{1,17},{17,1},{2,18},{18,2},{3,19},{19,3},{4,20},{20... | collective-permute-start | bytes 2654216 | tf_op jit(solution)/shard_map/ppermute | solution.py:1012
  888.1 36.8 %collective-permute-start.27 = (bf16[16,2,144,128]{3,2,1,0:T(8,128)(2,1)}, bf16[16,2,144,128]{3,2,1,0:T(8,128)(2,1)}, u32[]{:S(2)}, u32[]{:S(2)}) collective-permute-start(bf16[16,2,144,128]{3,2,1,0:T(8,128)(2,1)} %broadcast_select_fusion.4), channel_id=1, source_target_pairs={{0,16},{16,0},{1,17},{17,1},{2,18},{18,2},{3,19},{19,3},{4,20},{20... | collective-permute-start | bytes 3538952 | tf_op jit(solution)/shard_map/ppermute | solution.py:1012
  922.2 67.7 %collective-permute-start.35 = (bf16[2,384,1152]{2,1,0:T(8,128)(2,1)}, bf16[2,384,1152]{2,1,0:T(8,128)(2,1)}, u32[]{:S(2)}, u32[]{:S(2)}) collective-permute-start(bf16[2,384,1152]{2,1,0:T(8,128)(2,1)} %get-tuple-element.289), channel_id=1, source_target_pairs={{0,16},{16,0},{1,17},{17,1},{2,18},{18,2},{3,19},{19,3},{4,20},{20... | collective-permute-start | bytes 5308424 | tf_op jit(solution)/shard_map/ppermute | solution.py:1012
  983.0 6.2 collective-permute-start.28
  997.0 9.3 collective-permute-start.29
  998.0 8.3 collective-permute-start.30
  (272 other events, 1844.0 us)
Sparse Core Ops, SparseCore 0:
  122.1 70.3 all-gather.4
  194.1 70.1 all-gather.6
  266.4 69.8 all-gather.10
  338.3 69.7 all-gather.8
  594.7 40.1 reduce-scatter.8
  637.7 69.3 reduce-scatter.10
  709.4 31.0 reduce-scatter.18
  742.9 51.4 reduce-scatter.12
  797.7 62.8 reduce-scatter.14
  925.0 30.0 reduce-scatter.16

commit v4 on v3

--- a/solution.py
+++ b/solution.py
@@ -1374,6 +1374,37 @@
     )(total)
 
 
+def expert_outputs(own, got, section):
+    width, model_width = own.shape[1:]
+
+    def body(section_ref, own_ref, got_ref, up_ref, down_ref):
+        def fill(low, high):
+            across = lax.broadcasted_iota(jnp.int32, (2 * width, 2 * width), 0)
+            along = lax.broadcasted_iota(jnp.int32, (2 * width, 2 * width), 1)
+            same = jnp.where(across == along, 1.0, 0.0).astype(jnp.bfloat16)
+            up_ref[...] = rows_rows(jnp.concatenate([low[0], high[0]], axis=0), same)
+            down_ref[:width] = low[1].astype(jnp.float32)
+            down_ref[width:] = high[1].astype(jnp.float32)
+
+        @pl.when(section_ref[0] == 0)
+        def _():
+            fill(own_ref, got_ref)
+
+        @pl.when(section_ref[0] != 0)
+        def _():
+            fill(got_ref, own_ref)
+
+    vmem = pl.BlockSpec(memory_space=pltpu.VMEM)
+    return pl.pallas_call(
+        body,
+        in_specs=[pl.BlockSpec(memory_space=pltpu.SMEM), vmem, vmem],
+        out_specs=[vmem, vmem],
+        out_shape=[f32(model_width, 2 * width), f32(2 * width, model_width)],
+        compiler_params=pltpu.CompilerParams(vmem_limit_bytes=40 * 2**20),
+        name="expert_outputs",
+    )(jnp.reshape(section, (1,)), own, got)
+
+
 def doc_marks(documents, tap_count):
     own = documents[tap_count - 1 :]
     begins = own != documents[tap_count - 2 : -1]
@@ -1511,8 +1542,8 @@
     small_out = small_outputs(
         small_last, tap_count, states, ranks, low_rank, expert_count, part
     )
-    experts_back = hand_back((settled[0][2], settled[1][2]), first, 1)
-    up_back, down_back = experts_back[0].T, experts_back[1]
+    expert_own, expert_sent = pick(first, settled[0][2], settled[1][2])
+    up_back, down_back = expert_outputs(expert_own, swap(expert_sent), section)
     both_late = [(late_one[1][:part], late_one[1][part:]) for late_one in settled]
 
     def whole_input():

time: 1030 us -> 1030 us (level)
  waiting for transfers between devices: 106 us -> 122 us
  other arithmetic: 103 us -> 89.4 us
    ppermute x12, waiting for transfers between devices: 51.7 us -> 67.7 us  [advance(): moved.append(lax.ppermute(held.astype(jnp.bfloat16), 'dp', pairs))]
    unnamed x579 -> x572, local copies, waits for them, and re-layouts: 80.4 us -> 80.1 us
  transfers between devices with their start and end apart: 53 -> 53, of which waited for: 13 -> 13; matrix products, arithmetic and copies ran while one was open for 25% -> 23% of each run, Pallas kernels for 44% -> 44%
where the time goes in v4:
time: 1030 us; the launch traced here: 1020 us
  Pallas kernels  477 us (46%)
  local copies, waits for them, and re-layouts  133 us (13%)
  waiting for transfers between devices  122 us (12%)
  matrix products  95.9 us (9%)
  other arithmetic  89.4 us (9%)
  starting transfers between devices  73.5 us (7%)
  between operations  18.6 us (2%)
  blocking collectives  12.9 us (1%)
    pallas_call x2, Pallas kernels, gather_call(): pl.pallas_call(body, in_specs=[pl.BlockSpec(memory_space=pltpu.HBM)] * le...  177 us
    unnamed x572, local copies, waits for them, and re-layouts  80.1 us
    ppermute x12, waiting for transfers between devices, advance(): moved.append(lax.ppermute(held.astype(jnp.bfloat16), 'dp', pairs))  67.7 us
    pallas_call x2, Pallas kernels, back_call(): pl.pallas_call(back_kernel, grid=(width // block,), in_specs=[wide, wide,...  66.9 us
    pallas_call x1, Pallas kernels, settle_call(): pl.pallas_call(functools.partial(settle_kernel, along_dp, along_expert),...  53.7 us
    pallas_call x4, Pallas kernels, expert_call(): pl.pallas_call(expert_kernel if forward else expert_back_kernel, grid=(hi...  50.9 us
    pallas_call x4, Pallas kernels, carry_call(): pl.pallas_call(functools.partial(carry_kernel, count, backward), in_specs...  38.3 us
    dot_general x18, matrix products, cross_rows(): lax.dot_general(left, right, (((0,), (0,)), ((), ())), preferred_element_...  36.5 us
  transfers between devices with their start and end apart: 53, of which 13 were waited for; matrix products, arithmetic and copies ran while one was open for 23% of the time, Pallas kernels for 44%

profile of v4, /device:TPU:0, one launch (start us, length us, event | category | flops | bytes accessed | tf_op | source)
XLA Modules:
  0.0 1021.9 jit_solution(17175538338565172057)
XLA Ops:
  22.5 94.2 %weights_along_dp.1 = (bf16[16,144,384]{2,1,0:T(8,128)(2,1)}, bf16[16,72,2304]{2,1,0:T(8,128)(2,1)}, bf16[16,72,2304]{2,1,0:T(8,128)(2,1)}, bf16[16,144,1152]{2,...) custom-call(bf16[144,384]{1,0:T(8,128)(2,1)} %pack_small.1.refs_0_, ...), custom_call_target="tpu_custom_call" | custom-call | bytes 262144000 | tf_op jit(solution)/shard_map/weights_along_dp/pallas_call | solution.py:776
  130.2 83.1 %weights_across.1 = (bf16[16,144,384]{2,1,0:T(8,128)(2,1)}, bf16[16,72,2304]{2,1,0:T(8,128)(2,1)}, bf16[16,72,2304]{2,1,0:T(8,128)(2,1)}, bf16[16,144,1152]{2,1,...) custom-call(bf16[16,144,384]{2,1,0:T(8,128)(2,1)} %get-tuple-element, ...), custom_call_target="tpu_custom_call", output_to_operand_aliasing={{0}: (0, {}), {1}: (1, {}), {2}: (2, {}), {3}: (3, {}), {4}... | custom-call | bytes 262144000 | tf_op jit(solution)/shard_map/weights_across/pallas_call | solution.py:776
  214.9 4.0 convolution_convert_fusion.9
  230.7 7.8 state_end.2.refs_0_
  239.3 9.7 state_carry.2
  252.0 11.5 %state_scan.2 = f32[192,2304]{1,0:T(8,128)S(1)} custom-call(f32[192,2304]{1,0:T(8,128)S(1)} %copy-done.78, bf16[192,2304]{1,0:T(8,128)(2,1)S(1)} %get-tuple-element.310.act_ref, f32[192,128]{1,0:T(8,128)S(1)} %broadcast_in_dim.266.start_ref, f32[192,16,128]{2,1,0:T(8,128)S(1)} %broadcast_in_dim.267.in_ref, f32[192,16,128]{2,1,0:T(8,128)S(1)} %broadcast_in_dim.268.out_ref, ...), custom_call_target="tpu_custom_call" | custom-call | flops 84934656 | bytes 4423680 | tf_op jit(solution)/shard_map/state_scan/pallas_call | solution.py:256
  263.6 5.8 multiply_convert_fusion.2
  273.9 3.5 all-to-all-start
  277.4 11.2 %all-to-all-done = bf16[4,96,1152]{2,1,0:T(8,128)(2,1)S(1)} async-done(((bf16[4,96,1152]{2,1,0:T(8,128)(2,1)}), bf16[4,96,1152]{2,1,0:T(8,128)(2,1)S(1)}, u32[]{:S(2)}, u32[]{:S(2)}) %all-to-all-start) | async-done | bytes 884768 | tf_op jit(solution)/shard_map/all_to_all | solution.py:1215
  288.7 12.8 %expert_rows.2 = (f32[384,3072]{1,0:T(8,128)S(1)}, bf16[384,3072]{1,0:T(8,128)(2,1)S(1)}, bf16[384,1152]{1,0:T(8,128)(2,1)}) custom-call(bf16[384,1152]{1,0:T(8,128)(2,1)S(1)} %bitcast.263, bf16[1152,3072]{1,0:T(8,128)(2,1)} %all-gather.5.cloned.1.call-done.up_ref, bf16[3072,1152]{1,0:T(8,128)(2,1)} %all-gather.7.cloned.1.call-done.down_ref), custom_call_target="tpu_custom_call" | custom-call | flops 5435817984 | bytes 21233664 | tf_op jit(solution)/shard_map/expert_rows/pallas_call | solution.py:440
  305.0 4.0 all-to-all-start.1
  310.1 10.3 %all-to-all-done.1 = bf16[4,96,1152]{2,1,0:T(8,128)(2,1)S(1)} async-done(((bf16[4,96,1152]{2,1,0:T(8,128)(2,1)}), bf16[4,96,1152]{2,1,0:T(8,128)(2,1)S(1)}, u32[]{:S(2)}, u32[]{:S(2)}) %all-to-all-start.1) | async-done | bytes 884768 | tf_op jit(solution)/shard_map/all_to_all | solution.py:1223
  322.9 3.9 convolution_convert_fusion.7
  326.9 3.3 collective-permute-start.4
  338.3 7.8 state_end.3.refs_0_
  348.0 10.1 state_carry.3
  361.1 11.5 %state_scan.3 = f32[192,2304]{1,0:T(8,128)S(1)} custom-call(f32[192,2304]{1,0:T(8,128)S(1)} %copy-done.81, bf16[192,2304]{1,0:T(8,128)(2,1)S(1)} %get-tuple-element.306.act_ref, f32[192,128]{1,0:T(8,128)S(1)} %copy-done.61, f32[192,16,128]{2,1,0:T(8,128)S(1)} %broadcast_in_dim.272.in_ref, f32[192,16,128]{2,1,0:T(8,128)S(1)} %broadcast_in_dim.273.out_ref, ...), custom_call_target="tpu_custom_call" | custom-call | flops 84934656 | bytes 4423680 | tf_op jit(solution)/shard_map/state_scan/pallas_call | solution.py:256
  372.7 5.8 multiply_convert_fusion
  384.6 3.5 all-to-all-start.3
  390.4 7.1 all-to-all-done.3.refs_1_
  397.4 12.9 %all_to_all.40 = bf16[4,96,1152]{2,1,0:T(8,128)(2,1)} all-to-all(bf16[4,96,1152]{2,1,0:T(8,128)(2,1)S(1)} %bitcast.326), channel_id=1, replica_groups=mesh['section'=2,'dp'=4,'expert'=4] {'expert'}, dimensions={0} | all-to-all | bytes 1769472 | tf_op jit(solution)/shard_map/all_to_all | solution.py:1215
  411.6 12.4 %expert_rows.3 = (f32[384,3072]{1,0:T(8,128)S(1)}, bf16[384,3072]{1,0:T(8,128)(2,1)S(1)}, bf16[384,1152]{1,0:T(8,128)(2,1)}) custom-call(bf16[384,1152]{1,0:T(8,128)(2,1)S(1)} %copy-done.12, bf16[1152,3072]{1,0:T(8,128)(2,1)} %all-gather.9.cloned.1.call-done.up_ref, bf16[3072,1152]{1,0:T(8,128)(2,1)} %all-gather.11.cloned.1.call-done.down_ref), custom_call_target="tpu_custom_call" | custom-call | flops 5435817984 | bytes 21233664 | tf_op jit(solution)/shard_map/expert_rows/pallas_call | solution.py:440
  425.4 13.4 %expert_rows_back.2 = (bf16[384,3072]{1,0:T(8,128)(2,1)S(1)}, bf16[384,1152]{1,0:T(8,128)(2,1)}) custom-call(bf16[384,1152]{1,0:T(8,128)(2,1)S(1)} %bitcast.258, bf16[1152,3072]{1,0:T(8,128)(2,1)} %all-gather.9.cloned.1.call-done.up_ref, bf16[3072,1152]{1,0:T(8,128)(2,1)} %all-gather.11.cloned.1.call-done.down_ref, f32[384,3072]{1,0:T(8,128)S(1)} %get-tuple-element.119.pre_ref), custom_call_target="tpu_custom_call" | custom-call | flops 5435817984 | bytes 21233664 | tf_op jit(solution)/shard_map/expert_rows_back/pallas_call | solution.py:440
  440.2 3.6 all-to-all-start.5
  447.2 6.0 expert_grads.4
  454.0 3.8 all-to-all-start.4
  477.7 5.7 fusion.120
  488.9 6.7 expert_grads.5
  511.7 3.0 pad_maximum_fusion
  519.0 7.4 adjoint_entry.2.refs_0_
  527.1 9.0 adjoint_carry.2.adj_ref
  536.1 33.5 %scan_back.2 = (f32[192,2304]{1,0:T(8,128)}, f32[192,2304]{1,0:T(8,128)}, f32[16,2304]{1,0:T(8,128)}, f32[192,16,128]{2,1,0:T(8,128)}, f32[192,16,128]{2,1,0:T(8,128)}) custom-call(f32[192,2304]{1,0:T(8,128)} %copy-done.80, bf16[192,2304]{1,0:T(8,128)(2,1)} %copy-done.18, f32[192,128]{1,0:T(8,128)} %copy-done.60, f32[192,16,128]{2,1,0:T(8,128)} %copy-done.46, ...), custom_call_target="tpu_custom_call" | custom-call | flops 283115520 | bytes 8847360 | tf_op jit(solution)/shard_map/scan_back/pallas_call | solution.py:290
  582.0 4.0 collective-permute-done.12
  587.2 4.9 collective-permute-done.23
  607.6 4.7 fusion.179
  614.6 3.4 add_convert_fusion.14
  619.9 3.2 add_convert_fusion.15
  633.5 3.7 all-to-all-start.6
  642.7 11.9 %all-to-all-done.6 = bf16[4,96,1152]{2,1,0:T(8,128)(2,1)S(1)} async-done(((bf16[4,96,1152]{2,1,0:T(8,128)(2,1)}), bf16[4,96,1152]{2,1,0:T(8,128)(2,1)S(1)}, u32[]{:S(2)}, u32[]{:S(2)}) %all-to-all-start.6) | async-done | bytes 884768 | tf_op jit(solution)/shard_map/all_to_all | solution.py:1172
  657.3 12.4 %expert_rows_back.3 = (bf16[384,3072]{1,0:T(8,128)(2,1)S(1)}, bf16[384,1152]{1,0:T(8,128)(2,1)S(1)}) custom-call(bf16[384,1152]{1,0:T(8,128)(2,1)S(1)} %bitcast.266, bf16[1152,3072]{1,0:T(8,128)(2,1)} %all-gather.5.cloned.1.call-done.up_ref, bf16[3072,1152]{1,0:T(8,128)(2,1)} %all-gather.7.cloned.1.call-done.down_ref, f32[384,3072]{1,0:T(8,128)S(1)} %copy-done.76), custom_call_target="tpu_custom_call" | custom-call | flops 5435817984 | bytes 21233664 | tf_op jit(solution)/shard_map/expert_rows_back/pallas_call | solution.py:440
  672.1 3.6 all-to-all-start.7
  679.4 5.9 expert_grads.6
  685.8 3.2 add_convert_fusion.12
  695.5 5.9 fusion.119
  704.0 3.3 add_convert_fusion.13
  707.3 5.7 collective-permute-start.21
  716.5 6.7 expert_grads.7
  728.8 5.1 dynamic-slice_bitcast_fusion.10
  741.5 5.4 fusion.180
  746.9 3.1 add_convert_fusion.3
  760.4 7.4 adjoint_entry.3.refs_0_
  768.4 9.5 adjoint_carry.3.adj_ref
  778.0 33.4 %scan_back.3 = (f32[192,2304]{1,0:T(8,128)}, f32[192,2304]{1,0:T(8,128)}, f32[16,2304]{1,0:T(8,128)}, f32[192,16,128]{2,1,0:T(8,128)}, f32[192,16,128]{2,1,0:T(8,128)}) custom-call(f32[192,2304]{1,0:T(8,128)} %copy-done.77, bf16[192,2304]{1,0:T(8,128)(2,1)} %copy-done.15, f32[192,128]{1,0:T(8,128)} %copy-done.60, f32[192,16,128]{2,1,0:T(8,128)} %copy-done.43, ...), custom_call_target="tpu_custom_call" | custom-call | flops 283115520 | bytes 8847360 | tf_op jit(solution)/shard_map/scan_back/pallas_call | solution.py:290
  814.0 6.7 collective-permute-done.19.refs_1_
  824.3 4.6 collective-permute-start.31
  835.7 3.5 multiply_reduce_fusion.4
  852.6 13.9 %collective-permute-done.31 = bf16[2,384,1152]{2,1,0:T(8,128)(2,1)S(1)} collective-permute-done((bf16[2,384,1152]{2,1,0:T(8,128)(2,1)S(1)}, bf16[2,384,1152]{2,1,0:T(8,128)(2,1)S(1)}, u32[]{:S(2)}, u32[]{:S(2)}) %collective-permute-start.31) | collective-permute-done | bytes 1769504 | tf_op jit(solution)/shard_map/ppermute | solution.py:1094
  868.2 5.6 collective-permute-start.32
  880.6 4.2 add_convert_fusion.refs_2_
  891.5 39.8 %collective-permute-done.32 = bf16[2,384,1152]{2,1,0:T(8,128)(2,1)} collective-permute-done((bf16[2,384,1152]{2,1,0:T(8,128)(2,1)}, bf16[2,384,1152]{2,1,0:T(8,128)(2,1)}, u32[]{:S(2)}, u32[]{:S(2)}) %collective-permute-start.32) | collective-permute-done | bytes 1769504 | tf_op jit(solution)/shard_map/ppermute | solution.py:1094
  931.3 7.2 collective-permute-done.34
  938.5 4.9 broadcast_select_fusion
  945.2 53.7 %last_settle.1 = (bf16[72,1152]{1,0:T(8,128)(2,1)S(1)}, bf16[2,144,128]{2,1,0:T(8,128)(2,1)S(1)}) custom-call(bf16[4,4,72,1152]{3,2,1,0:T(8,128)(2,1)S(1)} %bitcast.257, bf16[4,4,2,144,128]{4,3,2,1,0:T(8,128)(2,1)S(1)} %bitcast.262), custom_call_target="tpu_custom_call" | custom-call | bytes 209715200 | tf_op jit(solution)/shard_map/last_settle/pallas_call | solution.py:949
  1005.9 6.5 expert_outputs.1
  (917 shorter events, 278.1 us)
Async XLA Ops:
  7.2 116.8 %copy-start = (s32[2,1,4]{2,1,0:T(1,128)S(1)}, s32[2,1,4]{2,1,0:T(1,128)}, u32[]{:S(2)}) copy-start(s32[2,1,4]{2,1,0:T(1,128)} %param.21) | copy-start | bytes 100
  7.2 281.5 %all-gather.5.cloned.1.call-start = ((), (), s32[]{:S(2)}) async-start(), calls=%async_computation.14 | async-start | bytes 7962624 | tf_op jit(solution)/shard_map/all_gather | solution.py:1048
  10.5 106.3 %collective-permute-start.3 = (bf16[384,1152]{1,0:T(8,128)(2,1)}, bf16[384,1152]{1,0:T(8,128)(2,1)}, u32[]{:S(2)}, u32[]{:S(2)}) collective-permute-start(bf16[384,1152]{1,0:T(8,128)(2,1)} %select_bitcast_fusion.2), channel_id=1, source_target_pairs={{0,16},{16,0},{1,17},{17,1},{2,18},{18,2},{3,19},{19,3},{4,20},{20... | collective-permute-start | bytes 2654216 | tf_op jit(solution)/shard_map/ppermute | solution.py:1012
  14.1 105.2 %collective-permute-start.2 = (bf16[1152,384]{1,0:T(8,128)(2,1)}, bf16[1152,384]{1,0:T(8,128)(2,1)}, u32[]{:S(2)}, u32[]{:S(2)}) collective-permute-start(bf16[1152,384]{1,0:T(8,128)(2,1)} %broadcast_select_fusion.6), channel_id=1, source_target_pairs={{0,16},{16,0},{1,17},{17,1},{2,18},{18,2},{3,19},{19,3},{4,20},{20... | collective-permute-start | bytes 2654216 | tf_op jit(solution)/shard_map/ppermute | solution.py:1012
  122.0 166.7 %all-gather.7.cloned.1.call-start = ((), (), s32[]{:S(2)}) async-start(), calls=%async_computation.15 | async-start | bytes 7962624 | tf_op jit(solution)/shard_map/all_gather | solution.py:1048
  122.7 287.7 %all-gather.11.cloned.1.call-start = ((), (), s32[]{:S(2)}) async-start(), calls=%async_computation.17 | async-start | bytes 7962624 | tf_op jit(solution)/shard_map/all_gather | solution.py:1048
  123.5 286.9 %all-gather.9.cloned.1.call-start = ((), (), s32[]{:S(2)}) async-start(), calls=%async_computation.16 | async-start | bytes 7962624 | tf_op jit(solution)/shard_map/all_gather | solution.py:1048
  123.5 1.6 collective-permute-start.1
  124.9 138.7 %copy-start.237 = (f32[192]{0:T(256)}, f32[192]{0:T(256)S(1)}, u32[]{:S(2)}) copy-start(f32[192]{0:T(256)S(1)} %fusion.140) | copy-start | bytes 2308
  125.0 98.9 %copy-start.225 = (pred[192]{0:T(512)(128)(4,1)}, pred[192]{0:T(512)(128)(4,1)S(1)}, u32[]{:S(2)}) copy-start(pred[192]{0:T(512)(128)(4,1)S(1)} %get-tuple-element.391) | copy-start | bytes 580
  125.0 98.9 %copy-start.229 = (pred[192]{0:T(512)(128)(4,1)}, pred[192]{0:T(512)(128)(4,1)S(1)}, u32[]{:S(2)}) copy-start(pred[192]{0:T(512)(128)(4,1)S(1)} %get-tuple-element.392) | copy-start | bytes 580
  125.0 98.9 %copy-start.233 = (pred[192]{0:T(512)(128)(4,1)}, pred[192]{0:T(512)(128)(4,1)S(1)}, u32[]{:S(2)}) copy-start(pred[192]{0:T(512)(128)(4,1)S(1)} %get-tuple-element.393) | copy-start | bytes 580
  125.1 102.1 %copy-start.264 = (pred[128]{0:T(512)(128)(4,1)}, pred[128]{0:T(512)(128)(4,1)S(1)}, u32[]{:S(2)}) copy-start(pred[128]{0:T(512)(128)(4,1)S(1)} %iota_compare_fusion.8) | copy-start | bytes 388
  125.1 184.9 %copy-start.216 = (s32[192]{0:T(256)}, s32[192]{0:T(256)S(1)}, u32[]{:S(2)}) copy-start(s32[192]{0:T(256)S(1)} %get-tuple-element.388) | copy-start | bytes 2308
  129.0 142.1 %copy-start.242 = (s32[1024]{0:T(1024)}, s32[1024]{0:T(1024)S(1)}, u32[]{:S(2)}) copy-start(s32[1024]{0:T(1024)S(1)} %pad_clamp_fusion.3) | copy-start | bytes 12292
  129.6 190.7 %copy-start.255 = (s32[1024]{0:T(1024)}, s32[1024]{0:T(1024)S(1)}, u32[]{:S(2)}) copy-start(s32[1024]{0:T(1024)S(1)} %pad_clamp_fusion.2) | copy-start | bytes 12292
  218.9 4.7 collective-permute-start
  223.5 86.2 %copy-start.210 = (bf16[4,1152]{1,0:T(4,128)(2,1)}, bf16[4,1152]{1,0:T(4,128)(2,1)S(1)}, u32[]{:S(2)}) copy-start(bf16[4,1152]{1,0:T(4,128)(2,1)S(1)} %convert_element_type.452) | copy-start | bytes 27652
  223.6 85.3 %copy-start.188 = (f32[6,16,144]{2,1,0:T(8,128)}, f32[6,16,144]{2,1,0:T(8,128)S(1)}, u32[]{:S(2)}) copy-start(f32[6,16,144]{2,1,0:T(8,128)S(1)} %reshape.638) | copy-start | bytes 165892
  273.9 14.8 %all-to-all-start = ((bf16[4,96,1152]{2,1,0:T(8,128)(2,1)}), bf16[4,96,1152]{2,1,0:T(8,128)(2,1)S(1)}, u32[]{:S(2)}, u32[]{:S(2)}) async-start(bf16[4,96,1152]{2,1,0:T(8,128)(2,1)} %bitcast.16), calls=%async_computation | async-start | bytes 1769472 | tf_op jit(solution)/shard_map/all_to_all | solution.py:1215
  305.0 15.4 %all-to-all-start.1 = ((bf16[4,96,1152]{2,1,0:T(8,128)(2,1)}), bf16[4,96,1152]{2,1,0:T(8,128)(2,1)S(1)}, u32[]{:S(2)}, u32[]{:S(2)}) async-start(bf16[4,96,1152]{2,1,0:T(8,128)(2,1)} %bitcast.21), calls=%async_computation.1 | async-start | bytes 1769472 | tf_op jit(solution)/shard_map/all_to_all | solution.py:1223
  326.9 4.8 collective-permute-start.4
  384.6 12.9 %all-to-all-start.3 = ((bf16[4,96,1152]{2,1,0:T(8,128)(2,1)}), bf16[4,96,1152]{2,1,0:T(8,128)(2,1)S(1)}, u32[]{:S(2)}, u32[]{:S(2)}) async-start(bf16[4,96,1152]{2,1,0:T(8,128)(2,1)} %bitcast.325), calls=%async_computation.3 | async-start | bytes 1769472 | tf_op jit(solution)/shard_map/all_to_all | solution.py:1172
  440.2 13.8 %all-to-all-start.5 = ((bf16[4,96,1152]{2,1,0:T(8,128)(2,1)}), bf16[4,96,1152]{2,1,0:T(8,128)(2,1)S(1)}, u32[]{:S(2)}, u32[]{:S(2)}) async-start(bf16[4,96,1152]{2,1,0:T(8,128)(2,1)} %bitcast.45), calls=%async_computation.5 | async-start | bytes 1769472 | tf_op jit(solution)/shard_map/all_to_all | solution.py:1257
  453.2 35.7 %collective-permute-start.6 = (bf16[1536,1152]{1,0:T(8,128)(2,1)}, bf16[1536,1152]{1,0:T(8,128)(2,1)}, u32[]{:S(2)}, u32[]{:S(2)}) collective-permute-start(bf16[1536,1152]{1,0:T(8,128)(2,1)} %get-tuple-element.123), channel_id=1, source_target_pairs={{0,16},{16,0},{1,17},{17,1},{2,18},{18,2},{3,19},{19,3},{4,20},{20... | collective-permute-start | bytes 10616840 | tf_op jit(solution)/shard_map/ppermute | solution.py:1012
  453.2 35.7 %collective-permute-start.7 = (bf16[1536,1152]{1,0:T(8,128)(2,1)}, bf16[1536,1152]{1,0:T(8,128)(2,1)}, u32[]{:S(2)}, u32[]{:S(2)}) collective-permute-start(bf16[1536,1152]{1,0:T(8,128)(2,1)} %get-tuple-element.124), channel_id=1, source_target_pairs={{0,16},{16,0},{1,17},{17,1},{2,18},{18,2},{3,19},{19,3},{4,20},{20... | collective-permute-start | bytes 10616840 | tf_op jit(solution)/shard_map/ppermute | solution.py:1012
  454.0 16.8 %all-to-all-start.4 = ((bf16[4,96,1152]{2,1,0:T(8,128)(2,1)}), bf16[4,96,1152]{2,1,0:T(8,128)(2,1)S(1)}, u32[]{:S(2)}, u32[]{:S(2)}) async-start(bf16[4,96,1152]{2,1,0:T(8,128)(2,1)} %bitcast.36), calls=%async_computation.4 | async-start | bytes 1769472 | tf_op jit(solution)/shard_map/all_to_all | solution.py:1223
  457.8 246.0 %reduce-scatter.9.cloned.1.call-start = ((), (), s32[]{:S(2)}) async-start(), calls=%async_computation.18 | async-start | bytes 3317760 | tf_op jit(solution)/shard_map/reduce_scatter | solution.py:1118
  485.9 23.8 %collective-permute-start.8 = (bf16[1152,1152]{1,0:T(8,128)(2,1)}, bf16[1152,1152]{1,0:T(8,128)(2,1)S(1)}, u32[]{:S(2)}, u32[]{:S(2)}) collective-permute-start(bf16[1152,1152]{1,0:T(8,128)(2,1)} %convolution_convert_fusion.5), channel_id=1, source_target_pairs={{0,16},{16,0},{1,17},{17,1},{2,18},{18,2},{3,19},{19,3},{4,20},{20... | collective-permute-start | bytes 7962632 | tf_op jit(solution)/shard_map/ppermute | solution.py:1012
  488.4 22.2 %collective-permute-start.9 = (bf16[1152,1152]{1,0:T(8,128)(2,1)}, bf16[1152,1152]{1,0:T(8,128)(2,1)S(1)}, u32[]{:S(2)}, u32[]{:S(2)}) collective-permute-start(bf16[1152,1152]{1,0:T(8,128)(2,1)} %convolution_convert_fusion.4), channel_id=1, source_target_pairs={{0,16},{16,0},{1,17},{17,1},{2,18},{18,2},{3,19},{19,3},{4,20},{20... | collective-permute-start | bytes 7962632 | tf_op jit(solution)/shard_map/ppermute | solution.py:1012
  503.5 68.6 %collective-permute-start.11 = (bf16[2,384,1152]{2,1,0:T(8,128)(2,1)}, bf16[2,384,1152]{2,1,0:T(8,128)(2,1)}, u32[]{:S(2)}, u32[]{:S(2)}) collective-permute-start(bf16[2,384,1152]{2,1,0:T(8,128)(2,1)} %pad_maximum_fusion.3), channel_id=1, source_target_pairs={{12,8},{13,9},{14,10},{15,11},{28,24},{29,25},{30,26},{31,27}} | collective-permute-start | bytes 5308424 | tf_op jit(solution)/shard_map/ppermute | solution.py:1094
  506.8 65.3 %collective-permute-start.10 = (bf16[2,384,1152]{2,1,0:T(8,128)(2,1)}, bf16[2,384,1152]{2,1,0:T(8,128)(2,1)}, u32[]{:S(2)}, u32[]{:S(2)}) collective-permute-start(bf16[2,384,1152]{2,1,0:T(8,128)(2,1)} %pad_maximum_fusion.2), channel_id=1, source_target_pairs={{0,4},{1,5},{2,6},{3,7},{16,20},{17,21},{18,22},{19,23}} | collective-permute-start | bytes 5308424 | tf_op jit(solution)/shard_map/ppermute | solution.py:1094
  580.2 5.9 collective-permute-start.12
  587.1 5.0 collective-permute-start.23
  594.7 134.0 %reduce-scatter.11.cloned.1.call-start = ((), (), s32[]{:S(2)}) async-start(), calls=%async_computation.19 | async-start | bytes 6635520 | tf_op jit(solution)/shard_map/reduce_scatter | solution.py:1118
  606.5 5.7 collective-permute-start.5
  618.0 54.1 %collective-permute-start.14 = (bf16[2,384,1152]{2,1,0:T(8,128)(2,1)}, bf16[2,384,1152]{2,1,0:T(8,128)(2,1)}, u32[]{:S(2)}, u32[]{:S(2)}) collective-permute-start(bf16[2,384,1152]{2,1,0:T(8,128)(2,1)} %add_convert_fusion.14), channel_id=1, source_target_pairs={{8,4},{12,8},{9,5},{13,9},{10,6},{14,10},{11,7},{15,11},{24,20},{2... | collective-permute-start | bytes 5308424 | tf_op jit(solution)/shard_map/ppermute | solution.py:1094
  623.1 49.0 %collective-permute-start.13 = (bf16[2,384,1152]{2,1,0:T(8,128)(2,1)}, bf16[2,384,1152]{2,1,0:T(8,128)(2,1)}, u32[]{:S(2)}, u32[]{:S(2)}) collective-permute-start(bf16[2,384,1152]{2,1,0:T(8,128)(2,1)} %add_convert_fusion.15), channel_id=1, source_target_pairs={{0,4},{4,8},{1,5},{5,9},{2,6},{6,10},{3,7},{7,11},{16,20},{20,24},... | collective-permute-start | bytes 5308424 | tf_op jit(solution)/shard_map/ppermute | solution.py:1094
  633.5 21.1 %all-to-all-start.6 = ((bf16[4,96,1152]{2,1,0:T(8,128)(2,1)}), bf16[4,96,1152]{2,1,0:T(8,128)(2,1)S(1)}, u32[]{:S(2)}, u32[]{:S(2)}) async-start(bf16[4,96,1152]{2,1,0:T(8,128)(2,1)} %bitcast.64), calls=%async_computation.6 | async-start | bytes 1769472 | tf_op jit(solution)/shard_map/all_to_all | solution.py:1172
  672.1 18.3 %all-to-all-start.7 = ((bf16[4,96,1152]{2,1,0:T(8,128)(2,1)}), bf16[4,96,1152]{2,1,0:T(8,128)(2,1)S(1)}, u32[]{:S(2)}, u32[]{:S(2)}) async-start(bf16[4,96,1152]{2,1,0:T(8,128)(2,1)} %get-tuple-element.137), calls=%async_computation.7 | async-start | bytes 1769472 | tf_op jit(solution)/shard_map/all_to_all | solution.py:1257
  675.8 145.0 %reduce-scatter.19.cloned.1.call-start = ((), (), s32[]{:S(2)}) async-start(), calls=%async_computation.23 | async-start | bytes 829440
  685.3 30.8 %collective-permute-start.15 = (bf16[1536,1152]{1,0:T(8,128)(2,1)}, bf16[1536,1152]{1,0:T(8,128)(2,1)}, u32[]{:S(2)}, u32[]{:S(2)}) collective-permute-start(bf16[1536,1152]{1,0:T(8,128)(2,1)} %get-tuple-element.140), channel_id=1, source_target_pairs={{0,16},{16,0},{1,17},{17,1},{2,18},{18,2},{3,19},{19,3},{4,20},{20... | collective-permute-start | bytes 10616840 | tf_op jit(solution)/shard_map/ppermute | solution.py:1012
  685.3 31.1 %collective-permute-start.16 = (bf16[1536,1152]{1,0:T(8,128)(2,1)}, bf16[1536,1152]{1,0:T(8,128)(2,1)}, u32[]{:S(2)}, u32[]{:S(2)}) collective-permute-start(bf16[1536,1152]{1,0:T(8,128)(2,1)} %get-tuple-element.141), channel_id=1, source_target_pairs={{0,16},{16,0},{1,17},{17,1},{2,18},{18,2},{3,19},{19,3},{4,20},{20... | collective-permute-start | bytes 10616840 | tf_op jit(solution)/shard_map/ppermute | solution.py:1012
  689.1 124.9 %collective-permute-start.22 = (bf16[2,384,1152]{2,1,0:T(8,128)(2,1)}, bf16[2,384,1152]{2,1,0:T(8,128)(2,1)}, u32[]{:S(2)}, u32[]{:S(2)}) collective-permute-start(bf16[2,384,1152]{2,1,0:T(8,128)(2,1)} %add_convert_fusion.12), channel_id=1, source_target_pairs={{4,0},{8,4},{12,8},{5,1},{9,5},{13,9},{6,2},{10,6},{14,10},{7,3},{... | collective-permute-start | bytes 5308424 | tf_op jit(solution)/shard_map/ppermute | solution.py:1094
  703.9 34.8 %collective-permute-start.17 = (bf16[1152,1152]{1,0:T(8,128)(2,1)}, bf16[1152,1152]{1,0:T(8,128)(2,1)}, u32[]{:S(2)}, u32[]{:S(2)}) collective-permute-start(bf16[1152,1152]{1,0:T(8,128)(2,1)} %convolution_convert_fusion.3), channel_id=1, source_target_pairs={{0,16},{16,0},{1,17},{17,1},{2,18},{18,2},{3,19},{19,3},{4,20},{20... | collective-permute-start | bytes 7962632 | tf_op jit(solution)/shard_map/ppermute | solution.py:1012
  703.9 116.8 %reduce-scatter.13.cloned.1.call-start = ((), (), s32[]{:S(2)}) async-start(), calls=%async_computation.20 | async-start | bytes 1658880 | tf_op jit(solution)/shard_map/reduce_scatter | solution.py:1122
  707.3 106.7 %collective-permute-start.21 = (bf16[2,384,1152]{2,1,0:T(8,128)(2,1)}, bf16[2,384,1152]{2,1,0:T(8,128)(2,1)}, u32[]{:S(2)}, u32[]{:S(2)}) collective-permute-start(bf16[2,384,1152]{2,1,0:T(8,128)(2,1)} %add_convert_fusion.13), channel_id=1, source_target_pairs={{0,4},{4,8},{8,12},{1,5},{5,9},{9,13},{2,6},{6,10},{10,14},{3,7},{... | collective-permute-start | bytes 5308424 | tf_op jit(solution)/shard_map/ppermute | solution.py:1094
  716.1 33.8 %collective-permute-start.18 = (bf16[1152,1152]{1,0:T(8,128)(2,1)}, bf16[1152,1152]{1,0:T(8,128)(2,1)}, u32[]{:S(2)}, u32[]{:S(2)}) collective-permute-start(bf16[1152,1152]{1,0:T(8,128)(2,1)} %convolution_convert_fusion.2), channel_id=1, source_target_pairs={{0,16},{16,0},{1,17},{17,1},{2,18},{18,2},{3,19},{19,3},{4,20},{20... | collective-permute-start | bytes 7962632 | tf_op jit(solution)/shard_map/ppermute | solution.py:1012
  728.7 151.8 %reduce-scatter.15.cloned.1.call-start = ((), (), s32[]{:S(2)}) async-start(), calls=%async_computation.21 | async-start | bytes 6635520 | tf_op jit(solution)/shard_map/reduce_scatter | solution.py:1118
  735.3 78.6 %collective-permute-start.20 = (bf16[2,384,1152]{2,1,0:T(8,128)(2,1)}, bf16[2,384,1152]{2,1,0:T(8,128)(2,1)}, u32[]{:S(2)}, u32[]{:S(2)}) collective-permute-start(bf16[2,384,1152]{2,1,0:T(8,128)(2,1)} %pad_maximum_fusion.5), channel_id=1, source_target_pairs={{12,8},{13,9},{14,10},{15,11},{28,24},{29,25},{30,26},{31,27}} | collective-permute-start | bytes 5308424 | tf_op jit(solution)/shard_map/ppermute | solution.py:1094
  738.6 82.1 %collective-permute-start.19 = (bf16[2,384,1152]{2,1,0:T(8,128)(2,1)}, bf16[2,384,1152]{2,1,0:T(8,128)(2,1)}, u32[]{:S(2)}, u32[]{:S(2)}) collective-permute-start(bf16[2,384,1152]{2,1,0:T(8,128)(2,1)} %pad_maximum_fusion.4), channel_id=1, source_target_pairs={{0,4},{1,5},{2,6},{3,7},{16,20},{17,21},{18,22},{19,23}} | collective-permute-start | bytes 5308424 | tf_op jit(solution)/shard_map/ppermute | solution.py:1094
  755.8 248.4 %reduce-scatter.17.cloned.1.call-start = ((), (), s32[]{:S(2)}) async-start(), calls=%async_computation.22 | async-start | bytes 1658880 | tf_op jit(solution)/shard_map/reduce_scatter | solution.py:1122
  824.3 42.2 %collective-permute-start.31 = (bf16[2,384,1152]{2,1,0:T(8,128)(2,1)S(1)}, bf16[2,384,1152]{2,1,0:T(8,128)(2,1)S(1)}, u32[]{:S(2)}, u32[]{:S(2)}) collective-permute-start(bf16[2,384,1152]{2,1,0:T(8,128)(2,1)S(1)} %add_convert_fusion.11), channel_id=1, source_target_pairs={{0,4},{4,8},{1,5},{5,9},{2,6},{6,10},{3,7},{7,11},{16,20},{20,24},... | collective-permute-start | bytes 5308424 | tf_op jit(solution)/shard_map/ppermute | solution.py:1094
  831.0 42.9 %collective-permute-start.33 = (bf16[2,384,1152]{2,1,0:T(8,128)(2,1)S(1)}, bf16[2,384,1152]{2,1,0:T(8,128)(2,1)S(1)}, u32[]{:S(2)}, u32[]{:S(2)}) collective-permute-start(bf16[2,384,1152]{2,1,0:T(8,128)(2,1)S(1)} %add_convert_fusion.9), channel_id=1, source_target_pairs={{8,4},{12,8},{9,5},{13,9},{10,6},{14,10},{11,7},{15,11},{24,20},{2... | collective-permute-start | bytes 5308424 | tf_op jit(solution)/shard_map/ppermute | solution.py:1094
  840.0 6.7 collective-permute-start.24
  849.4 31.1 %collective-permute-start.26 = (bf16[1152,1152]{1,0:T(8,128)(2,1)}, bf16[1152,1152]{1,0:T(8,128)(2,1)}, u32[]{:S(2)}, u32[]{:S(2)}) collective-permute-start(bf16[1152,1152]{1,0:T(8,128)(2,1)} %convolution_convert_fusion), channel_id=1, source_target_pairs={{0,16},{16,0},{1,17},{17,1},{2,18},{18,2},{3,19},{19,3},{4,20},{20... | collective-permute-start | bytes 7962632 | tf_op jit(solution)/shard_map/ppermute | solution.py:1012
  852.0 27.1 %collective-permute-start.25 = (f32[192,1152]{1,0:T(8,128)S(1)}, f32[192,1152]{1,0:T(8,128)S(1)}, u32[]{:S(2)}, u32[]{:S(2)}) collective-permute-start(f32[192,1152]{1,0:T(8,128)S(1)} %get-tuple-element.298), channel_id=1, source_target_pairs={{0,16},{16,0},{1,17},{17,1},{2,18},{18,2},{3,19},{19,3},{4,20},{20... | collective-permute-start | bytes 2654216 | tf_op jit(solution)/shard_map/ppermute | solution.py:1012
  868.2 63.1 %collective-permute-start.32 = (bf16[2,384,1152]{2,1,0:T(8,128)(2,1)}, bf16[2,384,1152]{2,1,0:T(8,128)(2,1)}, u32[]{:S(2)}, u32[]{:S(2)}) collective-permute-start(bf16[2,384,1152]{2,1,0:T(8,128)(2,1)} %add_convert_fusion.10), channel_id=1, source_target_pairs={{0,4},{4,8},{8,12},{1,5},{5,9},{9,13},{2,6},{6,10},{10,14},{3,7},{... | collective-permute-start | bytes 5308424 | tf_op jit(solution)/shard_map/ppermute | solution.py:1094
  875.5 63.0 %collective-permute-start.34 = (bf16[2,384,1152]{2,1,0:T(8,128)(2,1)}, bf16[2,384,1152]{2,1,0:T(8,128)(2,1)}, u32[]{:S(2)}, u32[]{:S(2)}) collective-permute-start(bf16[2,384,1152]{2,1,0:T(8,128)(2,1)} %add_convert_fusion.8), channel_id=1, source_target_pairs={{4,0},{8,4},{12,8},{5,1},{9,5},{13,9},{6,2},{10,6},{14,10},{7,3},{... | collective-permute-start | bytes 5308424 | tf_op jit(solution)/shard_map/ppermute | solution.py:1094
  888.9 54.5 %collective-permute-start.27 = (bf16[16,2,144,128]{3,2,1,0:T(8,128)(2,1)S(1)}, bf16[16,2,144,128]{3,2,1,0:T(8,128)(2,1)S(1)}, u32[]{:S(2)}, u32[]{:S(2)}) collective-permute-start(bf16[16,2,144,128]{3,2,1,0:T(8,128)(2,1)S(1)} %broadcast_select_fusion.2), channel_id=1, source_target_pairs={{0,16},{16,0},{1,17},{17,1},{2,18},{18,2},{3,19},{19,3},{4,20},{20... | collective-permute-start | bytes 3538952 | tf_op jit(solution)/shard_map/ppermute | solution.py:1012
  943.4 62.5 %collective-permute-start.35 = (bf16[2,384,1152]{2,1,0:T(8,128)(2,1)}, bf16[2,384,1152]{2,1,0:T(8,128)(2,1)}, u32[]{:S(2)}, u32[]{:S(2)}) collective-permute-start(bf16[2,384,1152]{2,1,0:T(8,128)(2,1)} %get-tuple-element.312), channel_id=1, source_target_pairs={{0,16},{16,0},{1,17},{17,1},{2,18},{18,2},{3,19},{19,3},{4,20},{20... | collective-permute-start | bytes 5308424 | tf_op jit(solution)/shard_map/ppermute | solution.py:1012
  998.9 6.9 collective-permute-start.28
  1005.3 7.2 collective-permute-start.29
  1005.3 7.1 collective-permute-start.30
  (269 other events, 1811.2 us)
Sparse Core Ops, SparseCore 0:
  122.1 70.3 all-gather.4
  194.1 70.1 all-gather.6
  266.4 69.8 all-gather.10
  338.3 69.7 all-gather.8
  594.8 40.0 reduce-scatter.8
  637.7 69.3 reduce-scatter.10
  709.4 31.0 reduce-scatter.18
  742.8 51.4 reduce-scatter.12
  797.6 63.2 reduce-scatter.14
  880.7 52.7 reduce-scatter.16
